TPU v7x, 256 devices: a whole 4x4x8 slice. The times are simulated.
256 devices in a mesh: dp: 8 (over x, core), ctx: 32 (over z, y).
Axes of the slice: x: 4, y: 4, z: 8, core: 2. Of those that a mesh axis runs over, the one named last changes fastest.
Arguments:
- injected_early: bfloat16 [8, 640, 4608], P('dp', 'ctx'), may hold values from -6 to 6
- injected_middle: bfloat16 [8, 640, 4608], P('dp', 'ctx'), may hold values from -6 to 6
- injected_late: bfloat16 [8, 640, 4608], P('dp', 'ctx'), may hold values from -6 to 6
- slot_source: int32 [8, 1024], P('dp', 'ctx'), may hold values from -1 to 639, as said below
- saved_early: bfloat16 [8, 4096, 1152], P('dp', 'ctx'), may hold values from -0.023925781 to 0.023925781
- projection_early: bfloat16 [1152, 1152], P('dp'), may hold values from -0.1875 to 0.1875
- projection_middle: bfloat16 [1152, 1152], P('dp'), may hold values from -0.1875 to 0.1875
- projection_late: bfloat16 [1152, 1152], P('dp'), may hold values from -0.1875 to 0.1875
Outputs:
- context_early: bfloat16 [8, 4096, 1152], P('dp', 'ctx')
- context_middle: bfloat16 [8, 4096, 1152], P('dp', 'ctx')
- context_late: bfloat16 [8, 4096, 1152], P('dp', 'ctx')
- stream_gradient: bfloat16 [8, 4096, 1152], P('dp', 'ctx')
- projection_gradient: float32 [1152, 1152], P('ctx', 'dp')
Inputs may be any that keep to these rules, and one draw needn't show every extreme that they name: `slot_source`: in each group the entries other than -1 name every visual token 0 to 639 once. Token q lies on context device q // 20; slot e lies on device e // 32. Each aligned block of 32 slots holds one image: its tokens, in order, fill the block's first slots and the rest are -1. Of the tokens of one device at most 1 fill slots of one device, and in every group one device receives exactly 1 from every device.
All inputs are finite; a program needn't handle non-finite values.
Results may differ from a plain program's by a relative error of at most 0.0051.
Values may be sent and summed in bfloat16 or wider, within the bound.
No kernel may reach another device: no remote copies, remote signals or barrier semaphores. Data moves between devices by JAX's collectives and lax.ppermute only.
A program may use at most 128 MiB of HBM per device.

v0:
```python
import jax
import jax.numpy as jnp
from jax import lax
from jax.sharding import PartitionSpec as P


def arrival_rank(lists, visual_rows):
    filled = lists >= 0
    sender = jnp.where(filled, lists // visual_rows, -1)
    before = (
        (sender[..., :, None] == sender[..., None, :])
        & (lists[..., None, :] < lists[..., :, None])
        & filled[..., None, :]
    )
    return (sender, filled, jnp.sum(before.astype(jnp.int32), axis=-1))


def through_projection(rounded, projection):
    return lax.dot_general(
        rounded,
        lax.all_gather(projection, "dp", axis=0, tiled=True),
        (((1,), (1,)), ((), ())),
        preferred_element_type=jnp.float32,
    ).astype(jnp.bfloat16)


def local(
    injected_early,
    injected_middle,
    injected_late,
    slot_source,
    saved_early,
    projection_early,
    projection_middle,
    projection_late,
):
    devices = lax.axis_size("ctx")
    myself = lax.axis_index("ctx")
    visual_rows = injected_early.shape[1]
    slot_count = slot_source.shape[1]
    capacity = slot_count // devices
    width = saved_early.shape[2]
    all_lists = lax.all_gather(slot_source, "ctx", axis=1, tiled=True).reshape(devices, slot_count)
    sender, filled, order = arrival_rank(all_lists, visual_rows)
    owners = jnp.arange(devices, dtype=jnp.int32)[:, None]
    places = owners * capacity + order
    local_row = jnp.where(
        filled & (sender == myself), all_lists - myself * visual_rows, visual_rows
    )
    target = (
        jnp.zeros((visual_rows,), jnp.int32)
        .at[local_row.reshape(-1)]
        .set(places.reshape(-1), mode="drop")
    )

    def packed(rows):
        return jnp.zeros((devices * capacity, rows.shape[2]), rows.dtype).at[target].set(rows[0])

    arrived = (
        lax.all_to_all(packed(injected_early), "ctx", split_axis=0, concat_axis=0, tiled=True),
        lax.all_to_all(packed(injected_middle), "ctx", split_axis=0, concat_axis=0, tiled=True),
        lax.all_to_all(packed(injected_late), "ctx", split_axis=0, concat_axis=0, tiled=True),
    )
    own_sender, own_filled, own_order = arrival_rank(slot_source[0], visual_rows)
    pick_rows = jnp.where(own_filled, own_sender * capacity + own_order, 0)

    def placed(rows):
        taken = jnp.where(own_filled[:, None], rows[pick_rows], jnp.zeros((), rows.dtype))
        return taken.reshape(slot_count * (rows.shape[1] // width), width)

    placed_early = placed(arrived[0])
    placed_middle = placed(arrived[1])
    placed_late = placed(arrived[2])
    down_late = placed_late.astype(jnp.float32)
    down_middle = down_late + placed_middle.astype(jnp.float32)
    down_early = down_middle + placed_early.astype(jnp.float32)
    rounded_late = down_late.astype(jnp.bfloat16)
    rounded_middle = down_middle.astype(jnp.bfloat16)
    rounded_early = down_early.astype(jnp.bfloat16)
    context_late = through_projection(rounded_late, projection_late)
    context_middle = through_projection(rounded_middle, projection_middle)
    context_early = through_projection(rounded_early, projection_early)
    activations = saved_early[0]
    row_share = lax.psum_scatter(
        lax.dot_general(
            activations, rounded_early, (((0,), (0,)), ((), ())), preferred_element_type=jnp.float32
        ),
        "ctx",
        scatter_dimension=0,
        tiled=True,
    )
    weights = lax.psum_scatter(row_share, "dp", scatter_dimension=1, tiled=True)
    return (
        context_early[None],
        context_middle[None],
        context_late[None],
        rounded_early[None],
        weights,
    )


def solution(mesh):
    return jax.shard_map(
        local,
        mesh=mesh,
        in_specs=(
            P("dp", "ctx", None),
            P("dp", "ctx", None),
            P("dp", "ctx", None),
            P("dp", "ctx"),
            P("dp", "ctx", None),
            P("dp", None),
            P("dp", None),
            P("dp", None),
        ),
        out_specs=(
            P("dp", "ctx", None),
            P("dp", "ctx", None),
            P("dp", "ctx", None),
            P("dp", "ctx", None),
            P("ctx", "dp"),
        ),
        check_vma=False,
    )
```

profile of v0, /device:TPU:6, one launch (start us, length us, event | category | flops | bytes accessed | tf_op | source)
XLA Modules:
  0.0 303.7 jit_solution(1624377837932468255)
XLA Ops:
  8.8 1.3 fusion.32
  11.5 23.5 %all-reduce = s32[1024]{0:T(1024)S(1)} all-reduce(s32[1024]{0:T(1024)S(1)} %get-tuple-element.37), channel_id=1, replica_groups=mesh['dp'=8,'ctx'=32] {'ctx'}, use_global_device_ids=true, to_apply=%add | all-reduce | flops 1024 | bytes 8192
  35.2 0.9 convert_reduce_fusion
  36.2 4.3 %scatter_custom_fusion = s32[20]{0:T(128)S(1)} fusion(s32[1024]{0:T(1024)S(1)} %bitcast.85, s32[1024]{0:T(1024)S(1)} %reshape.499, s32[]{:T(128)} %constant.8.clone.1), kind=kCustom, calls=%fused_computation.74 | custom fusion | bytes 84 | tf_op jit(solution)/shard_map/scatter | solution.py:53
  40.6 1.4 scatter_custom_fusion.1
  44.0 4.1 %all-to-all-start = ((bf16[32,2,2304]{2,1,0:T(2,128)(2,1)}), bf16[32,2,2304]{2,1,0:T(2,128)(2,1)S(1)}, u32[]{:S(2)}, u32[]{:S(2)}) async-start(bf16[32,2,2304]{2,1,0:T(2,128)(2,1)} %reshape.569), calls=%async_computation | async-start | bytes 589824 | tf_op jit(solution)/shard_map/all_to_all | solution.py:62
  48.1 0.9 scatter_custom_fusion.2
  49.1 0.8 reduce.1
  50.7 9.2 %all-to-all-done = bf16[32,2,2304]{2,1,0:T(2,128)(2,1)S(1)} async-done(((bf16[32,2,2304]{2,1,0:T(2,128)(2,1)}), bf16[32,2,2304]{2,1,0:T(2,128)(2,1)S(1)}, u32[]{:S(2)}, u32[]{:S(2)}) %all-to-all-start) | async-done | bytes 294944 | tf_op jit(solution)/shard_map/all_to_all | solution.py:62
  59.9 3.9 %all-to-all-start.1 = ((bf16[32,2,2304]{2,1,0:T(2,128)(2,1)}), bf16[32,2,2304]{2,1,0:T(2,128)(2,1)S(1)}, u32[]{:S(2)}, u32[]{:S(2)}) async-start(bf16[32,2,2304]{2,1,0:T(2,128)(2,1)} %reshape.567), calls=%async_computation.1 | async-start | bytes 589824 | tf_op jit(solution)/shard_map/all_to_all | solution.py:61
  63.9 0.9 scatter_custom_fusion.3
  64.8 0.8 reduce
  66.5 9.2 %all-to-all-done.1 = bf16[32,2,2304]{2,1,0:T(2,128)(2,1)S(1)} async-done(((bf16[32,2,2304]{2,1,0:T(2,128)(2,1)}), bf16[32,2,2304]{2,1,0:T(2,128)(2,1)S(1)}, u32[]{:S(2)}, u32[]{:S(2)}) %all-to-all-start.1) | async-done | bytes 294944 | tf_op jit(solution)/shard_map/all_to_all | solution.py:61
  75.7 3.9 %all-to-all-start.2 = ((bf16[32,2,2304]{2,1,0:T(2,128)(2,1)}), bf16[32,2,2304]{2,1,0:T(2,128)(2,1)S(1)}, u32[]{:S(2)}, u32[]{:S(2)}) async-start(bf16[32,2,2304]{2,1,0:T(2,128)(2,1)} %reshape.565), calls=%async_computation.2 | async-start | bytes 589824 | tf_op jit(solution)/shard_map/all_to_all | solution.py:60
  82.0 9.4 %all-to-all-done.2 = bf16[32,2,2304]{2,1,0:T(2,128)(2,1)S(1)} async-done(((bf16[32,2,2304]{2,1,0:T(2,128)(2,1)}), bf16[32,2,2304]{2,1,0:T(2,128)(2,1)S(1)}, u32[]{:S(2)}, u32[]{:S(2)}) %all-to-all-start.2) | async-done | bytes 294944 | tf_op jit(solution)/shard_map/all_to_all | solution.py:60
  92.9 3.2 %convolution_bitcast_fusion = f32[1152,1152]{0,1:T(8,128)} fusion(bf16[128,1152]{1,0:T(8,128)(2,1)S(1)} %convert_element_type.123, bf16[1,128,1152]{2,1,0:T(8,128)(2,1)S(1)} %copy-done), kind=kOutput, calls=%fused_computation.7 | convolution fusion | flops 339738624 | bytes 5898240 | tf_op jit(solution)/shard_map/dot_general | solution.py:85
  99.9 1.0 add_convert_fusion.1
  100.8 3.5 %fusion.1 = bf16[1,128,1152]{2,1,0:T(8,128)(2,1)} fusion(bf16[1152,1152]{1,0:T(8,128)(2,1)} %all-gather.6.cloned.1.call-done, bf16[128,1152]{1,0:T(8,128)(2,1)S(1)} %gather.24, pred[128]{0:T(512)(128)(4,1)S(1)} %broadcast_in_dim.62, bf16[128,1152]{1,0:T(8,128)(2,1)S(1)} %gather.22), kind=kOutput, calls=%fused_computation.12 | convolution fusion | flops 340770816 | bytes 3539072 | tf_op jit(solution)/shard_map/dot_general | solution.py:19
  104.3 159.7 %all-reduce.4.cloned.1.call-done = f32[1152,1152]{0,1:T(8,128)} async-done(((f32[1152,1152]{0,1:T(8,128)}), f32[1152,1152]{0,1:T(8,128)}) %all-reduce.4.cloned.1.call-update) | async-done | bytes 5308432
  264.0 2.3 constant_dynamic-slice_fusion
  266.4 3.4 %fusion.2 = bf16[1,128,1152]{2,1,0:T(8,128)(2,1)} fusion(bf16[1152,1152]{1,0:T(8,128)(2,1)} %all-gather.8.cloned.1.call-done, bf16[128,1152]{1,0:T(8,128)(2,1)S(1)} %gather.22, pred[128]{0:T(512)(128)(4,1)S(1)} %broadcast_in_dim.62), kind=kOutput, calls=%fused_computation.13 | convolution fusion | flops 340033536 | bytes 3244160 | tf_op jit(solution)/shard_map/dot_general | solution.py:19
  269.8 3.4 %fusion = bf16[1,128,1152]{2,1,0:T(8,128)(2,1)} fusion(bf16[1152,1152]{1,0:T(8,128)(2,1)} %all-gather.4.cloned.1.call-done, bf16[128,1152]{1,0:T(8,128)(2,1)S(1)} %gather.26, pred[128]{0:T(512)(128)(4,1)S(1)} %broadcast_in_dim.62, bf16[128,1152]{1,0:T(8,128)(2,1)S(1)} %gather.24, bf16[128,1152]{1,0:T(8,128)(2,1)S(1)} %gather.22), kind=kOutput, calls=%fused_computation.11 | convolution fusion | flops 341213184 | bytes 3833984 | tf_op jit(solution)/shard_map/dot_general | solution.py:19
  273.2 21.8 %reduce-scatter.3.cloned.1.call-done = f32[36,144]{0,1:T(8,128)} async-done(((f32[36,1152]{0,1:T(8,128)}), f32[36,144]{0,1:T(8,128)}) %reduce-scatter.3.cloned.1.call-update) | async-done | bytes 20752 | tf_op jit(solution)/shard_map/reduce_scatter | solution.py:92
  295.0 1.6 copy.26
  (62 shorter events, 12.2 us)
Async XLA Ops:
  8.0 84.9 %copy-start = (bf16[1,128,1152]{2,1,0:T(8,128)(2,1)S(1)}, bf16[1,128,1152]{2,1,0:T(8,128)(2,1)}, u32[]{:S(2)}) copy-start(bf16[1,128,1152]{2,1,0:T(8,128)(2,1)} %param.12) | copy-start | bytes 884740
  8.0 40.1 %copy-start.1 = (bf16[1,20,4608]{2,1,0:T(8,128)(2,1)S(1)}, bf16[1,20,4608]{2,1,0:T(8,128)(2,1)}, u32[]{:S(2)}) copy-start(bf16[1,20,4608]{2,1,0:T(8,128)(2,1)} %param.9) | copy-start | bytes 552964
  8.0 55.8 %copy-start.2 = (bf16[1,20,4608]{2,1,0:T(8,128)(2,1)S(1)}, bf16[1,20,4608]{2,1,0:T(8,128)(2,1)}, u32[]{:S(2)}) copy-start(bf16[1,20,4608]{2,1,0:T(8,128)(2,1)} %param.8) | copy-start | bytes 552964
  8.0 92.8 %all-gather.6.cloned.1.call-start = ((), (), s32[]{:S(2)}) async-start(), calls=%async_computation.5 | async-start | bytes 2985984 | tf_op jit(solution)/shard_map/all_gather | solution.py:21
  43.2 23.2 %copy-start.3 = (s32[1,32]{1,0:T(1,128)S(1)}, s32[1,32]{1,0:T(1,128)}, u32[]{:S(2)}) copy-start(s32[1,32]{1,0:T(1,128)} %param.11) | copy-start | bytes 388
  44.0 15.9 %all-to-all-start = ((bf16[32,2,2304]{2,1,0:T(2,128)(2,1)}), bf16[32,2,2304]{2,1,0:T(2,128)(2,1)S(1)}, u32[]{:S(2)}, u32[]{:S(2)}) async-start(bf16[32,2,2304]{2,1,0:T(2,128)(2,1)} %reshape.569), calls=%async_computation | async-start | bytes 589824 | tf_op jit(solution)/shard_map/all_to_all | solution.py:62
  59.9 15.8 %all-to-all-start.1 = ((bf16[32,2,2304]{2,1,0:T(2,128)(2,1)}), bf16[32,2,2304]{2,1,0:T(2,128)(2,1)S(1)}, u32[]{:S(2)}, u32[]{:S(2)}) async-start(bf16[32,2,2304]{2,1,0:T(2,128)(2,1)} %reshape.567), calls=%async_computation.1 | async-start | bytes 589824 | tf_op jit(solution)/shard_map/all_to_all | solution.py:61
  75.7 15.7 %all-to-all-start.2 = ((bf16[32,2,2304]{2,1,0:T(2,128)(2,1)}), bf16[32,2,2304]{2,1,0:T(2,128)(2,1)S(1)}, u32[]{:S(2)}, u32[]{:S(2)}) async-start(bf16[32,2,2304]{2,1,0:T(2,128)(2,1)} %reshape.565), calls=%async_computation.2 | async-start | bytes 589824 | tf_op jit(solution)/shard_map/all_to_all | solution.py:60
  79.6 184.4 %all-reduce.4.cloned.1.call-start = ((), (), s32[]{:S(2)}) async-start(), calls=%async_computation.8 | async-start | bytes 10616832
  96.1 170.2 %all-gather.8.cloned.1.call-start = ((), (), s32[]{:S(2)}) async-start(), calls=%async_computation.6 | async-start | bytes 2985984 | tf_op jit(solution)/shard_map/all_gather | solution.py:21
  96.9 172.9 %all-gather.4.cloned.1.call-start = ((), (), s32[]{:S(2)}) async-start(), calls=%async_computation.4 | async-start | bytes 2985984 | tf_op jit(solution)/shard_map/all_gather | solution.py:21
  97.6 197.4 %reduce-scatter.3.cloned.1.call-start = ((), (), s32[]{:S(2)}) async-start(), calls=%async_computation.7 | async-start | bytes 663552 | tf_op jit(solution)/shard_map/reduce_scatter | solution.py:92
Sparse Core Ops, SparseCore 0:
  10.7 30.6 all-gather.5
  98.8 23.1 all-gather.7
  123.8 29.2 all-gather.3
  266.4 28.5 reduce-scatter.2
Sparse Core Ops, SparseCore 1:
  96.2 167.7 all-reduce.3
where the time goes:
time: 307 us; the launch traced here: 304 us
  waiting for transfers between devices  211 us (69%)
  blocking collectives  23.5 us (8%)
  local copies, waits for them, and re-layouts  20.4 us (7%)
  between operations  16.9 us (6%)
  matrix products  13.5 us (4%)
  starting transfers between devices  12.3 us (4%)
  other arithmetic  5.6 us (2%)
    unnamed x6, waiting for transfers between devices  162 us
    unnamed x1, blocking collectives  23.5 us
    reduce_scatter x1, waiting for transfers between devices, local(): weights = lax.psum_scatter(row_share, 'dp', scatter_dimension=1, tiled=True)  21.8 us
    dot_general x3, matrix products, through_projection(): lax.dot_general(rounded, lax.all_gather(projection, 'dp', axis=0, tiled=T...  10.3 us
    all_to_all x1, waiting for transfers between devices, local(): lax.all_to_all(packed(injected_early), 'ctx', split_axis=0, concat_axis=0...  9.43 us
    all_to_all x1, waiting for transfers between devices, local(): lax.all_to_all(packed(injected_late), 'ctx', split_axis=0, concat_axis=0,...  9.22 us
    all_to_all x1, waiting for transfers between devices, local(): lax.all_to_all(packed(injected_middle), 'ctx', split_axis=0, concat_axis=...  9.22 us
    unnamed x21, local copies, waits for them, and re-layouts  8.52 us
  transfers between devices with their start and end apart: 8, of which 5 were waited for; matrix products, arithmetic and copies ran while one was open for 12% of the time, Pallas kernels for 0%

commit v1 on v0

v1 whole, which is shorter than its diff:
```python
import jax
import jax.numpy as jnp
from jax import lax
from jax.experimental import pallas as pl
from jax.experimental.pallas import tpu as pltpu
from jax.sharding import Mesh, PartitionSpec as P

DP = ("x", "core")
CTX = ("z", "y")
BF16 = jnp.bfloat16
F32 = jnp.float32


def turn(size, step):
    return [(i, (i + step) % size) for i in range(size)]


def select(rows, table):
    return jnp.dot(table.astype(BF16), rows, preferred_element_type=F32).astype(BF16)


def context_kernel(core_ref, rounded_ref, own_ref, other_ref, out_ref, weight, sem):
    core = core_ref[0]
    xs, rows = own_ref.shape[0], own_ref.shape[2]
    matrices = own_ref.shape[1]
    copies = []
    for m in range(matrices):
        for x in range(xs):
            for ref, c in ((own_ref, core), (other_ref, 1 - core)):
                at = pl.multiple_of((2 * x + c) * rows, 16)
                copies.append(
                    pltpu.make_async_copy(ref.at[x, m], weight.at[m, pl.ds(at, rows)], sem.at[m])
                )
    for copy in copies:
        copy.start()
    per = len(copies) // matrices
    for m in range(matrices):
        for copy in copies[m * per : (m + 1) * per]:
            copy.wait()
        out_ref[m] = lax.dot_general(
            rounded_ref[m], weight[m], (((1,), (1,)), ((), ())), preferred_element_type=F32
        ).astype(BF16)


def contexts(core, rounded, own, other):
    matrices, rows, width = rounded.shape
    return pl.pallas_call(
        context_kernel,
        out_shape=jax.ShapeDtypeStruct((matrices, rows, width), BF16),
        in_specs=[
            pl.BlockSpec(memory_space=pltpu.SMEM),
            pl.BlockSpec(memory_space=pltpu.VMEM),
            pl.BlockSpec(memory_space=pl.ANY),
            pl.BlockSpec(memory_space=pl.ANY),
        ],
        out_specs=pl.BlockSpec(memory_space=pltpu.VMEM),
        scratch_shapes=[
            pltpu.VMEM((matrices, width, width), BF16),
            pltpu.SemaphoreType.DMA((matrices,)),
        ],
        compiler_params=pltpu.CompilerParams(vmem_limit_bytes=32 << 20),
        cost_estimate=pl.CostEstimate(
            flops=2 * matrices * rows * width * width,
            bytes_accessed=2 * matrices * width * width,
            transcendentals=0,
        ),
    )(core, rounded, own, other)


def local(
    injected_early,
    injected_middle,
    injected_late,
    slot_source,
    saved_early,
    projection_early,
    projection_middle,
    projection_late,
):
    devices = lax.axis_size(CTX)
    xs, cores = lax.axis_size("x"), lax.axis_size("core")
    core = lax.axis_index("core")
    tokens, merged = injected_early.shape[1:]
    slots = slot_source.shape[1]
    patches, width = saved_early.shape[1:]
    merge = merged // width
    share = width // (xs * cores)

    stacked = jnp.stack([projection_early, projection_middle, projection_late])
    own = lax.all_gather(stacked, "x", axis=0)
    other = lax.ppermute(own, "core", turn(cores, 1))

    late = injected_late[0].reshape(tokens * merge, width)
    middle32 = late.astype(F32) + injected_middle[0].reshape(tokens * merge, width).astype(F32)
    early32 = middle32 + injected_early[0].reshape(tokens * merge, width).astype(F32)
    middle, early = middle32.astype(BF16), early32.astype(BF16)

    source = slot_source[0]
    filled = source >= 0
    sender = jnp.where(filled, source // tokens, -1)
    place = jnp.where(filled, source % tokens, 0)
    patch = jnp.arange(merge * slots, dtype=jnp.int32)
    sender_patch = jnp.repeat(sender, merge)
    by_sender = (sender_patch[None, :] == patch[:, None] // merge) & (
        patch[None, :] % merge == patch[:, None] % merge
    )
    outgoing = select(saved_early[0], by_sender)
    device = jnp.arange(devices, dtype=jnp.int32)
    wanted = jnp.sum(
        jnp.where(sender[None, :] == device[:, None], place[None, :] + 1, 0), axis=1
    )
    tag = jnp.broadcast_to(wanted[:, None, None], (devices, merge, 128)).astype(BF16)
    message = jnp.concatenate([outgoing.reshape(devices, merge, width), tag], axis=2)
    arrived = lax.all_to_all(message, CTX, 0, 0, tiled=True)
    asked = arrived[:, 0, width].astype(jnp.int32) - 1
    asked_patch = jnp.repeat(asked, merge)
    token_patch = jnp.arange(merge * tokens, dtype=jnp.int32)
    by_token = (asked_patch[None, :] == token_patch[:, None] // merge) & (
        patch[None, :] % merge == token_patch[:, None] % merge
    )
    saved_rows = select(arrived[:, :, :width].reshape(devices * merge, width), by_token)

    rows = jnp.concatenate([early, middle, late], axis=1)
    packed = select(rows, by_token.T).reshape(devices, merge, 3 * width)
    landed = lax.all_to_all(packed, CTX, 0, 0, tiled=True).reshape(devices * merge, 3 * width)
    placed = select(landed, by_sender.T)
    rounded = jnp.stack([placed[:, i * width : (i + 1) * width] for i in range(3)])

    pieces = early.reshape(tokens * merge, xs * cores, share).swapaxes(0, 1)
    columns = lax.all_to_all(pieces, DP, 0, 0, tiled=True).reshape(-1, share)
    gathered = lax.all_gather(saved_rows, DP, axis=0, tiled=True)
    partial = lax.dot_general(
        gathered, columns, (((0,), (0,)), ((), ())), preferred_element_type=F32
    ).astype(BF16)
    terms = lax.all_to_all(
        partial.reshape(devices, width // devices * share), CTX, 0, 0, tiled=True
    )
    weights = jnp.sum(terms.astype(F32), axis=0).reshape(width // devices, share)

    out = contexts(jnp.full((1,), core, jnp.int32), rounded, own, other)
    return out[0][None], out[1][None], out[2][None], rounded[0][None], weights


def solution(mesh):
    shape = mesh.shape
    fine = Mesh(mesh.devices.reshape(shape["dp"] // 2, 2, -1, 4), ("x", "core", "z", "y"))
    rows = P(DP, CTX, None)
    return jax.shard_map(
        local,
        mesh=fine,
        in_specs=(rows, rows, rows, P(DP, CTX), rows, P(DP, None), P(DP, None), P(DP, None)),
        out_specs=(rows, rows, rows, rows, P(CTX, DP)),
        check_vma=False,
    )
```

time: 307 us -> 148 us (0.48)
  waiting for transfers between devices: 211 us -> 70.6 us
  blocking collectives: 23.5 us -> 0 us
  starting transfers between devices: 12.3 us -> 32.1 us
  matrix products: 13.5 us -> 4.08 us
  local copies, waits for them, and re-layouts: 20.4 us -> 11.6 us
  Pallas kernels: 0 us -> 4.48 us
    unnamed x6 -> x2, waiting for transfers between devices: 162 us -> 0.03 us
    unnamed x1 -> x0, blocking collectives: 23.5 us -> none
    all_to_all x3 -> x4, waiting for transfers between devices: 27.9 us -> 50.1 us  [the longest x1 25 us: local(): lax.all_to_all(packed, CTX, 0, 0, tiled=True)]
    reduce_scatter x1 -> x0, waiting for transfers between devices: 21.8 us -> none  [local(): weights = lax.psum_scatter(row_share, 'dp', scatter_dimension=1, tiled=True)]
    all_gather x3 -> x2, waiting for transfers between devices: 0.02 us -> 20.5 us  [the longest x1 20.5 us: local(): own = lax.all_gather(stacked, 'x', axis=0)]
    all_to_all x3 -> x4, starting transfers between devices: 11.9 us -> 32.1 us  [the longest x1 11.5 us: local(): arrived = lax.all_to_all(message, CTX, 0, 0, tiled=True)]
    dot_general x4 -> x5, matrix products: 13.5 us -> 4.08 us  [the longest x4 2.25 us: select(): jnp.dot(table.astype(BF16), rows, preferred_element_type=F32).astype(BF16)]
    scatter x4 -> x0, local copies, waits for them, and re-layouts: 7.55 us -> none  [the longest x1 4.3 us: local(): target = jnp.zeros((visual_rows,), jnp.int32).at[local_row.reshape(-1)].s...]
  transfers between devices with their start and end apart: 8 -> 7, of which waited for: 5 -> 4; matrix products, arithmetic and copies ran while one was open for 12% -> 11% of each run, Pallas kernels for 0% -> 0%
where the time goes in v1:
time: 148 us; the launch traced here: 146 us
  waiting for transfers between devices  70.6 us (48%)
  starting transfers between devices  32.1 us (22%)
  between operations  15.8 us (11%)
  local copies, waits for them, and re-layouts  11.6 us (8%)
  other arithmetic  7.61 us (5%)
  Pallas kernels  4.48 us (3%)
  matrix products  4.08 us (3%)
    all_to_all x1, waiting for transfers between devices, local(): lax.all_to_all(packed, CTX, 0, 0, tiled=True)  25 us
    all_gather x1, waiting for transfers between devices, local(): own = lax.all_gather(stacked, 'x', axis=0)  20.5 us
    all_to_all x1, waiting for transfers between devices, local(): lax.all_to_all(partial.reshape(devices, width // devices * share), CTX, 0...  13.1 us
    all_to_all x1, waiting for transfers between devices, local(): arrived = lax.all_to_all(message, CTX, 0, 0, tiled=True)  12 us
    all_to_all x1, starting transfers between devices, local(): arrived = lax.all_to_all(message, CTX, 0, 0, tiled=True)  11.5 us
    all_to_all x1, starting transfers between devices, local(): lax.all_to_all(packed, CTX, 0, 0, tiled=True)  10.1 us
    all_to_all x1, starting transfers between devices, local(): lax.all_to_all(partial.reshape(devices, width // devices * share), CTX, 0...  5.72 us
    all_to_all x1, starting transfers between devices, local(): columns = lax.all_to_all(pieces, DP, 0, 0, tiled=True).reshape(-1, share)  4.78 us
  transfers between devices with their start and end apart: 7, of which 4 were waited for; matrix products, arithmetic and copies ran while one was open for 11% of the time, Pallas kernels for 0%

profile of v1, /device:TPU:6, one launch (start us, length us, event | category | flops | bytes accessed | tf_op | source)
XLA Modules:
  0.0 146.3 jit_solution(1796070634976786818)
XLA Ops:
  8.1 2.3 %pad_maximum_fusion = bf16[3,144,1152]{2,1,0:T(8,128)(2,1)} fusion(bf16[1,144,1152]{2,1,0:T(8,128)(2,1)} %bitcast.36, bf16[1,144,1152]{2,1,0:T(8,128)(2,1)} %bitcast.37, bf16[1,144,1152]{2,1,0:T(8,128)(2,1)} %bitcast.38), kind=kLoop, calls=%fused_computation.5 | loop fusion | flops 995328 | bytes 1990656 | tf_op jit(solution)/shard_map/stack | solution.py:89
  11.3 0.9 pad_maximum_fusion.2
  12.2 11.5 %all-to-all-start = ((bf16[32,4,1280]{2,1,0:T(4,128)(2,1)}), bf16[32,4,1280]{2,1,0:T(4,128)(2,1)S(1)}, u32[]{:S(2)}, u32[]{:S(2)}) async-start(bf16[32,4,1280]{2,1,0:T(4,128)(2,1)} %pad_maximum_fusion.2), calls=%async_computation | async-start | bytes 655360 | tf_op jit(solution)/shard_map/all_to_all | solution.py:114
  24.1 0.5 convert_element_type.87
  24.7 1.0 copy.22
  25.7 12.0 %all-to-all-done = bf16[32,4,1280]{2,1,0:T(4,128)(2,1)S(1)} async-done(((bf16[32,4,1280]{2,1,0:T(4,128)(2,1)}), bf16[32,4,1280]{2,1,0:T(4,128)(2,1)S(1)}, u32[]{:S(2)}, u32[]{:S(2)}) %all-to-all-start) | async-done | bytes 327712 | tf_op jit(solution)/shard_map/all_to_all | solution.py:114
  37.6 4.8 %all-to-all-start.2 = ((bf16[8,80,144]{1,2,0:T(8,128)(2,1)}), bf16[8,80,144]{1,2,0:T(8,128)(2,1)S(1)}, u32[]{:S(2)}, u32[]{:S(2)}) async-start(bf16[8,80,144]{1,2,0:T(8,128)(2,1)} %copy.22), calls=%async_computation.2 | async-start | bytes 589824 | tf_op jit(solution)/shard_map/all_to_all | solution.py:130
  42.6 0.7 fusion.24
  43.5 20.5 %all-gather.6.cloned.1.call-done = bf16[12,144,1152]{2,1,0:T(8,128)(2,1)} async-done(((bf16[3,144,1152]{2,1,0:T(8,128)(2,1)}), bf16[12,144,1152]{2,1,0:T(8,128)(2,1)}) %all-gather.6.cloned.1.call-update) | async-done | bytes 3981328 | tf_op jit(solution)/shard_map/all_gather | solution.py:90
  64.0 0.9 convolution_convert_fusion.4
  65.5 1.1 reshape.186
  66.7 10.1 %all-to-all-start.1 = ((bf16[32,4,3456]{2,1,0:T(4,128)(2,1)}), bf16[32,4,3456]{2,1,0:T(4,128)(2,1)S(1)}, u32[]{:S(2)}, u32[]{:S(2)}) async-start(bf16[32,4,3456]{2,1,0:T(4,128)(2,1)} %reshape.186), calls=%async_computation.1 | async-start | bytes 1769472 | tf_op jit(solution)/shard_map/all_to_all | solution.py:125
  77.1 25.0 %all-to-all-done.1 = bf16[32,4,3456]{2,1,0:T(4,128)(2,1)S(1)} async-done(((bf16[32,4,3456]{2,1,0:T(4,128)(2,1)}), bf16[32,4,3456]{2,1,0:T(4,128)(2,1)S(1)}, u32[]{:S(2)}, u32[]{:S(2)}) %all-to-all-start.1) | async-done | bytes 884768 | tf_op jit(solution)/shard_map/all_to_all | solution.py:125
  102.8 1.8 %convolution_convert_fusion.2 = bf16[1152,144]{0,1:T(8,128)(2,1)S(1)} fusion(bf16[640,144]{0,1:T(8,128)(2,1)S(1)} %reshape.189, bf16[640,1152]{1,0:T(8,128)(2,1)} %all-gather.4.cloned.1.call-done), kind=kOutput, calls=%fused_computation.2 | convolution fusion | flops 212502528 | bytes 1990656 | tf_op jit(solution)/shard_map/dot_general | solution.py:132
  104.9 1.1 all_to_all.20
  106.5 2.7 %reduce.3 = bf16[32,5184]{1,0:T(8,128)(2,1)S(1)} reduce(bf16[32,1,5184]{2,1,0:T(2,128)(2,1)S(1)} %all_to_all.20, bf16[]{:T(256)} %broadcast.201), dimensions={1}, to_apply=%all_to_all.20.reduce_sub_computation | reduce | bytes 663554 | tf_op jit(solution)/shard_map/all_to_all | solution.py:135
  109.2 1.2 reshape.195
  110.4 5.7 %all-to-all-start.3 = ((bf16[32,2,2592]{2,1,0:T(2,128)(2,1)}), bf16[32,2,2592]{2,1,0:T(2,128)(2,1)S(1)}, u32[]{:S(2)}, u32[]{:S(2)}) async-start(bf16[32,2,2592]{2,1,0:T(2,128)(2,1)} %reshape.195), calls=%async_computation.3 | async-start | bytes 688128 | tf_op jit(solution)/shard_map/all_to_all | solution.py:135
  116.3 13.1 %all-to-all-done.3 = bf16[32,2,2592]{2,1,0:T(2,128)(2,1)S(1)} async-done(((bf16[32,2,2592]{2,1,0:T(2,128)(2,1)}), bf16[32,2,2592]{2,1,0:T(2,128)(2,1)S(1)}, u32[]{:S(2)}, u32[]{:S(2)}) %all-to-all-start.3) | async-done | bytes 331808 | tf_op jit(solution)/shard_map/all_to_all | solution.py:135
  129.9 0.6 convert_reduce_fusion
  130.6 0.7 reshape.190
  131.3 2.1 %copy-done.1 = bf16[12,144,1152]{2,1,0:T(8,128)(2,1)S(1)} copy-done((bf16[12,144,1152]{2,1,0:T(8,128)(2,1)S(1)}, bf16[12,144,1152]{2,1,0:T(8,128)(2,1)}, u32[]{:S(2)}) %copy-start.1) | copy-done | bytes 3981336
  133.4 4.5 %shard_map.119 = bf16[3,128,1152]{2,1,0:T(8,128)(2,1)S(1)} custom-call(s32[1]{0:T(128)} %bitcast.core_ref, bf16[3,128,1152]{2,1,0:T(8,128)(2,1)S(1)} %pad_maximum_fusion.1.rounded_ref, bf16[4,3,144,1152]{3,2,1,0:T(8,128)(2,1)S(1)} %bitcast.34, bf16[4,3,144,1152]{3,2,1,0:T(8,128)(2,1)} %collective-permute-done.other_ref), custom_call_target="tpu_custom_call" | custom-call | flops 1019215872 | bytes 7962624 | tf_op jit(solution)/shard_map/pallas_call | solution.py:47
  137.9 0.9 fusion.29
  (51 shorter events, 4.8 us)
Async XLA Ops:
  8.0 2.8 %copy-start = (bf16[1,128,1152]{2,1,0:T(8,128)(2,1)S(1)}, bf16[1,128,1152]{2,1,0:T(8,128)(2,1)}, u32[]{:S(2)}) copy-start(bf16[1,128,1152]{2,1,0:T(8,128)(2,1)} %param.12) | copy-start | bytes 884740
  8.0 56.0 %all-gather.6.cloned.1.call-start = ((), (), s32[]{:S(2)}) async-start(), calls=%async_computation.5 | async-start | bytes 4976640 | tf_op jit(solution)/shard_map/all_gather | solution.py:90
  8.1 2.3 %copy-start.6 = (s32[1,32]{1,0:T(1,128)S(1)}, s32[1,32]{1,0:T(1,128)}, u32[]{:S(2)}) copy-start(s32[1,32]{1,0:T(1,128)} %param.11) | copy-start | bytes 388
  10.4 13.2 %copy-start.3 = (bf16[1,20,4608]{2,1,0:T(8,128)(2,1)S(1)}, bf16[1,20,4608]{2,1,0:T(8,128)(2,1)}, u32[]{:S(2)}) copy-start(bf16[1,20,4608]{2,1,0:T(8,128)(2,1)} %param.10) | copy-start | bytes 552964
  10.4 13.2 %copy-start.4 = (bf16[1,20,4608]{2,1,0:T(8,128)(2,1)S(1)}, bf16[1,20,4608]{2,1,0:T(8,128)(2,1)}, u32[]{:S(2)}) copy-start(bf16[1,20,4608]{2,1,0:T(8,128)(2,1)} %param.8) | copy-start | bytes 552964
  10.4 13.2 %copy-start.5 = (bf16[1,20,4608]{2,1,0:T(8,128)(2,1)S(1)}, bf16[1,20,4608]{2,1,0:T(8,128)(2,1)}, u32[]{:S(2)}) copy-start(bf16[1,20,4608]{2,1,0:T(8,128)(2,1)} %param.9) | copy-start | bytes 552964
  12.2 25.5 %all-to-all-start = ((bf16[32,4,1280]{2,1,0:T(4,128)(2,1)}), bf16[32,4,1280]{2,1,0:T(4,128)(2,1)S(1)}, u32[]{:S(2)}, u32[]{:S(2)}) async-start(bf16[32,4,1280]{2,1,0:T(4,128)(2,1)} %pad_maximum_fusion.2), calls=%async_computation | async-start | bytes 655360 | tf_op jit(solution)/shard_map/all_to_all | solution.py:114
  37.6 29.0 %all-to-all-start.2 = ((bf16[8,80,144]{1,2,0:T(8,128)(2,1)}), bf16[8,80,144]{1,2,0:T(8,128)(2,1)S(1)}, u32[]{:S(2)}, u32[]{:S(2)}) async-start(bf16[8,80,144]{1,2,0:T(8,128)(2,1)} %copy.22), calls=%async_computation.2 | async-start | bytes 589824 | tf_op jit(solution)/shard_map/all_to_all | solution.py:130
  42.4 60.3 %all-gather.4.cloned.1.call-start = ((), (), s32[]{:S(2)}) async-start(), calls=%async_computation.4 | async-start | bytes 1658880 | tf_op jit(solution)/shard_map/all_gather | solution.py:131
  64.0 67.3 %collective-permute-start = (bf16[4,3,144,1152]{3,2,1,0:T(8,128)(2,1)}, bf16[4,3,144,1152]{3,2,1,0:T(8,128)(2,1)}, u32[]{:S(2)}, u32[]{:S(2)}) collective-permute-start(bf16[4,3,144,1152]{3,2,1,0:T(8,128)(2,1)} %bitcast.33), channel_id=1, source_target_pairs={{0,32},{32,0},{1,33},{33,1},{2,34},{34,2},{3,35},{35,3},{4,36},{36... | collective-permute-start | bytes 11943944 | tf_op jit(solution)/shard_map/ppermute | solution.py:91
  66.7 35.4 %all-to-all-start.1 = ((bf16[32,4,3456]{2,1,0:T(4,128)(2,1)}), bf16[32,4,3456]{2,1,0:T(4,128)(2,1)S(1)}, u32[]{:S(2)}, u32[]{:S(2)}) async-start(bf16[32,4,3456]{2,1,0:T(4,128)(2,1)} %reshape.186), calls=%async_computation.1 | async-start | bytes 1769472 | tf_op jit(solution)/shard_map/all_to_all | solution.py:125
  110.4 19.1 %all-to-all-start.3 = ((bf16[32,2,2592]{2,1,0:T(2,128)(2,1)}), bf16[32,2,2592]{2,1,0:T(2,128)(2,1)S(1)}, u32[]{:S(2)}, u32[]{:S(2)}) async-start(bf16[32,2,2592]{2,1,0:T(2,128)(2,1)} %reshape.195), calls=%async_computation.3 | async-start | bytes 688128 | tf_op jit(solution)/shard_map/all_to_all | solution.py:135
  116.2 14.4 %copy-start.2 = (bf16[1,128,1152]{2,1,0:T(8,128)(2,1)}, bf16[1,128,1152]{2,1,0:T(8,128)(2,1)S(1)}, u32[]{:S(2)}) copy-start(bf16[1,128,1152]{2,1,0:T(8,128)(2,1)S(1)} %get-tuple-element.8) | copy-start | bytes 884740
  131.3 2.1 %copy-start.1 = (bf16[12,144,1152]{2,1,0:T(8,128)(2,1)S(1)}, bf16[12,144,1152]{2,1,0:T(8,128)(2,1)}, u32[]{:S(2)}) copy-start(bf16[12,144,1152]{2,1,0:T(8,128)(2,1)} %all-gather.6.cloned.1.call-done) | copy-start | bytes 11943940
Sparse Core Ops, SparseCore 0:
  10.7 53.2 all-gather.5
Sparse Core Ops, SparseCore 1:
  65.0 27.2 all-gather.3

commit v2 on v1

v2 whole, which is shorter than its diff:
```python
import jax
import jax.numpy as jnp
from jax import lax
from jax.experimental import pallas as pl
from jax.experimental.pallas import tpu as pltpu
from jax.sharding import Mesh, PartitionSpec as P

DP = ("x", "core")
CTX = ("z", "y")
BF16 = jnp.bfloat16
F32 = jnp.float32
VMEM = pl.BlockSpec(memory_space=pltpu.VMEM)
SMEM = pl.BlockSpec(memory_space=pltpu.SMEM)
ANY = pl.BlockSpec(memory_space=pl.ANY)


def over_x(array, step):
    size = lax.axis_size("x")
    return lax.ppermute(array, "x", [(i, (i + step) % size) for i in range(size)])


def over_core(array):
    return lax.ppermute(array, "core", [(0, 1), (1, 0)])


def select(rows, table):
    return jnp.dot(table.astype(BF16), rows, preferred_element_type=F32).astype(BF16)


def context_kernel(shard, cut, at_ref, table_ref, landed_ref, *refs):
    pieces = refs[:10]
    early_out, middle_out, late_out, stream_out, weight, sem = refs[10:]
    x, core = at_ref[0], at_ref[1]
    width = weight.shape[1]
    copies = ([], [], [])

    def put(ref, first, rows, m, inside, of_x, of_core):
        base = pl.multiple_of((2 * of_x + of_core) * shard + inside, 16)
        copies[m].append(
            pltpu.make_async_copy(
                ref.at[pl.ds(first, rows)], weight.at[m, pl.ds(base, rows)], sem.at[m]
            )
        )

    for index, of_core in ((0, core), (5, 1 - core)):
        for k, step in enumerate((0, 3, 1)):
            of_x = lax.rem(x + step, 4)
            for m in range(3):
                put(pieces[index + k], m * shard, shard, m, 0, of_x, of_core)
        of_x = lax.rem(x + 2, 4)
        for ref, start, stop in ((pieces[index + 3], 0, cut), (pieces[index + 4], cut, 3 * shard)):
            for m in range(3):
                low, high = max(start, m * shard), min(stop, (m + 1) * shard)
                if low < high:
                    put(ref, low - start, high - low, m, low - m * shard, of_x, of_core)
    for m in range(3):
        for copy in copies[m]:
            copy.start()
    rounded = jnp.dot(
        table_ref[...], landed_ref[...], preferred_element_type=F32
    ).astype(BF16)
    stream_out[...] = rounded[:, :width]
    for m, out in enumerate((early_out, middle_out, late_out)):
        for copy in copies[m]:
            copy.wait()
        out[...] = lax.dot_general(
            rounded[:, m * width : (m + 1) * width],
            weight[m],
            (((1,), (1,)), ((), ())),
            preferred_element_type=F32,
        ).astype(BF16)


def contexts(at, table, landed, pieces, shard, cut):
    rows, width = table.shape[0], landed.shape[1] // 3
    out = jax.ShapeDtypeStruct((rows, width), BF16)
    return pl.pallas_call(
        lambda *refs: context_kernel(shard, cut, *refs),
        out_shape=(out,) * 4,
        in_specs=[SMEM, VMEM, VMEM] + [ANY] * 10,
        out_specs=(VMEM,) * 4,
        scratch_shapes=[
            pltpu.VMEM((3, width, width), BF16),
            pltpu.SemaphoreType.DMA((3,)),
        ],
        compiler_params=pltpu.CompilerParams(vmem_limit_bytes=32 << 20),
        cost_estimate=pl.CostEstimate(
            flops=6 * rows * width * width, bytes_accessed=6 * width * width, transcendentals=0
        ),
    )(at, table, landed, *pieces)


def gradient_kernel(saved0, saved1, saved2, saved3, keep, give, keep_out, give_out):
    saved = (saved0, saved1, saved2, saved3)

    def product(columns):
        return sum(
            lax.dot_general(
                saved[k][...], columns[k], (((0,), (0,)), ((), ())), preferred_element_type=F32
            )
            for k in range(4)
        )

    give_out[...] = product(give).astype(BF16)
    keep_out[...] = product(keep)


def gradient(saved, keep, give):
    width, share = saved[0].shape[1], keep.shape[2]
    return pl.pallas_call(
        gradient_kernel,
        out_shape=(
            jax.ShapeDtypeStruct((width, share), F32),
            jax.ShapeDtypeStruct((width, share), BF16),
        ),
        in_specs=[VMEM] * 6,
        out_specs=(VMEM,) * 2,
        compiler_params=pltpu.CompilerParams(vmem_limit_bytes=32 << 20),
    )(*saved, keep, give)


def local(
    injected_early,
    injected_middle,
    injected_late,
    slot_source,
    saved_early,
    projection_early,
    projection_middle,
    projection_late,
):
    devices = lax.axis_size(CTX)
    x, core = lax.axis_index("x"), lax.axis_index("core")
    tokens, merged = injected_early.shape[1:]
    slots = slot_source.shape[1]
    width = saved_early.shape[2]
    merge = merged // width
    shard = projection_early.shape[0]
    share = width // 8

    stacked = jnp.concatenate([projection_early, projection_middle, projection_late])
    cut = -(-stacked.shape[0] // 32) * 16
    from_left, from_right = over_x(stacked, 1), over_x(stacked, 3)
    far_left, far_right = over_x(from_left[:cut], 1), over_x(from_right[cut:], 3)
    pieces = (stacked, from_left, from_right, far_left, far_right)
    pieces = pieces + tuple(over_core(piece) for piece in pieces)

    late = injected_late[0].reshape(tokens * merge, width)
    middle32 = late.astype(F32) + injected_middle[0].reshape(tokens * merge, width).astype(F32)
    early32 = middle32 + injected_early[0].reshape(tokens * merge, width).astype(F32)
    middle, early = middle32.astype(BF16), early32.astype(BF16)

    columns = early.reshape(tokens * merge, 4, 2, share).transpose(1, 2, 0, 3)
    columns = jnp.where(core == 0, columns, columns[:, ::-1])
    shares = [
        lax.dynamic_index_in_dim(columns, (x + step) % 4, 0, keepdims=False) for step in range(4)
    ]
    shares = [shares[0]] + [over_x(shares[step], step) for step in (1, 2, 3)]
    keep = jnp.stack([piece[0] for piece in shares])
    give = jnp.stack([piece[1] for piece in shares])

    source = slot_source[0]
    filled = source >= 0
    sender = jnp.where(filled, source // tokens, -1)
    place = jnp.where(filled, source % tokens, 0)
    patch = jnp.arange(merge * slots, dtype=jnp.int32)
    sender_patch = jnp.repeat(sender, merge)
    by_sender = (sender_patch[None, :] == patch[:, None] // merge) & (
        patch[None, :] % merge == patch[:, None] % merge
    )
    outgoing = select(saved_early[0], by_sender)
    device = jnp.arange(devices, dtype=jnp.int32)
    wanted = jnp.sum(
        jnp.where(sender[None, :] == device[:, None], place[None, :] + 1, 0), axis=1
    )
    tag = jnp.broadcast_to(wanted[:, None, None], (devices, merge, 128)).astype(BF16)
    message = jnp.concatenate([outgoing.reshape(devices, merge, width), tag], axis=2)
    arrived = lax.all_to_all(message, CTX, 0, 0, tiled=True)
    asked = arrived[:, 0, width].astype(jnp.int32) - 1
    asked_patch = jnp.repeat(asked, merge)
    token_patch = jnp.arange(merge * tokens, dtype=jnp.int32)
    by_token = (asked_patch[None, :] == token_patch[:, None] // merge) & (
        patch[None, :] % merge == token_patch[:, None] % merge
    )
    saved_rows = select(arrived[:, :, :width].reshape(devices * merge, width), by_token)

    rows = jnp.concatenate([early, middle, late], axis=1)
    packed = select(rows, by_token.T).reshape(devices, merge, 3 * width)
    landed = lax.all_to_all(packed, CTX, 0, 0, tiled=True).reshape(devices * merge, 3 * width)

    saved = [saved_rows] + [over_x(saved_rows, step) for step in (1, 2, 3)]
    kept, given = gradient(saved, keep, give)
    partial = (kept + over_core(given).astype(F32)).astype(BF16)
    terms = lax.all_to_all(
        partial.reshape(devices, width // devices * share), CTX, 0, 0, tiled=True
    )
    weights = jnp.sum(terms.astype(F32), axis=0).reshape(width // devices, share)

    context_early, context_middle, context_late, stream = contexts(
        jnp.stack([x, core]).astype(jnp.int32),
        by_sender.T.astype(BF16),
        landed,
        pieces,
        shard,
        cut,
    )
    return context_early[None], context_middle[None], context_late[None], stream[None], weights


def solution(mesh):
    fine = Mesh(mesh.devices.reshape(4, 2, 8, 4), ("x", "core", "z", "y"))
    rows = P(DP, CTX, None)
    return jax.shard_map(
        local,
        mesh=fine,
        in_specs=(rows, rows, rows, P(DP, CTX), rows, P(DP, None), P(DP, None), P(DP, None)),
        out_specs=(rows, rows, rows, rows, P(CTX, DP)),
        check_vma=False,
    )
```

time: 148 us -> 127 us (0.86)
  waiting for transfers between devices: 70.6 us -> 46 us
  between operations: 15.8 us -> 1.25 us
  local copies, waits for them, and re-layouts: 11.6 us -> 23.6 us
  starting transfers between devices: 32.1 us -> 36.3 us
  matrix products: 4.08 us -> 1.06 us
  Pallas kernels: 4.48 us -> 7.31 us
  other arithmetic: 7.61 us -> 9.61 us
    all_gather x2 -> x0, waiting for transfers between devices: 20.5 us -> none  [the longest x1 20.5 us: local(): own = lax.all_gather(stacked, 'x', axis=0)]
    all_to_all x1, waiting for transfers between devices: 25 us -> 4.62 us  [local(): lax.all_to_all(packed, CTX, 0, 0, tiled=True)]
    ppermute x1 -> x16, waiting for transfers between devices: 0.01 us -> 16.2 us  [the longest x10 16.1 us: over_x(): lax.ppermute(array, 'x', [(i, (i + step) % size) for i in range(size)])]
    ppermute x1 -> x16, starting transfers between devices: 0.01 us -> 15.1 us  [the longest x10 14.1 us: over_x(): lax.ppermute(array, 'x', [(i, (i + step) % size) for i in range(size)])]
    all_to_all x1, starting transfers between devices: 10.1 us -> 4.63 us  [local(): lax.all_to_all(packed, CTX, 0, 0, tiled=True)]
    all_to_all x1 -> x0, starting transfers between devices: 4.78 us -> none  [local(): columns = lax.all_to_all(pieces, DP, 0, 0, tiled=True).reshape(-1, share)]
    pallas_call x1 -> x2, Pallas kernels: 4.48 us -> 7.31 us  [the longest x1 5.9 us: contexts(): pl.pallas_call(lambda *refs: context_kernel(shard, cut, *refs), out_shape...]
    unnamed x16 -> x20, local copies, waits for them, and re-layouts: 3.81 us -> 6.37 us
  transfers between devices with their start and end apart: 7 -> 19, of which waited for: 4 -> 7; matrix products, arithmetic and copies ran while one was open for 11% -> 23% of each run, Pallas kernels for 0% -> 0%
where the time goes in v2:
time: 127 us; the launch traced here: 125 us
  waiting for transfers between devices  46 us (36%)
  starting transfers between devices  36.3 us (29%)
  local copies, waits for them, and re-layouts  23.6 us (19%)
  other arithmetic  9.61 us (8%)
  Pallas kernels  7.31 us (6%)
    ppermute x10, waiting for transfers between devices, over_x(): lax.ppermute(array, 'x', [(i, (i + step) % size) for i in range(size)])  16.1 us
    ppermute x10, starting transfers between devices, over_x(): lax.ppermute(array, 'x', [(i, (i + step) % size) for i in range(size)])  14.1 us
    all_to_all x1, waiting for transfers between devices, local(): lax.all_to_all(partial.reshape(devices, width // devices * share), CTX, 0...  12.7 us
    all_to_all x1, waiting for transfers between devices, local(): arrived = lax.all_to_all(message, CTX, 0, 0, tiled=True)  12.6 us
    all_to_all x1, starting transfers between devices, local(): arrived = lax.all_to_all(message, CTX, 0, 0, tiled=True)  11.1 us
    unnamed x20, local copies, waits for them, and re-layouts  6.37 us
    pallas_call x1, Pallas kernels, contexts(): pl.pallas_call(lambda *refs: context_kernel(shard, cut, *refs), out_shape...  5.9 us
    all_to_all x1, starting transfers between devices, local(): lax.all_to_all(partial.reshape(devices, width // devices * share), CTX, 0...  5.4 us
  transfers between devices with their start and end apart: 19, of which 7 were waited for; matrix products, arithmetic and copies ran while one was open for 23% of the time, Pallas kernels for 0%

profile of v2, /device:TPU:6, one launch (start us, length us, event | category | flops | bytes accessed | tf_op | source)
XLA Modules:
  0.0 125.2 jit_solution(17793685502107093458)
XLA Ops:
  2.7 2.3 %collective-permute-start.12 = (bf16[2,80,144]{2,1,0:T(8,128)(2,1)S(1)}, bf16[2,80,144]{2,1,0:T(8,128)(2,1)S(1)}, u32[]{:S(2)}, u32[]{:S(2)}) collective-permute-start(bf16[2,80,144]{2,1,0:T(8,128)(2,1)S(1)} %get-tuple-element.21), channel_id=1, source_target_pairs={{0,64},{64,128},{128,192},{192,0},{1,65},{65,129},{129,193},{193,1... | collective-permute-start | bytes 138248 | tf_op jit(solution)/shard_map/ppermute | solution.py:19
  5.0 1.6 %collective-permute-start.13 = (bf16[2,80,144]{2,1,0:T(8,128)(2,1)S(1)}, bf16[2,80,144]{2,1,0:T(8,128)(2,1)S(1)}, u32[]{:S(2)}, u32[]{:S(2)}) collective-permute-start(bf16[2,80,144]{2,1,0:T(8,128)(2,1)S(1)} %get-tuple-element.23), channel_id=1, source_target_pairs={{0,128},{64,192},{128,0},{192,64},{1,129},{65,193},{129,1},{193,65... | collective-permute-start | bytes 138248 | tf_op jit(solution)/shard_map/ppermute | solution.py:19
  8.3 11.1 %all-to-all-start = ((bf16[32,4,1280]{2,1,0:T(4,128)(2,1)}), bf16[32,4,1280]{2,1,0:T(4,128)(2,1)S(1)}, u32[]{:S(2)}, u32[]{:S(2)}) async-start(bf16[32,4,1280]{2,1,0:T(4,128)(2,1)} %pad_maximum_fusion), calls=%async_computation | async-start | bytes 655360 | tf_op jit(solution)/shard_map/all_to_all | solution.py:178
  20.3 12.6 %all-to-all-done = bf16[32,4,1280]{2,1,0:T(4,128)(2,1)S(1)} async-done(((bf16[32,4,1280]{2,1,0:T(4,128)(2,1)}), bf16[32,4,1280]{2,1,0:T(4,128)(2,1)S(1)}, u32[]{:S(2)}, u32[]{:S(2)}) %all-to-all-start) | async-done | bytes 327712 | tf_op jit(solution)/shard_map/all_to_all | solution.py:178
  35.4 2.4 %collective-permute-start.10 = (bf16[80,1152]{1,0:T(8,128)(2,1)S(1)}, bf16[80,1152]{1,0:T(8,128)(2,1)S(1)}, u32[]{:S(2)}, u32[]{:S(2)}) collective-permute-start(bf16[80,1152]{1,0:T(8,128)(2,1)S(1)} %convolution_convert_fusion.2.saved0), channel_id=1, source_target_pairs={{0,128},{64,192},{128,0},{192,64},{1,129},{65,193},{129,1},{193,65... | collective-permute-start | bytes 552968 | tf_op jit(solution)/shard_map/ppermute | solution.py:19
  39.2 1.9 %collective-permute-done.11.saved3 = bf16[80,1152]{1,0:T(8,128)(2,1)S(1)} collective-permute-done((bf16[80,1152]{1,0:T(8,128)(2,1)S(1)}, bf16[80,1152]{1,0:T(8,128)(2,1)S(1)}, u32[]{:S(2)}, u32[]{:S(2)}) %collective-permute-start.11) | collective-permute-done | bytes 184352 | tf_op jit(solution)/shard_map/ppermute | solution.py:19
  41.0 2.3 %collective-permute-done.10.saved2 = bf16[80,1152]{1,0:T(8,128)(2,1)S(1)} collective-permute-done((bf16[80,1152]{1,0:T(8,128)(2,1)S(1)}, bf16[80,1152]{1,0:T(8,128)(2,1)S(1)}, u32[]{:S(2)}, u32[]{:S(2)}) %collective-permute-start.10) | collective-permute-done | bytes 184352 | tf_op jit(solution)/shard_map/ppermute | solution.py:19
  49.3 1.7 %collective-permute-start = (bf16[432,1152]{1,0:T(8,128)(2,1)}, bf16[432,1152]{1,0:T(8,128)(2,1)S(1)}, u32[]{:S(2)}, u32[]{:S(2)}) collective-permute-start(bf16[432,1152]{1,0:T(8,128)(2,1)} %constant_dynamic-update-slice_fusion.refs_3_), channel_id=1, source_target_pairs={{0,64},{64,128},{128,192},{192,0},{1,65},{65,129},{129,193},{193,1... | collective-permute-start | bytes 2985992 | tf_op jit(solution)/shard_map/ppermute | solution.py:19
  51.0 1.7 %reshape_squeeze.2 = bf16[80,1152]{1,0:T(8,128)(2,1)} reshape(bf16[1,20,4608]{2,1,0:T(8,128)(2,1)} %param.10) | data formatting | bytes 368640 | tf_op jit(solution)/shard_map/reshape;squeeze | solution.py:148
  52.7 1.8 %reshape.190 = f32[80,1152]{1,0:T(8,128)} reshape(bf16[1,20,4608]{2,1,0:T(8,128)(2,1)} %param.8) | data formatting | bytes 552960 | tf_op jit(solution)/shard_map/convert_element_type | solution.py:150
  54.5 1.8 %reshape.189 = f32[80,1152]{1,0:T(8,128)} reshape(bf16[1,20,4608]{2,1,0:T(8,128)(2,1)} %param.9) | data formatting | bytes 552960 | tf_op jit(solution)/shard_map/convert_element_type | solution.py:149
  56.3 2.0 %copy.22 = bf16[1152,144]{1,0:T(8,128)(2,1)} copy(bf16[1152,144]{0,1:T(8,128)(2,1)} %collective-permute-done.15) | data formatting | bytes 663552 | tf_op jit(solution)/shard_map/ppermute | solution.py:23
  58.3 2.1 %add_convert_fusion = bf16[1152,144]{1,0:T(8,128)(2,1)} fusion(f32[1152,144]{1,0:T(8,128)S(1)} %get-tuple-element.15, bf16[1152,144]{1,0:T(8,128)(2,1)} %copy.22), kind=kLoop, calls=%fused_computation.3 | loop fusion | flops 497664 | bytes 1327104 | tf_op jit(solution)/shard_map/convert_element_type | solution.py:193
  60.4 2.8 %all_to_all.16 = bf16[32,1,5184]{2,1,0:T(2,128)(2,1)S(1)} reshape(bf16[1152,144]{1,0:T(8,128)(2,1)} %add_convert_fusion) | data formatting | bytes 663552 | tf_op jit(solution)/shard_map/all_to_all | solution.py:194
  63.7 3.5 %reduce.3 = bf16[32,5184]{1,0:T(8,128)(2,1)} reduce(bf16[32,1,5184]{2,1,0:T(2,128)(2,1)S(1)} %all_to_all.16, bf16[]{:T(256)} %broadcast.209), dimensions={1}, to_apply=%all_to_all.16.reduce_sub_computation | reduce | bytes 663554 | tf_op jit(solution)/shard_map/all_to_all | solution.py:194
  67.2 2.1 %reshape.192 = bf16[32,2,2592]{2,1,0:T(2,128)(2,1)} reshape(bf16[32,5184]{1,0:T(8,128)(2,1)} %reduce.3) | data formatting | bytes 663552
  69.3 5.4 %all-to-all-start.2 = ((bf16[32,2,2592]{2,1,0:T(2,128)(2,1)}), bf16[32,2,2592]{2,1,0:T(2,128)(2,1)}, u32[]{:S(2)}, u32[]{:S(2)}) async-start(bf16[32,2,2592]{2,1,0:T(2,128)(2,1)} %reshape.192), calls=%async_computation.2 | async-start | bytes 688128 | tf_op jit(solution)/shard_map/all_to_all | solution.py:194
  76.5 12.7 %all-to-all-done.2 = bf16[32,2,2592]{2,1,0:T(2,128)(2,1)} async-done(((bf16[32,2,2592]{2,1,0:T(2,128)(2,1)}), bf16[32,2,2592]{2,1,0:T(2,128)(2,1)}, u32[]{:S(2)}, u32[]{:S(2)}) %all-to-all-start.2) | async-done | bytes 331808 | tf_op jit(solution)/shard_map/all_to_all | solution.py:194
  89.1 4.6 %all-to-all-start.1 = ((bf16[32,4,3456]{2,1,0:T(4,128)(2,1)}), bf16[32,4,3456]{2,1,0:T(4,128)(2,1)}, u32[]{:S(2)}, u32[]{:S(2)}) async-start(bf16[32,4,3456]{2,1,0:T(4,128)(2,1)} %reshape.185), calls=%async_computation.1 | async-start | bytes 1769472 | tf_op jit(solution)/shard_map/all_to_all | solution.py:189
  96.6 11.4 %collective-permute-done.3.refs_7_ = bf16[208,1152]{1,0:T(8,128)(2,1)} collective-permute-done((bf16[208,1152]{1,0:T(8,128)(2,1)S(1)}, bf16[208,1152]{1,0:T(8,128)(2,1)}, u32[]{:S(2)}, u32[]{:S(2)}) %collective-permute-start.3) | collective-permute-done | bytes 479264 | tf_op jit(solution)/shard_map/ppermute | solution.py:19
  108.7 2.7 %reshape.193 = bf16[32,1,5184]{2,1,0:T(2,128)(2,1)S(1)} reshape(bf16[32,2,2592]{2,1,0:T(2,128)(2,1)} %all-to-all-done.2) | data formatting | bytes 663552
  112.8 4.6 %all-to-all-done.1 = bf16[32,4,3456]{2,1,0:T(4,128)(2,1)} async-done(((bf16[32,4,3456]{2,1,0:T(4,128)(2,1)}), bf16[32,4,3456]{2,1,0:T(4,128)(2,1)}, u32[]{:S(2)}, u32[]{:S(2)}) %all-to-all-start.1) | async-done | bytes 884768 | tf_op jit(solution)/shard_map/all_to_all | solution.py:189
  117.4 1.6 %reshape.186.refs_2_ = bf16[128,3456]{1,0:T(8,128)(2,1)S(1)} reshape(bf16[32,4,3456]{2,1,0:T(4,128)(2,1)} %all-to-all-done.1) | data formatting | bytes 1769472 | tf_op jit(solution)/shard_map/reshape | solution.py:189
  119.1 5.9 %shard_map.119 = (bf16[128,1152]{1,0:T(8,128)(2,1)}, bf16[128,1152]{1,0:T(8,128)(2,1)}, bf16[128,1152]{1,0:T(8,128)(2,1)}, bf16[128,1152]{1,0:T(8,128)(2,1)}) custom-call(s32[2]{0:T(128)S(1)} %pad_add_fusion.refs_0_, bf16[128,128]{1,0:T(8,128)(2,1)S(1)} %and_convert_fusion.refs_1_, bf16[128,3456]{1,0:T(8,128)(2,1)S(1)} %reshape.186.refs_2_, ...), custom_call_target="tpu_custom_call" | custom-call | flops 1019215872 | bytes 7962624 | tf_op jit(solution)/shard_map/pallas_call | solution.py:77
  (85 shorter events, 21.3 us)
Async XLA Ops:
  2.7 17.5 %collective-permute-start.12 = (bf16[2,80,144]{2,1,0:T(8,128)(2,1)S(1)}, bf16[2,80,144]{2,1,0:T(8,128)(2,1)S(1)}, u32[]{:S(2)}, u32[]{:S(2)}) collective-permute-start(bf16[2,80,144]{2,1,0:T(8,128)(2,1)S(1)} %get-tuple-element.21), channel_id=1, source_target_pairs={{0,64},{64,128},{128,192},{192,0},{1,65},{65,129},{129,193},{193,1... | collective-permute-start | bytes 138248 | tf_op jit(solution)/shard_map/ppermute | solution.py:19
  5.0 15.3 %collective-permute-start.14 = (bf16[2,80,144]{2,1,0:T(8,128)(2,1)S(1)}, bf16[2,80,144]{2,1,0:T(8,128)(2,1)S(1)}, u32[]{:S(2)}, u32[]{:S(2)}) collective-permute-start(bf16[2,80,144]{2,1,0:T(8,128)(2,1)S(1)} %get-tuple-element.22), channel_id=1, source_target_pairs={{0,192},{64,0},{128,64},{192,128},{1,193},{65,1},{129,65},{193,129... | collective-permute-start | bytes 138248 | tf_op jit(solution)/shard_map/ppermute | solution.py:19
  5.0 34.0 %collective-permute-start.13 = (bf16[2,80,144]{2,1,0:T(8,128)(2,1)S(1)}, bf16[2,80,144]{2,1,0:T(8,128)(2,1)S(1)}, u32[]{:S(2)}, u32[]{:S(2)}) collective-permute-start(bf16[2,80,144]{2,1,0:T(8,128)(2,1)S(1)} %get-tuple-element.23), channel_id=1, source_target_pairs={{0,128},{64,192},{128,0},{192,64},{1,129},{65,193},{129,1},{193,65... | collective-permute-start | bytes 138248 | tf_op jit(solution)/shard_map/ppermute | solution.py:19
  6.9 12.5 %copy-start.4 = (bf16[144,1152]{1,0:T(8,128)(2,1)S(1)}, bf16[144,1152]{1,0:T(8,128)(2,1)}, u32[]{:S(2)}) copy-start(bf16[144,1152]{1,0:T(8,128)(2,1)} %param.13) | copy-start | bytes 995332
  8.3 24.6 %all-to-all-start = ((bf16[32,4,1280]{2,1,0:T(4,128)(2,1)}), bf16[32,4,1280]{2,1,0:T(4,128)(2,1)S(1)}, u32[]{:S(2)}, u32[]{:S(2)}) async-start(bf16[32,4,1280]{2,1,0:T(4,128)(2,1)} %pad_maximum_fusion), calls=%async_computation | async-start | bytes 655360 | tf_op jit(solution)/shard_map/all_to_all | solution.py:178
  34.2 6.8 %collective-permute-start.11 = (bf16[80,1152]{1,0:T(8,128)(2,1)S(1)}, bf16[80,1152]{1,0:T(8,128)(2,1)S(1)}, u32[]{:S(2)}, u32[]{:S(2)}) collective-permute-start(bf16[80,1152]{1,0:T(8,128)(2,1)S(1)} %convolution_convert_fusion.2.saved0), channel_id=1, source_target_pairs={{0,192},{64,0},{128,64},{192,128},{1,193},{65,1},{129,65},{193,129... | collective-permute-start | bytes 552968 | tf_op jit(solution)/shard_map/ppermute | solution.py:19
  35.4 7.9 %collective-permute-start.10 = (bf16[80,1152]{1,0:T(8,128)(2,1)S(1)}, bf16[80,1152]{1,0:T(8,128)(2,1)S(1)}, u32[]{:S(2)}, u32[]{:S(2)}) collective-permute-start(bf16[80,1152]{1,0:T(8,128)(2,1)S(1)} %convolution_convert_fusion.2.saved0), channel_id=1, source_target_pairs={{0,128},{64,192},{128,0},{192,64},{1,129},{65,193},{129,1},{193,65... | collective-permute-start | bytes 552968 | tf_op jit(solution)/shard_map/ppermute | solution.py:19
  37.8 6.0 %collective-permute-start.9 = (bf16[80,1152]{1,0:T(8,128)(2,1)S(1)}, bf16[80,1152]{1,0:T(8,128)(2,1)S(1)}, u32[]{:S(2)}, u32[]{:S(2)}) collective-permute-start(bf16[80,1152]{1,0:T(8,128)(2,1)S(1)} %convolution_convert_fusion.2.saved0), channel_id=1, source_target_pairs={{0,64},{64,128},{128,192},{192,0},{1,65},{65,129},{129,193},{193,1... | collective-permute-start | bytes 552968 | tf_op jit(solution)/shard_map/ppermute | solution.py:19
  39.1 7.2 %copy-start.5 = (bf16[144,1152]{1,0:T(8,128)(2,1)S(1)}, bf16[144,1152]{1,0:T(8,128)(2,1)}, u32[]{:S(2)}) copy-start(bf16[144,1152]{1,0:T(8,128)(2,1)} %param.14) | copy-start | bytes 995332
  46.2 10.1 %collective-permute-start.15 = (bf16[1152,144]{0,1:T(8,128)(2,1)}, bf16[1152,144]{0,1:T(8,128)(2,1)}, u32[]{:S(2)}, u32[]{:S(2)}) collective-permute-start(bf16[1152,144]{0,1:T(8,128)(2,1)} %copy.21), channel_id=1, source_target_pairs={{0,32},{32,0},{1,33},{33,1},{2,34},{34,2},{3,35},{35,3},{4,36},{36... | collective-permute-start | bytes 995336 | tf_op jit(solution)/shard_map/ppermute | solution.py:23
  47.7 47.6 %collective-permute-start.1 = (bf16[432,1152]{1,0:T(8,128)(2,1)}, bf16[432,1152]{1,0:T(8,128)(2,1)S(1)}, u32[]{:S(2)}, u32[]{:S(2)}) collective-permute-start(bf16[432,1152]{1,0:T(8,128)(2,1)} %constant_dynamic-update-slice_fusion.refs_3_), channel_id=1, source_target_pairs={{0,192},{64,0},{128,64},{192,128},{1,193},{65,1},{129,65},{193,129... | collective-permute-start | bytes 2985992 | tf_op jit(solution)/shard_map/ppermute | solution.py:19
  49.3 44.5 %collective-permute-start = (bf16[432,1152]{1,0:T(8,128)(2,1)}, bf16[432,1152]{1,0:T(8,128)(2,1)S(1)}, u32[]{:S(2)}, u32[]{:S(2)}) collective-permute-start(bf16[432,1152]{1,0:T(8,128)(2,1)} %constant_dynamic-update-slice_fusion.refs_3_), channel_id=1, source_target_pairs={{0,64},{64,128},{128,192},{192,0},{1,65},{65,129},{129,193},{193,1... | collective-permute-start | bytes 2985992 | tf_op jit(solution)/shard_map/ppermute | solution.py:19
  63.7 11.0 %copy-start.1 = (f32[80,1152]{1,0:T(8,128)S(1)}, f32[80,1152]{1,0:T(8,128)}, u32[]{:S(2)}) copy-start(f32[80,1152]{1,0:T(8,128)} %reshape.190) | copy-start | bytes 1105924
  63.7 11.0 %copy-start.3 = (bf16[80,1152]{1,0:T(8,128)(2,1)S(1)}, bf16[80,1152]{1,0:T(8,128)(2,1)}, u32[]{:S(2)}) copy-start(bf16[80,1152]{1,0:T(8,128)(2,1)} %reshape_squeeze.2) | copy-start | bytes 552964
  67.2 7.5 %copy-start.2 = (f32[80,1152]{1,0:T(8,128)S(1)}, f32[80,1152]{1,0:T(8,128)}, u32[]{:S(2)}) copy-start(f32[80,1152]{1,0:T(8,128)} %reshape.189) | copy-start | bytes 1105924
  69.3 19.8 %all-to-all-start.2 = ((bf16[32,2,2592]{2,1,0:T(2,128)(2,1)}), bf16[32,2,2592]{2,1,0:T(2,128)(2,1)}, u32[]{:S(2)}, u32[]{:S(2)}) async-start(bf16[32,2,2592]{2,1,0:T(2,128)(2,1)} %reshape.192), calls=%async_computation.2 | async-start | bytes 688128 | tf_op jit(solution)/shard_map/all_to_all | solution.py:194
  89.1 28.3 %all-to-all-start.1 = ((bf16[32,4,3456]{2,1,0:T(4,128)(2,1)}), bf16[32,4,3456]{2,1,0:T(4,128)(2,1)}, u32[]{:S(2)}, u32[]{:S(2)}) async-start(bf16[32,4,3456]{2,1,0:T(4,128)(2,1)} %reshape.185), calls=%async_computation.1 | async-start | bytes 1769472 | tf_op jit(solution)/shard_map/all_to_all | solution.py:189
  93.8 14.2 %collective-permute-start.2 = (bf16[224,1152]{1,0:T(8,128)(2,1)S(1)}, bf16[224,1152]{1,0:T(8,128)(2,1)}, u32[]{:S(2)}, u32[]{:S(2)}) collective-permute-start(bf16[224,1152]{1,0:T(8,128)(2,1)S(1)} %slice.57), channel_id=1, source_target_pairs={{0,64},{64,128},{128,192},{192,0},{1,65},{65,129},{129,193},{193,1... | collective-permute-start | bytes 1548296 | tf_op jit(solution)/shard_map/ppermute | solution.py:19
  95.4 12.6 %collective-permute-start.3 = (bf16[208,1152]{1,0:T(8,128)(2,1)S(1)}, bf16[208,1152]{1,0:T(8,128)(2,1)}, u32[]{:S(2)}, u32[]{:S(2)}) collective-permute-start(bf16[208,1152]{1,0:T(8,128)(2,1)S(1)} %slice.58), channel_id=1, source_target_pairs={{0,192},{64,0},{128,64},{192,128},{1,193},{65,1},{129,65},{193,129... | collective-permute-start | bytes 1437704 | tf_op jit(solution)/shard_map/ppermute | solution.py:19
  96.1 23.0 %collective-permute-start.4 = (bf16[432,1152]{1,0:T(8,128)(2,1)}, bf16[432,1152]{1,0:T(8,128)(2,1)}, u32[]{:S(2)}, u32[]{:S(2)}) collective-permute-start(bf16[432,1152]{1,0:T(8,128)(2,1)} %constant_dynamic-update-slice_fusion.refs_3_), channel_id=1, source_target_pairs={{0,32},{32,0},{1,33},{33,1},{2,34},{34,2},{3,35},{35,3},{4,36},{36... | collective-permute-start | bytes 2985992 | tf_op jit(solution)/shard_map/ppermute | solution.py:23
  96.1 23.0 %collective-permute-start.6 = (bf16[432,1152]{1,0:T(8,128)(2,1)S(1)}, bf16[432,1152]{1,0:T(8,128)(2,1)}, u32[]{:S(2)}, u32[]{:S(2)}) collective-permute-start(bf16[432,1152]{1,0:T(8,128)(2,1)S(1)} %collective-permute-done.1.refs_5_), channel_id=1, source_target_pairs={{0,32},{32,0},{1,33},{33,1},{2,34},{34,2},{3,35},{35,3},{4,36},{36... | collective-permute-start | bytes 2985992 | tf_op jit(solution)/shard_map/ppermute | solution.py:23
  96.6 22.5 %collective-permute-start.5 = (bf16[432,1152]{1,0:T(8,128)(2,1)S(1)}, bf16[432,1152]{1,0:T(8,128)(2,1)}, u32[]{:S(2)}, u32[]{:S(2)}) collective-permute-start(bf16[432,1152]{1,0:T(8,128)(2,1)S(1)} %collective-permute-done.refs_4_), channel_id=1, source_target_pairs={{0,32},{32,0},{1,33},{33,1},{2,34},{34,2},{3,35},{35,3},{4,36},{36... | collective-permute-start | bytes 2985992 | tf_op jit(solution)/shard_map/ppermute | solution.py:23
  108.0 11.0 %collective-permute-start.8 = (bf16[208,1152]{1,0:T(8,128)(2,1)}, bf16[208,1152]{1,0:T(8,128)(2,1)}, u32[]{:S(2)}, u32[]{:S(2)}) collective-permute-start(bf16[208,1152]{1,0:T(8,128)(2,1)} %collective-permute-done.3.refs_7_), channel_id=1, source_target_pairs={{0,32},{32,0},{1,33},{33,1},{2,34},{34,2},{3,35},{35,3},{4,36},{36... | collective-permute-start | bytes 1437704 | tf_op jit(solution)/shard_map/ppermute | solution.py:23
  108.0 11.1 %collective-permute-start.7 = (bf16[224,1152]{1,0:T(8,128)(2,1)}, bf16[224,1152]{1,0:T(8,128)(2,1)}, u32[]{:S(2)}, u32[]{:S(2)}) collective-permute-start(bf16[224,1152]{1,0:T(8,128)(2,1)} %collective-permute-done.2.refs_6_), channel_id=1, source_target_pairs={{0,32},{32,0},{1,33},{33,1},{2,34},{34,2},{3,35},{35,3},{4,36},{36... | collective-permute-start | bytes 1548296 | tf_op jit(solution)/shard_map/ppermute | solution.py:23
  (3 other events, 14.0 us)

commit v3 on v2

v3 whole, which is shorter than its diff:
```python
import jax
import jax.numpy as jnp
from jax import lax
from jax.experimental import pallas as pl
from jax.experimental.pallas import tpu as pltpu
from jax.sharding import Mesh, PartitionSpec as P

DP = ("x", "core")
CTX = ("z", "y")
BF16 = jnp.bfloat16
F32 = jnp.float32
VMEM = pl.BlockSpec(memory_space=pltpu.VMEM)
SMEM = pl.BlockSpec(memory_space=pltpu.SMEM)
ANY = pl.BlockSpec(memory_space=pl.ANY)
PARAMS = pltpu.CompilerParams(vmem_limit_bytes=32 << 20)

WIDTH = 1152
MERGE = 4
TOKENS = 20
SLOTS = 32
SHARD = 144
OWN = 36
SAVED_HALF = 640
ROWS_HALF = 1792
TERM_ROWS = 48
REST = 5


def over_x(array, step):
    return lax.ppermute(array, "x", [(i, (i + step) % 4) for i in range(4)])


def over_core(array):
    return lax.ppermute(array, "core", [(0, 1), (1, 0)])


def iota(shape, dim):
    return lax.broadcasted_iota(jnp.int32, shape, dim)


def onehot(condition):
    return jnp.where(condition, 1.0, 0.0).astype(BF16)


def matmul(a, b):
    return jnp.dot(a, b, preferred_element_type=F32)


def matmul_tn(a, b):
    return lax.dot_general(a, b, (((0,), (0,)), ((), ())), preferred_element_type=F32)


def quotient(value, by):
    return jnp.floor((value + 0.5) * (1.0 / by))


def message_kernel(slot_ref, saved_ref, message_ref, table_ref):
    source = slot_ref[...].astype(F32)
    sender = quotient(source, TOKENS)
    place = source - TOKENS * sender
    both = jnp.where(iota((8, SLOTS), 0) == 0, sender, place).astype(BF16)
    repeat = onehot(iota((SLOTS, SLOTS * MERGE), 1) // MERGE == iota((SLOTS, SLOTS * MERGE), 0))
    wide = matmul(both, repeat)
    sender, place = wide[0:1], wide[1:2]
    shape = (8 * SLOTS, MERGE * SLOTS)
    row, column = iota(shape, 0), iota(shape, 1)
    match = (sender == (row // 8).astype(F32)) & (row % MERGE == column % MERGE)
    first = match & (row % 8 < MERGE)
    second = match & (row % 8 >= MERGE)
    tag = jnp.sum(jnp.where(second, place + 1.0, 0.0), axis=1, keepdims=True)
    first, second = onehot(first), onehot(second)
    table_ref[:, : MERGE * SLOTS] = first
    table_ref[:, MERGE * SLOTS :] = second
    rest = WIDTH - SAVED_HALF
    left = matmul(first, saved_ref[:, :SAVED_HALF])
    right = matmul(second, saved_ref[:, SAVED_HALF:])
    message = jnp.concatenate([left[:, :rest] + right, left[:, rest:] + tag], axis=1)
    message_ref[...] = message.reshape(SLOTS, 8, SAVED_HALF).astype(BF16)


def make_message(slot, saved):
    return pl.pallas_call(
        message_kernel,
        out_shape=(
            jax.ShapeDtypeStruct((SLOTS, 8, SAVED_HALF), BF16),
            jax.ShapeDtypeStruct((8 * SLOTS, 2 * MERGE * SLOTS), BF16),
        ),
        in_specs=[VMEM] * 2,
        out_specs=(VMEM,) * 2,
        compiler_params=PARAMS,
    )(slot, saved)


def rows_kernel(at_ref, early_ref, middle_ref, late_ref, rows_ref, keep_ref, give_ref, sums):
    x, core = at_ref[0], at_ref[1]
    used = MERGE * TOKENS
    for j in range(MERGE):
        at = slice(j * WIDTH, (j + 1) * WIDTH)
        to = slice(j * TOKENS, (j + 1) * TOKENS)
        late = late_ref[:, at].astype(F32)
        middle = late + middle_ref[:, at].astype(F32)
        sums[to, 2 * WIDTH : 3 * WIDTH] = late
        sums[to, WIDTH : 2 * WIDTH] = middle
        sums[to, :WIDTH] = middle + early_ref[:, at].astype(F32)
    rows_ref[...] = jnp.zeros_like(rows_ref)
    rows_ref[:used, : 3 * WIDTH] = sums[...].astype(BF16)
    early = sums[:, :WIDTH]
    for d in range(8):
        main = early[:, d * SHARD : d * SHARD + 128]
        rest = early[:, d * SHARD + 128 : (d + 1) * SHARD]
        piece = jnp.concatenate([main] + [rest] * 8, axis=1).astype(BF16)
        step = lax.rem(d // 2 + 4 - x, 4)

        @pl.when(core == d % 2)
        def _():
            keep_ref[step] = piece

        @pl.when(core != d % 2)
        def _():
            give_ref[step] = piece


def make_rows(at, early, middle, late):
    piece = jax.ShapeDtypeStruct((4, MERGE * TOKENS, 256), BF16)
    return pl.pallas_call(
        rows_kernel,
        out_shape=(jax.ShapeDtypeStruct((128, 2 * ROWS_HALF), BF16), piece, piece),
        in_specs=[SMEM] + [VMEM] * 3,
        out_specs=(VMEM,) * 3,
        scratch_shapes=[pltpu.VMEM((MERGE * TOKENS, 3 * WIDTH), F32)],
        compiler_params=PARAMS,
    )(at, early, middle, late)


def pack_kernel(arrived_ref, rows_ref, saved_ref, packed_ref):
    count = 8 * SLOTS
    arrived = arrived_ref[...].astype(F32).reshape(count, SAVED_HALF).astype(BF16)
    rest = WIDTH - SAVED_HALF
    row, column = iota((count, count), 0), iota((count, count), 1)
    spread = onehot((row // 8 == column // 8) & (column % 8 == MERGE))
    asked = matmul(spread, arrived[:, rest:])
    row, column = iota((count, 128), 0), iota((count, 128), 1)
    j = sum((column >= k * TOKENS).astype(jnp.int32) for k in range(1, MERGE + 1))
    token = (column - TOKENS * j + 1).astype(F32)
    match = (asked == token) & (row % MERGE == j)
    first = onehot(match & (row % 8 < MERGE))
    second = onehot(match & (row % 8 >= MERGE))
    packed = matmul(first, rows_ref[:, :ROWS_HALF]) + matmul(second, rows_ref[:, ROWS_HALF:])
    packed_ref[...] = packed.reshape(SLOTS, 8, ROWS_HALF).astype(BF16)
    used = MERGE * TOKENS
    saved_ref[:, :SAVED_HALF] = matmul_tn(first, arrived)[:used].astype(BF16)
    saved_ref[:, SAVED_HALF:] = matmul_tn(second, arrived[:, :rest])[:used].astype(BF16)


def pack(arrived, rows):
    return pl.pallas_call(
        pack_kernel,
        out_shape=(
            jax.ShapeDtypeStruct((MERGE * TOKENS, WIDTH), BF16),
            jax.ShapeDtypeStruct((SLOTS, 8, ROWS_HALF), BF16),
        ),
        in_specs=[VMEM] * 2,
        out_specs=(VMEM,) * 2,
        compiler_params=PARAMS,
    )(arrived, rows)


def gradient_kernel(*refs):
    own, other, columns = refs[:4], refs[4:8], refs[8:12]
    terms_ref, product = refs[12:]
    saved = jnp.concatenate([ref[...] for k in range(4) for ref in (own[k], other[k])], axis=0)
    product[...] = matmul_tn(saved, jnp.concatenate([ref[...] for ref in columns], axis=0))
    line = iota((WIDTH, 128), 0).astype(F32)
    inside = line - OWN * quotient(line, OWN)
    group = (iota((WIDTH, 128), 1) // 16).astype(F32)
    rest = jnp.where(inside - 8 * quotient(inside, 8) == group, product[:, 128:], 0.0)
    line = iota((1, WIDTH), 1).astype(F32)
    block = quotient(line, OWN)
    to = REST * block + quotient(line - OWN * block, 8)
    fold = onehot(iota((REST * SLOTS, WIDTH), 0).astype(F32) == to)
    folded = matmul(fold, rest.astype(BF16))
    fill = jnp.zeros((TERM_ROWS - OWN - REST, 128), F32)
    for c in range(SLOTS):
        main = product[c * OWN : (c + 1) * OWN, :128]
        message = jnp.concatenate([main, folded[c * REST : (c + 1) * REST], fill], axis=0)
        terms_ref[c] = message.astype(BF16)


def gradient(own, other, columns):
    return pl.pallas_call(
        gradient_kernel,
        out_shape=jax.ShapeDtypeStruct((SLOTS, TERM_ROWS, 128), BF16),
        in_specs=[VMEM] * 12,
        out_specs=VMEM,
        scratch_shapes=[pltpu.VMEM((WIDTH, 256), F32)],
        compiler_params=PARAMS,
    )(*own, *other, *columns)


def total_kernel(terms_ref, out_ref):
    total = terms_ref[0].astype(F32)
    for c in range(1, SLOTS):
        total = total + terms_ref[c].astype(F32)
    rest = jnp.concatenate(
        [jnp.broadcast_to(total[OWN + a : OWN + a + 1], (8, 128)) for a in range(REST)], axis=0
    )[:OWN]
    line, column = iota((OWN, 128), 0), iota((OWN, 128), 1)
    rest = jnp.where(line % 8 == column // 16, rest, 0.0)
    for shift in (64, 32, 16):
        rest = rest + pltpu.roll(rest, shift, 1)
    out_ref[:, :128] = total[:OWN]
    out_ref[:, 128:] = rest[:, : SHARD - 128]


def add_up(terms):
    return pl.pallas_call(
        total_kernel,
        out_shape=jax.ShapeDtypeStruct((OWN, SHARD), F32),
        in_specs=[VMEM],
        out_specs=VMEM,
        compiler_params=PARAMS,
    )(terms)


def context_kernel(cut, at_ref, table_ref, landed_ref, *refs):
    pieces = refs[:10]
    early_out, middle_out, late_out, stream_out, weight, sem = refs[10:]
    x, core = at_ref[0], at_ref[1]
    copies = ([], [], [])

    def put(ref, first, rows, m, inside, of_x, of_core):
        base = pl.multiple_of((2 * of_x + of_core) * SHARD + inside, 16)
        copies[m].append(
            pltpu.make_async_copy(
                ref.at[pl.ds(first, rows)], weight.at[m, pl.ds(base, rows)], sem.at[m]
            )
        )

    for index, of_core in ((0, core), (5, 1 - core)):
        for k, step in enumerate((0, 3, 1)):
            for m in range(3):
                put(pieces[index + k], m * SHARD, SHARD, m, 0, lax.rem(x + step, 4), of_core)
        of_x = lax.rem(x + 2, 4)
        for ref, start, stop in ((pieces[index + 3], 0, cut), (pieces[index + 4], cut, 3 * SHARD)):
            for m in range(3):
                low, high = max(start, m * SHARD), min(stop, (m + 1) * SHARD)
                if low < high:
                    put(ref, low - start, high - low, m, low - m * SHARD, of_x, of_core)
    for m in range(3):
        for copy in copies[m]:
            copy.start()
    landed = landed_ref[...].astype(F32).reshape(8 * SLOTS, ROWS_HALF).astype(BF16)
    placed = matmul_tn(table_ref[...], landed).astype(BF16)
    half = MERGE * SLOTS
    placed = jnp.concatenate([placed[:half], placed[half:, : 3 * WIDTH - ROWS_HALF]], axis=1)
    stream_out[...] = placed[:, :WIDTH]
    for m, out in enumerate((early_out, middle_out, late_out)):
        for copy in copies[m]:
            copy.wait()
        out[...] = lax.dot_general(
            placed[:, m * WIDTH : (m + 1) * WIDTH],
            weight[m],
            (((1,), (1,)), ((), ())),
            preferred_element_type=F32,
        ).astype(BF16)


def contexts(at, table, landed, pieces, cut):
    rows = MERGE * SLOTS
    out = jax.ShapeDtypeStruct((rows, WIDTH), BF16)
    return pl.pallas_call(
        lambda *refs: context_kernel(cut, *refs),
        out_shape=(out,) * 4,
        in_specs=[SMEM, VMEM, VMEM] + [ANY] * 10,
        out_specs=(VMEM,) * 4,
        scratch_shapes=[
            pltpu.VMEM((3, WIDTH, WIDTH), BF16),
            pltpu.SemaphoreType.DMA((3,)),
        ],
        compiler_params=PARAMS,
        cost_estimate=pl.CostEstimate(
            flops=6 * rows * WIDTH * WIDTH, bytes_accessed=6 * WIDTH * WIDTH, transcendentals=0
        ),
    )(at, table, landed, *pieces)


def local(
    injected_early,
    injected_middle,
    injected_late,
    slot_source,
    saved_early,
    projection_early,
    projection_middle,
    projection_late,
):
    at = jnp.stack([lax.axis_index("x"), lax.axis_index("core")]).astype(jnp.int32)

    message, table = make_message(slot_source, saved_early[0])
    arrived = lax.all_to_all(message, CTX, 0, 0, tiled=True)

    stacked = jnp.concatenate([projection_early, projection_middle, projection_late])
    cut = 224
    from_left, from_right = over_x(stacked, 1), over_x(stacked, 3)
    rows, keep, give = make_rows(at, injected_early[0], injected_middle[0], injected_late[0])
    arrived, rows, from_left, from_right = lax.optimization_barrier(
        (arrived, rows, from_left, from_right)
    )
    far_left, far_right = over_x(from_left[:cut], 1), over_x(from_right[cut:], 3)
    pieces = (stacked, from_left, from_right, far_left, far_right)
    pieces = pieces + tuple(over_core(piece) for piece in pieces)

    given = over_core(give)
    mixed = [jnp.concatenate([keep[step], given[step]]) for step in range(4)]
    columns = [mixed[0]] + [over_x(mixed[step], step) for step in (1, 2, 3)]

    saved_rows, packed = pack(arrived, rows)
    landed = lax.all_to_all(packed, CTX, 0, 0, tiled=True)

    own = [saved_rows] + [over_x(saved_rows, step) for step in (1, 2, 3)]
    other = [over_core(piece) for piece in own]
    own, other, columns, landed = lax.optimization_barrier((own, other, columns, landed))
    terms = lax.all_to_all(gradient(own, other, columns), CTX, 0, 0, tiled=True)
    weights = add_up(terms)

    context_early, context_middle, context_late, stream = contexts(at, table, landed, pieces, cut)
    return context_early[None], context_middle[None], context_late[None], stream[None], weights


def solution(mesh):
    fine = Mesh(mesh.devices.reshape(4, 2, 8, 4), ("x", "core", "z", "y"))
    rows = P(DP, CTX, None)
    return jax.shard_map(
        local,
        mesh=fine,
        in_specs=(rows, rows, rows, P(DP, CTX), rows, P(DP, None), P(DP, None), P(DP, None)),
        out_specs=(rows, rows, rows, rows, P(CTX, DP)),
        check_vma=False,
    )
```

time: 127 us -> 110 us (0.87)
  waiting for transfers between devices: 46 us -> 31.6 us
  other arithmetic: 9.61 us -> 0.1 us
  starting transfers between devices: 36.3 us -> 45 us
  local copies, waits for them, and re-layouts: 23.6 us -> 18.3 us
  Pallas kernels: 7.31 us -> 11.7 us
    all_to_all x2, waiting for transfers between devices: 17.3 us -> 6.43 us  [the longest x1 6.43 us: local(): terms = lax.all_to_all(gradient(own, other, columns), CTX, 0, 0, tiled=True)]
    unnamed x20 -> x60, local copies, waits for them, and re-layouts: 6.37 us -> 15.9 us
    all_to_all x2, starting transfers between devices: 10 us -> 16.5 us  [the longest x1 9.91 us: local(): terms = lax.all_to_all(gradient(own, other, columns), CTX, 0, 0, tiled=True)]
    ppermute x10, waiting for transfers between devices: 16.1 us -> 10.8 us  [over_x(): return lax.ppermute(array, 'x', [(i, (i + step) % 4) for i in range(4)])]
    pallas_call x2 -> x6, Pallas kernels: 7.31 us -> 11.7 us  [the longest x1 6.26 us: contexts(): pl.pallas_call(lambda *refs: context_kernel(cut, *refs), out_shape=(out,)...]
    convert_element_type x4 -> x0, local copies, waits for them, and re-layouts: 4.19 us -> none  [the longest x1 1.8 us: local(): injected_middle[0].reshape(tokens * merge, width).astype(F32)]
    ppermute x6 -> x10, waiting for transfers between devices: 0.02 us -> 3.66 us  [over_core(): return lax.ppermute(array, 'core', [(0, 1), (1, 0)])]
    reshape x5 -> x0, local copies, waits for them, and re-layouts: 3.59 us -> none  [the longest x1 1.63 us: local(): lax.all_to_all(packed, CTX, 0, 0, tiled=True)]
  transfers between devices with their start and end apart: 19 -> 23, of which waited for: 7 -> 6; matrix products, arithmetic and copies ran while one was open for 23% -> 2% of each run, Pallas kernels for 0% -> 9%
where the time goes in v3:
time: 110 us; the launch traced here: 108 us
  starting transfers between devices  45 us (41%)
  waiting for transfers between devices  31.6 us (29%)
  local copies, waits for them, and re-layouts  18.3 us (17%)
  Pallas kernels  11.7 us (11%)
    unnamed x60, local copies, waits for them, and re-layouts  15.9 us
    ppermute x10, starting transfers between devices, over_x(): return lax.ppermute(array, 'x', [(i, (i + step) % 4) for i in range(4)])  14.6 us
    all_to_all x1, starting transfers between devices, local(): arrived = lax.all_to_all(message, CTX, 0, 0, tiled=True)  11.6 us
    all_to_all x1, waiting for transfers between devices, local(): arrived = lax.all_to_all(message, CTX, 0, 0, tiled=True)  10.8 us
    ppermute x10, waiting for transfers between devices, over_x(): return lax.ppermute(array, 'x', [(i, (i + step) % 4) for i in range(4)])  10.8 us
    all_to_all x1, starting transfers between devices, local(): terms = lax.all_to_all(gradient(own, other, columns), CTX, 0, 0, tiled=True)  9.91 us
    all_to_all x1, starting transfers between devices, local(): landed = lax.all_to_all(packed, CTX, 0, 0, tiled=True)  6.57 us
    all_to_all x1, waiting for transfers between devices, local(): terms = lax.all_to_all(gradient(own, other, columns), CTX, 0, 0, tiled=True)  6.43 us
  transfers between devices with their start and end apart: 23, of which 6 were waited for; matrix products, arithmetic and copies ran while one was open for 2% of the time, Pallas kernels for 9%

profile of v3, /device:TPU:6, one launch (start us, length us, event | category | flops | bytes accessed | tf_op | source)
XLA Modules:
  0.0 107.6 jit_solution(9652483816915636158)
XLA Ops:
  0.6 1.8 %constant_dynamic-update-slice_fusion.2 = bf16[432,1152]{1,0:T(8,128)(2,1)} fusion(bf16[144,1152]{1,0:T(8,128)(2,1)} %param.13), kind=kLoop, calls=%fused_computation.14 | loop fusion | bytes 663552
  5.1 2.4 %collective-permute-start = (bf16[432,1152]{1,0:T(8,128)(2,1)}, bf16[432,1152]{1,0:T(8,128)(2,1)S(1)}, u32[]{:S(2)}, u32[]{:S(2)}) collective-permute-start(bf16[432,1152]{1,0:T(8,128)(2,1)} %constant_dynamic-update-slice_fusion.refs_3_), channel_id=1, source_target_pairs={{0,64},{64,128},{128,192},{192,0},{1,65},{65,129},{129,193},{193,1... | collective-permute-start | bytes 2985992 | tf_op jit(solution)/shard_map/ppermute | solution.py:30
  7.5 1.2 %shard_map.119 = (bf16[32,8,640]{2,1,0:T(8,128)(2,1)}, bf16[256,256]{1,0:T(8,128)(2,1)S(1)}) custom-call(s32[1,32]{1,0:T(1,128)S(1)} %copy-done.26, bf16[128,1152]{1,0:T(8,128)(2,1)S(1)} %bitcast.26), custom_call_target="tpu_custom_call" | custom-call | tf_op jit(solution)/shard_map/pallas_call | solution.py:82
  9.3 11.6 %all-to-all-start = ((bf16[32,8,640]{2,1,0:T(8,128)(2,1)}), bf16[32,8,640]{2,1,0:T(8,128)(2,1)S(1)}, u32[]{:S(2)}, u32[]{:S(2)}) async-start(bf16[32,8,640]{2,1,0:T(8,128)(2,1)} %get-tuple-element.34), calls=%async_computation | async-start | bytes 655360 | tf_op jit(solution)/shard_map/all_to_all | solution.py:300
  21.0 1.6 %shard_map.120 = (bf16[128,3584]{1,0:T(8,128)(2,1)S(1)}, bf16[4,80,256]{2,1,0:T(8,128)(2,1)S(1)}, bf16[4,80,256]{2,1,0:T(8,128)(2,1)S(1)}) custom-call(s32[2]{0:T(128)S(1)} %pad_add_fusion.at_ref.refs_0_, bf16[20,4608]{1,0:T(8,128)(2,1)S(1)} %bitcast.27, bf16[20,4608]{1,0:T(8,128)(2,1)S(1)} %bitcast.28, bf16[20,4608]{1,0:T(8,128)(2,1)S(1)} %bitcast.29), custom_call_target="tpu_custom_call" | custom-call | tf_op jit(solution)/shard_map/pallas_call | solution.py:125
  23.6 10.8 %all-to-all-done.arrived_ref = bf16[32,8,640]{2,1,0:T(8,128)(2,1)S(1)} async-done(((bf16[32,8,640]{2,1,0:T(8,128)(2,1)}), bf16[32,8,640]{2,1,0:T(8,128)(2,1)S(1)}, u32[]{:S(2)}, u32[]{:S(2)}) %all-to-all-start) | async-done | bytes 327712 | tf_op jit(solution)/shard_map/all_to_all | solution.py:300
  34.4 1.2 %copy-done.3 = bf16[128,3584]{1,0:T(8,128)(2,1)S(1)} copy-done((bf16[128,3584]{1,0:T(8,128)(2,1)S(1)}, bf16[128,3584]{1,0:T(8,128)(2,1)}, u32[]{:S(2)}) %copy-start.3) | copy-done | bytes 917528
  36.4 0.9 copy-done.1
  37.3 6.6 %all-to-all-start.1 = ((bf16[32,8,1792]{2,1,0:T(8,128)(2,1)}), bf16[32,8,1792]{2,1,0:T(8,128)(2,1)S(1)}, u32[]{:S(2)}, u32[]{:S(2)}) async-start(bf16[32,8,1792]{2,1,0:T(8,128)(2,1)} %copy-done.1), calls=%async_computation.1 | async-start | bytes 1835008 | tf_op jit(solution)/shard_map/all_to_all | solution.py:318
  44.0 1.4 %collective-permute-done.9 = bf16[4,80,256]{2,1,0:T(8,128)(2,1)S(1)} collective-permute-done((bf16[4,80,256]{2,1,0:T(8,128)(2,1)S(1)}, bf16[4,80,256]{2,1,0:T(8,128)(2,1)S(1)}, u32[]{:S(2)}, u32[]{:S(2)}) %collective-permute-start.9) | collective-permute-done | bytes 163872 | tf_op jit(solution)/shard_map/ppermute | solution.py:34
  45.5 4.4 %collective-permute-start.3 = (bf16[80,1152]{1,0:T(8,128)(2,1)S(1)}, bf16[80,1152]{1,0:T(8,128)(2,1)S(1)}, u32[]{:S(2)}, u32[]{:S(2)}) collective-permute-start(bf16[80,1152]{1,0:T(8,128)(2,1)S(1)} %get-tuple-element.49.refs_0_), channel_id=1, source_target_pairs={{0,128},{64,192},{128,0},{192,64},{1,129},{65,193},{129,1},{193,65... | collective-permute-start | bytes 552968 | tf_op jit(solution)/shard_map/ppermute | solution.py:30
  50.5 3.5 %collective-permute-start.11 = (bf16[160,256]{1,0:T(8,128)(2,1)S(1)}, bf16[160,256]{1,0:T(8,128)(2,1)S(1)}, u32[]{:S(2)}, u32[]{:S(2)}) collective-permute-start(bf16[160,256]{1,0:T(8,128)(2,1)S(1)} %pad_maximum_fusion.2), channel_id=1, source_target_pairs={{0,128},{64,192},{128,0},{192,64},{1,129},{65,193},{129,1},{193,65... | collective-permute-start | bytes 245768 | tf_op jit(solution)/shard_map/ppermute | solution.py:30
  54.0 6.7 %collective-permute-done.10.refs_9_ = bf16[160,256]{1,0:T(8,128)(2,1)S(1)} collective-permute-done((bf16[160,256]{1,0:T(8,128)(2,1)S(1)}, bf16[160,256]{1,0:T(8,128)(2,1)S(1)}, u32[]{:S(2)}, u32[]{:S(2)}) %collective-permute-start.10) | collective-permute-done | bytes 81952 | tf_op jit(solution)/shard_map/ppermute | solution.py:30
  64.0 4.1 %collective-permute-done.12.refs_11_ = bf16[160,256]{1,0:T(8,128)(2,1)S(1)} collective-permute-done((bf16[160,256]{1,0:T(8,128)(2,1)S(1)}, bf16[160,256]{1,0:T(8,128)(2,1)S(1)}, u32[]{:S(2)}, u32[]{:S(2)}) %collective-permute-start.12) | collective-permute-done | bytes 81952 | tf_op jit(solution)/shard_map/ppermute | solution.py:30
  68.0 1.4 %collective-permute-start.13 = (bf16[224,1152]{1,0:T(8,128)(2,1)}, bf16[224,1152]{1,0:T(8,128)(2,1)}, u32[]{:S(2)}, u32[]{:S(2)}) collective-permute-start(bf16[224,1152]{1,0:T(8,128)(2,1)} %slice.38), channel_id=1, source_target_pairs={{0,64},{64,128},{128,192},{192,0},{1,65},{65,129},{129,193},{193,1... | collective-permute-start | bytes 1548296 | tf_op jit(solution)/shard_map/ppermute | solution.py:30
  73.2 0.9 copy-done.11
  74.1 0.9 copy-done.13
  75.0 0.9 copy-done.15
  75.9 0.9 copy-done.17
  79.5 0.9 shard_map.123
  81.2 9.9 %all-to-all-start.2 = ((bf16[32,48,128]{2,1,0:T(8,128)(2,1)}), bf16[32,48,128]{2,1,0:T(8,128)(2,1)S(1)}, u32[]{:S(2)}, u32[]{:S(2)}) async-start(bf16[32,48,128]{2,1,0:T(8,128)(2,1)} %copy-done), calls=%async_computation.2 | async-start | bytes 786432 | tf_op jit(solution)/shard_map/all_to_all | solution.py:323
  91.7 2.3 %collective-permute-done.19.refs_12_ = bf16[208,1152]{1,0:T(8,128)(2,1)S(1)} collective-permute-done((bf16[208,1152]{1,0:T(8,128)(2,1)}, bf16[208,1152]{1,0:T(8,128)(2,1)S(1)}, u32[]{:S(2)}, u32[]{:S(2)}) %collective-permute-start.19) | collective-permute-done | bytes 479264 | tf_op jit(solution)/shard_map/ppermute | solution.py:34
  94.0 6.3 %shard_map.122 = (bf16[128,1152]{1,0:T(8,128)(2,1)}, bf16[128,1152]{1,0:T(8,128)(2,1)}, bf16[128,1152]{1,0:T(8,128)(2,1)}, bf16[128,1152]{1,0:T(8,128)(2,1)}) custom-call(s32[2]{0:T(128)S(1)} %pad_add_fusion.at_ref.refs_0_, bf16[256,256]{1,0:T(8,128)(2,1)S(1)} %copy-done.19, bf16[32,8,1792]{2,1,0:T(8,128)(2,1)S(1)} %all-to-all-done.1.refs_2_, ...), custom_call_target="tpu_custom_call" | custom-call | flops 1019215872 | bytes 7962624 | tf_op jit(solution)/shard_map/pallas_call | solution.py:271
  100.3 6.4 %all-to-all-done.2.terms_ref = bf16[32,48,128]{2,1,0:T(8,128)(2,1)S(1)} async-done(((bf16[32,48,128]{2,1,0:T(8,128)(2,1)}), bf16[32,48,128]{2,1,0:T(8,128)(2,1)S(1)}, u32[]{:S(2)}, u32[]{:S(2)}) %all-to-all-start.2) | async-done | bytes 393248 | tf_op jit(solution)/shard_map/all_to_all | solution.py:323
  (98 shorter events, 17.7 us)
Async XLA Ops:
  4.3 30.1 %collective-permute-start.1 = (bf16[432,1152]{1,0:T(8,128)(2,1)}, bf16[432,1152]{1,0:T(8,128)(2,1)S(1)}, u32[]{:S(2)}, u32[]{:S(2)}) collective-permute-start(bf16[432,1152]{1,0:T(8,128)(2,1)} %constant_dynamic-update-slice_fusion.refs_3_), channel_id=1, source_target_pairs={{0,192},{64,0},{128,64},{192,128},{1,193},{65,1},{129,65},{193,129... | collective-permute-start | bytes 2985992 | tf_op jit(solution)/shard_map/ppermute | solution.py:30
  5.1 29.3 %collective-permute-start = (bf16[432,1152]{1,0:T(8,128)(2,1)}, bf16[432,1152]{1,0:T(8,128)(2,1)S(1)}, u32[]{:S(2)}, u32[]{:S(2)}) collective-permute-start(bf16[432,1152]{1,0:T(8,128)(2,1)} %constant_dynamic-update-slice_fusion.refs_3_), channel_id=1, source_target_pairs={{0,64},{64,128},{128,192},{192,0},{1,65},{65,129},{129,193},{193,1... | collective-permute-start | bytes 2985992 | tf_op jit(solution)/shard_map/ppermute | solution.py:30
  9.3 25.0 %all-to-all-start = ((bf16[32,8,640]{2,1,0:T(8,128)(2,1)}), bf16[32,8,640]{2,1,0:T(8,128)(2,1)S(1)}, u32[]{:S(2)}, u32[]{:S(2)}) async-start(bf16[32,8,640]{2,1,0:T(8,128)(2,1)} %get-tuple-element.34), calls=%async_computation | async-start | bytes 655360 | tf_op jit(solution)/shard_map/all_to_all | solution.py:300
  37.3 34.9 %all-to-all-start.1 = ((bf16[32,8,1792]{2,1,0:T(8,128)(2,1)}), bf16[32,8,1792]{2,1,0:T(8,128)(2,1)S(1)}, u32[]{:S(2)}, u32[]{:S(2)}) async-start(bf16[32,8,1792]{2,1,0:T(8,128)(2,1)} %copy-done.1), calls=%async_computation.1 | async-start | bytes 1835008 | tf_op jit(solution)/shard_map/all_to_all | solution.py:318
  43.9 1.5 %collective-permute-start.9 = (bf16[4,80,256]{2,1,0:T(8,128)(2,1)S(1)}, bf16[4,80,256]{2,1,0:T(8,128)(2,1)S(1)}, u32[]{:S(2)}, u32[]{:S(2)}) collective-permute-start(bf16[4,80,256]{2,1,0:T(8,128)(2,1)S(1)} %get-tuple-element.40), channel_id=1, source_target_pairs={{0,32},{32,0},{1,33},{33,1},{2,34},{34,2},{3,35},{35,3},{4,36},{36... | collective-permute-start | bytes 491528 | tf_op jit(solution)/shard_map/ppermute | solution.py:34
  45.4 15.3 %collective-permute-start.4 = (bf16[80,1152]{1,0:T(8,128)(2,1)S(1)}, bf16[80,1152]{1,0:T(8,128)(2,1)S(1)}, u32[]{:S(2)}, u32[]{:S(2)}) collective-permute-start(bf16[80,1152]{1,0:T(8,128)(2,1)S(1)} %get-tuple-element.49.refs_0_), channel_id=1, source_target_pairs={{0,192},{64,0},{128,64},{192,128},{1,193},{65,1},{129,65},{193,129... | collective-permute-start | bytes 552968 | tf_op jit(solution)/shard_map/ppermute | solution.py:30
  45.5 15.7 %collective-permute-start.3 = (bf16[80,1152]{1,0:T(8,128)(2,1)S(1)}, bf16[80,1152]{1,0:T(8,128)(2,1)S(1)}, u32[]{:S(2)}, u32[]{:S(2)}) collective-permute-start(bf16[80,1152]{1,0:T(8,128)(2,1)S(1)} %get-tuple-element.49.refs_0_), channel_id=1, source_target_pairs={{0,128},{64,192},{128,0},{192,64},{1,129},{65,193},{129,1},{193,65... | collective-permute-start | bytes 552968 | tf_op jit(solution)/shard_map/ppermute | solution.py:30
  49.9 11.4 %collective-permute-start.2 = (bf16[80,1152]{1,0:T(8,128)(2,1)S(1)}, bf16[80,1152]{1,0:T(8,128)(2,1)S(1)}, u32[]{:S(2)}, u32[]{:S(2)}) collective-permute-start(bf16[80,1152]{1,0:T(8,128)(2,1)S(1)} %get-tuple-element.49.refs_0_), channel_id=1, source_target_pairs={{0,64},{64,128},{128,192},{192,0},{1,65},{65,129},{129,193},{193,1... | collective-permute-start | bytes 552968 | tf_op jit(solution)/shard_map/ppermute | solution.py:30
  49.9 10.8 %collective-permute-start.10 = (bf16[160,256]{1,0:T(8,128)(2,1)S(1)}, bf16[160,256]{1,0:T(8,128)(2,1)S(1)}, u32[]{:S(2)}, u32[]{:S(2)}) collective-permute-start(bf16[160,256]{1,0:T(8,128)(2,1)S(1)} %pad_maximum_fusion.1), channel_id=1, source_target_pairs={{0,64},{64,128},{128,192},{192,0},{1,65},{65,129},{129,193},{193,1... | collective-permute-start | bytes 245768 | tf_op jit(solution)/shard_map/ppermute | solution.py:30
  50.5 11.3 %collective-permute-start.11 = (bf16[160,256]{1,0:T(8,128)(2,1)S(1)}, bf16[160,256]{1,0:T(8,128)(2,1)S(1)}, u32[]{:S(2)}, u32[]{:S(2)}) collective-permute-start(bf16[160,256]{1,0:T(8,128)(2,1)S(1)} %pad_maximum_fusion.2), channel_id=1, source_target_pairs={{0,128},{64,192},{128,0},{192,64},{1,129},{65,193},{129,1},{193,65... | collective-permute-start | bytes 245768 | tf_op jit(solution)/shard_map/ppermute | solution.py:30
  60.7 8.8 %collective-permute-start.5 = (bf16[80,1152]{1,0:T(8,128)(2,1)S(1)}, bf16[80,1152]{1,0:T(8,128)(2,1)S(1)}, u32[]{:S(2)}, u32[]{:S(2)}) collective-permute-start(bf16[80,1152]{1,0:T(8,128)(2,1)S(1)} %get-tuple-element.49.refs_0_), channel_id=1, source_target_pairs={{0,32},{32,0},{1,33},{33,1},{2,34},{34,2},{3,35},{35,3},{4,36},{36... | collective-permute-start | bytes 552968 | tf_op jit(solution)/shard_map/ppermute | solution.py:34
  60.7 8.8 %collective-permute-start.8 = (bf16[80,1152]{1,0:T(8,128)(2,1)S(1)}, bf16[80,1152]{1,0:T(8,128)(2,1)S(1)}, u32[]{:S(2)}, u32[]{:S(2)}) collective-permute-start(bf16[80,1152]{1,0:T(8,128)(2,1)S(1)} %collective-permute-done.4.refs_3_), channel_id=1, source_target_pairs={{0,32},{32,0},{1,33},{33,1},{2,34},{34,2},{3,35},{35,3},{4,36},{36... | collective-permute-start | bytes 552968 | tf_op jit(solution)/shard_map/ppermute | solution.py:34
  61.2 8.8 %collective-permute-start.7 = (bf16[80,1152]{1,0:T(8,128)(2,1)S(1)}, bf16[80,1152]{1,0:T(8,128)(2,1)S(1)}, u32[]{:S(2)}, u32[]{:S(2)}) collective-permute-start(bf16[80,1152]{1,0:T(8,128)(2,1)S(1)} %collective-permute-done.3.refs_2_), channel_id=1, source_target_pairs={{0,32},{32,0},{1,33},{33,1},{2,34},{34,2},{3,35},{35,3},{4,36},{36... | collective-permute-start | bytes 552968 | tf_op jit(solution)/shard_map/ppermute | solution.py:34
  61.3 9.6 %collective-permute-start.6 = (bf16[80,1152]{1,0:T(8,128)(2,1)S(1)}, bf16[80,1152]{1,0:T(8,128)(2,1)S(1)}, u32[]{:S(2)}, u32[]{:S(2)}) collective-permute-start(bf16[80,1152]{1,0:T(8,128)(2,1)S(1)} %collective-permute-done.2.refs_1_), channel_id=1, source_target_pairs={{0,32},{32,0},{1,33},{33,1},{2,34},{34,2},{3,35},{35,3},{4,36},{36... | collective-permute-start | bytes 552968 | tf_op jit(solution)/shard_map/ppermute | solution.py:34
  62.4 5.7 %collective-permute-start.12 = (bf16[160,256]{1,0:T(8,128)(2,1)S(1)}, bf16[160,256]{1,0:T(8,128)(2,1)S(1)}, u32[]{:S(2)}, u32[]{:S(2)}) collective-permute-start(bf16[160,256]{1,0:T(8,128)(2,1)S(1)} %pad_maximum_fusion.3), channel_id=1, source_target_pairs={{0,192},{64,0},{128,64},{192,128},{1,193},{65,1},{129,65},{193,129... | collective-permute-start | bytes 245768 | tf_op jit(solution)/shard_map/ppermute | solution.py:30
  68.0 23.1 %collective-permute-start.13 = (bf16[224,1152]{1,0:T(8,128)(2,1)}, bf16[224,1152]{1,0:T(8,128)(2,1)}, u32[]{:S(2)}, u32[]{:S(2)}) collective-permute-start(bf16[224,1152]{1,0:T(8,128)(2,1)} %slice.38), channel_id=1, source_target_pairs={{0,64},{64,128},{128,192},{192,0},{1,65},{65,129},{129,193},{193,1... | collective-permute-start | bytes 1548296 | tf_op jit(solution)/shard_map/ppermute | solution.py:30
  69.5 22.3 %collective-permute-start.15 = (bf16[432,1152]{1,0:T(8,128)(2,1)}, bf16[432,1152]{1,0:T(8,128)(2,1)}, u32[]{:S(2)}, u32[]{:S(2)}) collective-permute-start(bf16[432,1152]{1,0:T(8,128)(2,1)} %constant_dynamic-update-slice_fusion.refs_3_), channel_id=1, source_target_pairs={{0,32},{32,0},{1,33},{33,1},{2,34},{34,2},{3,35},{35,3},{4,36},{36... | collective-permute-start | bytes 2985992 | tf_op jit(solution)/shard_map/ppermute | solution.py:34
  69.5 24.5 %collective-permute-start.16 = (bf16[432,1152]{1,0:T(8,128)(2,1)S(1)}, bf16[432,1152]{1,0:T(8,128)(2,1)}, u32[]{:S(2)}, u32[]{:S(2)}) collective-permute-start(bf16[432,1152]{1,0:T(8,128)(2,1)S(1)} %collective-permute-done.refs_4_), channel_id=1, source_target_pairs={{0,32},{32,0},{1,33},{33,1},{2,34},{34,2},{3,35},{35,3},{4,36},{36... | collective-permute-start | bytes 2985992 | tf_op jit(solution)/shard_map/ppermute | solution.py:34
  70.0 24.0 %collective-permute-start.17 = (bf16[432,1152]{1,0:T(8,128)(2,1)S(1)}, bf16[432,1152]{1,0:T(8,128)(2,1)}, u32[]{:S(2)}, u32[]{:S(2)}) collective-permute-start(bf16[432,1152]{1,0:T(8,128)(2,1)S(1)} %collective-permute-done.1.refs_5_), channel_id=1, source_target_pairs={{0,32},{32,0},{1,33},{33,1},{2,34},{34,2},{3,35},{35,3},{4,36},{36... | collective-permute-start | bytes 2985992 | tf_op jit(solution)/shard_map/ppermute | solution.py:34
  71.6 19.6 %collective-permute-start.14 = (bf16[208,1152]{1,0:T(8,128)(2,1)}, bf16[208,1152]{1,0:T(8,128)(2,1)}, u32[]{:S(2)}, u32[]{:S(2)}) collective-permute-start(bf16[208,1152]{1,0:T(8,128)(2,1)} %slice.39), channel_id=1, source_target_pairs={{0,192},{64,0},{128,64},{192,128},{1,193},{65,1},{129,65},{193,129... | collective-permute-start | bytes 1437704 | tf_op jit(solution)/shard_map/ppermute | solution.py:30
  81.2 12.8 %copy-start.19 = (bf16[256,256]{1,0:T(8,128)(2,1)S(1)}, bf16[256,256]{1,0:T(8,128)(2,1)}, u32[]{:S(2)}) copy-start(bf16[256,256]{1,0:T(8,128)(2,1)} %copy-done.18) | copy-start | bytes 393220
  81.2 25.5 %all-to-all-start.2 = ((bf16[32,48,128]{2,1,0:T(8,128)(2,1)}), bf16[32,48,128]{2,1,0:T(8,128)(2,1)S(1)}, u32[]{:S(2)}, u32[]{:S(2)}) async-start(bf16[32,48,128]{2,1,0:T(8,128)(2,1)} %copy-done), calls=%async_computation.2 | async-start | bytes 786432 | tf_op jit(solution)/shard_map/all_to_all | solution.py:323
  91.1 2.9 %collective-permute-start.18 = (bf16[224,1152]{1,0:T(8,128)(2,1)}, bf16[224,1152]{1,0:T(8,128)(2,1)S(1)}, u32[]{:S(2)}, u32[]{:S(2)}) collective-permute-start(bf16[224,1152]{1,0:T(8,128)(2,1)} %collective-permute-done.13.refs_6_), channel_id=1, source_target_pairs={{0,32},{32,0},{1,33},{33,1},{2,34},{34,2},{3,35},{35,3},{4,36},{36... | collective-permute-start | bytes 1548296 | tf_op jit(solution)/shard_map/ppermute | solution.py:34
  91.2 2.8 %collective-permute-start.19 = (bf16[208,1152]{1,0:T(8,128)(2,1)}, bf16[208,1152]{1,0:T(8,128)(2,1)S(1)}, u32[]{:S(2)}, u32[]{:S(2)}) collective-permute-start(bf16[208,1152]{1,0:T(8,128)(2,1)} %collective-permute-done.14.refs_7_), channel_id=1, source_target_pairs={{0,32},{32,0},{1,33},{33,1},{2,34},{34,2},{3,35},{35,3},{4,36},{36... | collective-permute-start | bytes 1437704 | tf_op jit(solution)/shard_map/ppermute | solution.py:34
  (28 other events, 68.7 us)

commit v4 on v3

--- a/solution.py
+++ b/solution.py
@@ -30,6 +30,10 @@
     return lax.ppermute(array, "x", [(i, (i + step) % 4) for i in range(4)])
 
 
+def over_y(array, step):
+    return lax.ppermute(array, "y", [(i, (i + step) % 4) for i in range(4)])
+
+
 def over_core(array):
     return lax.ppermute(array, "core", [(0, 1), (1, 0)])
 
@@ -54,7 +58,17 @@
     return jnp.floor((value + 0.5) * (1.0 / by))
 
 
-def message_kernel(slot_ref, saved_ref, message_ref, table_ref):
+def message_kernel(
+    slot_ref, saved_hbm, early, middle, late, message_ref, table_ref, stacked, saved_ref, sem
+):
+    fetch = pltpu.make_async_copy(saved_hbm, saved_ref, sem.at[3])
+    fetch.start()
+    stack = [
+        pltpu.make_async_copy(ref, stacked.at[pl.ds(m * SHARD, SHARD)], sem.at[m])
+        for m, ref in enumerate((early, middle, late))
+    ]
+    for copy in stack:
+        copy.start()
     source = slot_ref[...].astype(F32)
     sender = quotient(source, TOKENS)
     place = source - TOKENS * sender
@@ -72,23 +86,31 @@
     table_ref[:, : MERGE * SLOTS] = first
     table_ref[:, MERGE * SLOTS :] = second
     rest = WIDTH - SAVED_HALF
+    fetch.wait()
     left = matmul(first, saved_ref[:, :SAVED_HALF])
     right = matmul(second, saved_ref[:, SAVED_HALF:])
     message = jnp.concatenate([left[:, :rest] + right, left[:, rest:] + tag], axis=1)
     message_ref[...] = message.reshape(SLOTS, 8, SAVED_HALF).astype(BF16)
-
-
-def make_message(slot, saved):
+    for copy in stack:
+        copy.wait()
+
+
+def make_message(slot, saved, projections):
     return pl.pallas_call(
         message_kernel,
         out_shape=(
             jax.ShapeDtypeStruct((SLOTS, 8, SAVED_HALF), BF16),
             jax.ShapeDtypeStruct((8 * SLOTS, 2 * MERGE * SLOTS), BF16),
+            jax.ShapeDtypeStruct((3 * SHARD, WIDTH), BF16),
         ),
-        in_specs=[VMEM] * 2,
-        out_specs=(VMEM,) * 2,
-        compiler_params=PARAMS,
-    )(slot, saved)
+        in_specs=[VMEM] + [ANY] * 4,
+        out_specs=(VMEM, VMEM, ANY),
+        scratch_shapes=[
+            pltpu.VMEM((MERGE * SLOTS, WIDTH), BF16),
+            pltpu.SemaphoreType.DMA((4,)),
+        ],
+        compiler_params=PARAMS,
+    )(slot, saved, *projections)
 
 
 def rows_kernel(at_ref, early_ref, middle_ref, late_ref, rows_ref, keep_ref, give_ref, sums):
@@ -132,7 +154,7 @@
     )(at, early, middle, late)
 
 
-def pack_kernel(arrived_ref, rows_ref, saved_ref, packed_ref):
+def unpack_kernel(arrived_ref, saved_ref, table_ref):
     count = 8 * SLOTS
     arrived = arrived_ref[...].astype(F32).reshape(count, SAVED_HALF).astype(BF16)
     rest = WIDTH - SAVED_HALF
@@ -145,61 +167,118 @@
     match = (asked == token) & (row % MERGE == j)
     first = onehot(match & (row % 8 < MERGE))
     second = onehot(match & (row % 8 >= MERGE))
-    packed = matmul(first, rows_ref[:, :ROWS_HALF]) + matmul(second, rows_ref[:, ROWS_HALF:])
-    packed_ref[...] = packed.reshape(SLOTS, 8, ROWS_HALF).astype(BF16)
+    table_ref[:, :128] = first
+    table_ref[:, 128:] = second
     used = MERGE * TOKENS
     saved_ref[:, :SAVED_HALF] = matmul_tn(first, arrived)[:used].astype(BF16)
     saved_ref[:, SAVED_HALF:] = matmul_tn(second, arrived[:, :rest])[:used].astype(BF16)
 
 
-def pack(arrived, rows):
-    return pl.pallas_call(
-        pack_kernel,
+def unpack(arrived):
+    return pl.pallas_call(
+        unpack_kernel,
         out_shape=(
             jax.ShapeDtypeStruct((MERGE * TOKENS, WIDTH), BF16),
-            jax.ShapeDtypeStruct((SLOTS, 8, ROWS_HALF), BF16),
+            jax.ShapeDtypeStruct((8 * SLOTS, 256), BF16),
         ),
+        in_specs=[VMEM],
+        out_specs=(VMEM,) * 2,
+        compiler_params=PARAMS,
+    )(arrived)
+
+
+def pack_kernel(table_ref, rows_ref, packed_ref):
+    packed = matmul(table_ref[:, :128], rows_ref[:, :ROWS_HALF])
+    packed = packed + matmul(table_ref[:, 128:], rows_ref[:, ROWS_HALF:])
+    packed_ref[...] = packed.reshape(SLOTS, 8, ROWS_HALF).astype(BF16)
+
+
+def pack(table, rows):
+    return pl.pallas_call(
+        pack_kernel,
+        out_shape=jax.ShapeDtypeStruct((SLOTS, 8, ROWS_HALF), BF16),
         in_specs=[VMEM] * 2,
-        out_specs=(VMEM,) * 2,
-        compiler_params=PARAMS,
-    )(arrived, rows)
-
-
-def gradient_kernel(*refs):
-    own, other, columns = refs[:4], refs[4:8], refs[8:12]
-    terms_ref, product = refs[12:]
-    saved = jnp.concatenate([ref[...] for k in range(4) for ref in (own[k], other[k])], axis=0)
-    product[...] = matmul_tn(saved, jnp.concatenate([ref[...] for ref in columns], axis=0))
+        out_specs=VMEM,
+        compiler_params=PARAMS,
+    )(table, rows)
+
+
+def gradient_kernel(y_ref, *refs):
+    pieces, (own_ref, *out_refs), (saved, columns, product, folded, terms, sem) = (
+        refs[:12],
+        refs[12:16],
+        refs[16:],
+    )
+    rows = MERGE * TOKENS
+    copies = []
+    for k, ref in enumerate(pieces):
+        if k < 8:
+            to = saved.at[pl.ds(k * rows, rows)]
+        else:
+            to = columns.at[pl.ds((k - 8) * 2 * rows, 2 * rows)]
+        copies.append(pltpu.make_async_copy(ref, to, sem.at[k]))
+    for copy in copies:
+        copy.start()
     line = iota((WIDTH, 128), 0).astype(F32)
     inside = line - OWN * quotient(line, OWN)
     group = (iota((WIDTH, 128), 1) // 16).astype(F32)
-    rest = jnp.where(inside - 8 * quotient(inside, 8) == group, product[:, 128:], 0.0)
+    mine = inside - 8 * quotient(inside, 8) == group
     line = iota((1, WIDTH), 1).astype(F32)
     block = quotient(line, OWN)
     to = REST * block + quotient(line - OWN * block, 8)
     fold = onehot(iota((REST * SLOTS, WIDTH), 0).astype(F32) == to)
-    folded = matmul(fold, rest.astype(BF16))
+    for copy in copies:
+        copy.wait()
+    product[...] = matmul_tn(saved[...], columns[...])
+    folded[...] = matmul(fold, jnp.where(mine, product[:, 128:], 0.0).astype(BF16))
     fill = jnp.zeros((TERM_ROWS - OWN - REST, 128), F32)
     for c in range(SLOTS):
-        main = product[c * OWN : (c + 1) * OWN, :128]
-        message = jnp.concatenate([main, folded[c * REST : (c + 1) * REST], fill], axis=0)
-        terms_ref[c] = message.astype(BF16)
-
-
-def gradient(own, other, columns):
+        step = lax.rem(c % 4 + 4 - y_ref[0], 4)
+        parts = [product[c * OWN : (c + 1) * OWN, :128], folded[c * REST : (c + 1) * REST], fill]
+        terms[step, c // 4] = jnp.concatenate(parts, axis=0)
+    for step, out in enumerate((own_ref, *out_refs)):
+        out[...] = terms[step].astype(out.dtype)
+
+
+def gradient(y, own, other, columns):
+    shape = (8, TERM_ROWS, 128)
     return pl.pallas_call(
         gradient_kernel,
-        out_shape=jax.ShapeDtypeStruct((SLOTS, TERM_ROWS, 128), BF16),
-        in_specs=[VMEM] * 12,
+        out_shape=[jax.ShapeDtypeStruct(shape, F32)] + [jax.ShapeDtypeStruct(shape, BF16)] * 3,
+        in_specs=[SMEM] + [ANY] * 12,
+        out_specs=[VMEM] * 4,
+        scratch_shapes=[
+            pltpu.VMEM((8 * MERGE * TOKENS, WIDTH), BF16),
+            pltpu.VMEM((8 * MERGE * TOKENS, 256), BF16),
+            pltpu.VMEM((WIDTH, 256), F32),
+            pltpu.VMEM((REST * SLOTS, 128), F32),
+            pltpu.VMEM((4, 8, TERM_ROWS, 128), F32),
+            pltpu.SemaphoreType.DMA((12,)),
+        ],
+        compiler_params=PARAMS,
+    )(y, *(piece for pair in zip(own, other) for piece in pair), *columns)
+
+
+def sum_kernel(own_ref, first, second, third, out_ref):
+    total = own_ref[...]
+    for ref in (first, second, third):
+        total = total + ref[...].astype(F32)
+    out_ref[...] = total.astype(BF16)
+
+
+def sum_y(own, parts):
+    return pl.pallas_call(
+        sum_kernel,
+        out_shape=jax.ShapeDtypeStruct(own.shape, BF16),
+        in_specs=[VMEM] * 4,
         out_specs=VMEM,
-        scratch_shapes=[pltpu.VMEM((WIDTH, 256), F32)],
-        compiler_params=PARAMS,
-    )(*own, *other, *columns)
+        compiler_params=PARAMS,
+    )(own, *parts)
 
 
 def total_kernel(terms_ref, out_ref):
     total = terms_ref[0].astype(F32)
-    for c in range(1, SLOTS):
+    for c in range(1, 8):
         total = total + terms_ref[c].astype(F32)
     rest = jnp.concatenate(
         [jnp.broadcast_to(total[OWN + a : OWN + a + 1], (8, 128)) for a in range(REST)], axis=0
@@ -295,33 +374,38 @@
     projection_late,
 ):
     at = jnp.stack([lax.axis_index("x"), lax.axis_index("core")]).astype(jnp.int32)
-
-    message, table = make_message(slot_source, saved_early[0])
+    y = lax.axis_index("y").astype(jnp.int32).reshape(1)
+
+    projections = (projection_early, projection_middle, projection_late)
+    message, table, stacked = make_message(slot_source, saved_early[0], projections)
     arrived = lax.all_to_all(message, CTX, 0, 0, tiled=True)
 
-    stacked = jnp.concatenate([projection_early, projection_middle, projection_late])
     cut = 224
     from_left, from_right = over_x(stacked, 1), over_x(stacked, 3)
+
     rows, keep, give = make_rows(at, injected_early[0], injected_middle[0], injected_late[0])
-    arrived, rows, from_left, from_right = lax.optimization_barrier(
-        (arrived, rows, from_left, from_right)
+    given = over_core(give)
+    mixed = [jnp.concatenate([keep[step], given[step]]) for step in range(4)]
+    columns = [mixed[0]] + [over_x(mixed[step], step) for step in (1, 2, 3)]
+    arrived, from_left, from_right, columns = lax.optimization_barrier(
+        (arrived, from_left, from_right, columns)
     )
+
+    saved_rows, by_token = unpack(arrived)
+    own = [saved_rows] + [over_x(saved_rows, step) for step in (1, 2, 3)]
+    landed = lax.all_to_all(pack(by_token, rows), CTX, 0, 0, tiled=True)
+
+    own, from_left, from_right = lax.optimization_barrier((own, from_left, from_right))
     far_left, far_right = over_x(from_left[:cut], 1), over_x(from_right[cut:], 3)
     pieces = (stacked, from_left, from_right, far_left, far_right)
     pieces = pieces + tuple(over_core(piece) for piece in pieces)
 
-    given = over_core(give)
-    mixed = [jnp.concatenate([keep[step], given[step]]) for step in range(4)]
-    columns = [mixed[0]] + [over_x(mixed[step], step) for step in (1, 2, 3)]
-
-    saved_rows, packed = pack(arrived, rows)
-    landed = lax.all_to_all(packed, CTX, 0, 0, tiled=True)
-
-    own = [saved_rows] + [over_x(saved_rows, step) for step in (1, 2, 3)]
     other = [over_core(piece) for piece in own]
-    own, other, columns, landed = lax.optimization_barrier((own, other, columns, landed))
-    terms = lax.all_to_all(gradient(own, other, columns), CTX, 0, 0, tiled=True)
-    weights = add_up(terms)
+    mine, *parts = gradient(y, own, other, columns)
+    parts = [over_y(part, step) for step, part in zip((1, 2, 3), parts)]
+    terms = sum_y(mine, parts)
+    terms, landed = lax.optimization_barrier((terms, landed))
+    weights = add_up(lax.all_to_all(terms, "z", 0, 0, tiled=True))
 
     context_early, context_middle, context_late, stream = contexts(at, table, landed, pieces, cut)
     return context_early[None], context_middle[None], context_late[None], stream[None], weights

time: 110 us -> 113 us (1.027)
  local copies, waits for them, and re-layouts: 18.3 us -> 11 us
  waiting for transfers between devices: 31.6 us -> 37.4 us
  Pallas kernels: 11.7 us -> 15.8 us
  starting transfers between devices: 45 us -> 46.5 us
    ppermute x10, waiting for transfers between devices: 10.8 us -> 30 us  [over_x(): return lax.ppermute(array, 'x', [(i, (i + step) % 4) for i in range(4)])]
    all_to_all x1, waiting for transfers between devices: 10.8 us -> 3.55 us  [local(): arrived = lax.all_to_all(message, CTX, 0, 0, tiled=True)]
    ppermute x0 -> x3, starting transfers between devices: none -> 5.73 us  [over_y(): return lax.ppermute(array, 'y', [(i, (i + step) % 4) for i in range(4)])]
    unnamed x60 -> x36, local copies, waits for them, and re-layouts: 15.9 us -> 10.9 us
    all_to_all x2, waiting for transfers between devices: 6.43 us -> 2.09 us  [the longest x1 2.08 us: local(): weights = add_up(lax.all_to_all(terms, 'z', 0, 0, tiled=True))]
    pallas_call x2 -> x4, Pallas kernels: 1.78 us -> 5.57 us  [the longest x1 2.79 us: gradient(): pl.pallas_call(gradient_kernel, out_shape=[jax.ShapeDtypeStruct(shape, F3...]
    ppermute x10, waiting for transfers between devices: 3.66 us -> 1.34 us  [over_core(): return lax.ppermute(array, 'core', [(0, 1), (1, 0)])]
    all_to_all x2, starting transfers between devices: 16.5 us -> 14.7 us  [the longest x1 8.05 us: local(): landed = lax.all_to_all(pack(by_token, rows), CTX, 0, 0, tiled=True)]
  transfers between devices with their start and end apart: 23 -> 26, of which waited for: 6 -> 13; matrix products, arithmetic and copies ran while one was open for 2% -> 0% of each run, Pallas kernels for 9% -> 10%
where the time goes in v4:
time: 113 us; the launch traced here: 112 us
  starting transfers between devices  46.5 us (41%)
  waiting for transfers between devices  37.4 us (33%)
  Pallas kernels  15.8 us (14%)
  local copies, waits for them, and re-layouts  11 us (10%)
    ppermute x10, waiting for transfers between devices, over_x(): return lax.ppermute(array, 'x', [(i, (i + step) % 4) for i in range(4)])  30 us
    ppermute x10, starting transfers between devices, over_x(): return lax.ppermute(array, 'x', [(i, (i + step) % 4) for i in range(4)])  13 us
    all_to_all x1, starting transfers between devices, local(): arrived = lax.all_to_all(message, CTX, 0, 0, tiled=True)  11.5 us
    unnamed x36, local copies, waits for them, and re-layouts  10.9 us
    all_to_all x1, starting transfers between devices, local(): landed = lax.all_to_all(pack(by_token, rows), CTX, 0, 0, tiled=True)  8.05 us
    all_to_all x1, starting transfers between devices, local(): weights = add_up(lax.all_to_all(terms, 'z', 0, 0, tiled=True))  6.66 us
    pallas_call x1, Pallas kernels, contexts(): pl.pallas_call(lambda *refs: context_kernel(cut, *refs), out_shape=(out,)...  5.99 us
    ppermute x3, starting transfers between devices, over_y(): return lax.ppermute(array, 'y', [(i, (i + step) % 4) for i in range(4)])  5.73 us
  transfers between devices with their start and end apart: 26, of which 13 were waited for; matrix products, arithmetic and copies ran while one was open for 0% of the time, Pallas kernels for 10%

profile of v4, /device:TPU:6, one launch (start us, length us, event | category | flops | bytes accessed | tf_op | source)
XLA Modules:
  0.0 111.6 jit_solution(10944600990096265100)
XLA Ops:
  5.2 1.8 %shard_map.119 = (bf16[32,8,640]{2,1,0:T(8,128)(2,1)}, bf16[256,256]{1,0:T(8,128)(2,1)S(1)}, bf16[432,1152]{1,0:T(8,128)(2,1)}) custom-call(s32[1,32]{1,0:T(1,128)S(1)} %copy-done.17, bf16[128,1152]{1,0:T(8,128)(2,1)S(1)} %bitcast.27, bf16[144,1152]{1,0:T(8,128)(2,1)S(1)} %copy-done.2, bf16[144,1152]{1,0:T(8,128)(2,1)S(1)} %copy-done.3, ...), custom_call_target="tpu_custom_call" | custom-call | tf_op jit(solution)/shard_map/pallas_call | solution.py:99
  8.5 2.4 %collective-permute-start = (bf16[432,1152]{1,0:T(8,128)(2,1)}, bf16[432,1152]{1,0:T(8,128)(2,1)S(1)}, u32[]{:S(2)}, u32[]{:S(2)}) collective-permute-start(bf16[432,1152]{1,0:T(8,128)(2,1)} %get-tuple-element.38.refs_3_), channel_id=1, source_target_pairs={{0,64},{64,128},{128,192},{192,0},{1,65},{65,129},{129,193},{193,1... | collective-permute-start | bytes 2985992 | tf_op jit(solution)/shard_map/ppermute | solution.py:30
  11.0 1.6 %shard_map.120 = (bf16[128,3584]{1,0:T(8,128)(2,1)S(1)}, bf16[4,80,256]{2,1,0:T(8,128)(2,1)S(1)}, bf16[4,80,256]{2,1,0:T(8,128)(2,1)S(1)}) custom-call(s32[2]{0:T(128)S(1)} %pad_add_fusion.at_ref.refs_0_, bf16[20,4608]{1,0:T(8,128)(2,1)S(1)} %bitcast.28, bf16[20,4608]{1,0:T(8,128)(2,1)S(1)} %bitcast.29, bf16[20,4608]{1,0:T(8,128)(2,1)S(1)} %bitcast.30), custom_call_target="tpu_custom_call" | custom-call | tf_op jit(solution)/shard_map/pallas_call | solution.py:147
  13.5 11.5 %all-to-all-start = ((bf16[32,8,640]{2,1,0:T(8,128)(2,1)}), bf16[32,8,640]{2,1,0:T(8,128)(2,1)S(1)}, u32[]{:S(2)}, u32[]{:S(2)}) async-start(bf16[32,8,640]{2,1,0:T(8,128)(2,1)} %get-tuple-element.37), calls=%async_computation | async-start | bytes 655360 | tf_op jit(solution)/shard_map/all_to_all | solution.py:381
  25.2 1.7 %collective-permute-start.4 = (bf16[160,256]{1,0:T(8,128)(2,1)S(1)}, bf16[160,256]{1,0:T(8,128)(2,1)S(1)}, u32[]{:S(2)}, u32[]{:S(2)}) collective-permute-start(bf16[160,256]{1,0:T(8,128)(2,1)S(1)} %pad_maximum_fusion.2), channel_id=1, source_target_pairs={{0,128},{64,192},{128,0},{192,64},{1,129},{65,193},{129,1},{193,65... | collective-permute-start | bytes 245768 | tf_op jit(solution)/shard_map/ppermute | solution.py:30
  27.3 8.3 %collective-permute-done.3.refs_9_ = bf16[160,256]{1,0:T(8,128)(2,1)S(1)} collective-permute-done((bf16[160,256]{1,0:T(8,128)(2,1)S(1)}, bf16[160,256]{1,0:T(8,128)(2,1)S(1)}, u32[]{:S(2)}, u32[]{:S(2)}) %collective-permute-start.3) | collective-permute-done | bytes 81952 | tf_op jit(solution)/shard_map/ppermute | solution.py:30
  36.3 3.5 %all-to-all-done.arrived_ref = bf16[32,8,640]{2,1,0:T(8,128)(2,1)S(1)} async-done(((bf16[32,8,640]{2,1,0:T(8,128)(2,1)}), bf16[32,8,640]{2,1,0:T(8,128)(2,1)S(1)}, u32[]{:S(2)}, u32[]{:S(2)}) %all-to-all-start) | async-done | bytes 327712 | tf_op jit(solution)/shard_map/all_to_all | solution.py:381
  40.4 1.2 %copy-done.1 = bf16[128,3584]{1,0:T(8,128)(2,1)S(1)} copy-done((bf16[128,3584]{1,0:T(8,128)(2,1)S(1)}, bf16[128,3584]{1,0:T(8,128)(2,1)}, u32[]{:S(2)}) %copy-start.1) | copy-done | bytes 917528
  41.6 1.6 %shard_map.124 = bf16[32,8,1792]{2,1,0:T(8,128)(2,1)} custom-call(bf16[256,256]{1,0:T(8,128)(2,1)S(1)} %get-tuple-element.57.table_ref, bf16[128,3584]{1,0:T(8,128)(2,1)S(1)} %copy-done.1), custom_call_target="tpu_custom_call" | custom-call | tf_op jit(solution)/shard_map/pallas_call | solution.py:197
  43.2 8.1 %all-to-all-start.1 = ((bf16[32,8,1792]{2,1,0:T(8,128)(2,1)}), bf16[32,8,1792]{2,1,0:T(8,128)(2,1)S(1)}, u32[]{:S(2)}, u32[]{:S(2)}) async-start(bf16[32,8,1792]{2,1,0:T(8,128)(2,1)} %shard_map.124), calls=%async_computation.1 | async-start | bytes 1835008 | tf_op jit(solution)/shard_map/all_to_all | solution.py:396
  51.3 1.0 collective-permute-start.8
  52.3 3.5 %collective-permute-start.7 = (bf16[80,1152]{1,0:T(8,128)(2,1)S(1)}, bf16[80,1152]{1,0:T(8,128)(2,1)S(1)}, u32[]{:S(2)}, u32[]{:S(2)}) collective-permute-start(bf16[80,1152]{1,0:T(8,128)(2,1)S(1)} %get-tuple-element.45.refs_0_), channel_id=1, source_target_pairs={{0,128},{64,192},{128,0},{192,64},{1,129},{65,193},{129,1},{193,65... | collective-permute-start | bytes 552968 | tf_op jit(solution)/shard_map/ppermute | solution.py:30
  55.8 4.0 %collective-permute-done.8.refs_6_ = bf16[80,1152]{1,0:T(8,128)(2,1)S(1)} collective-permute-done((bf16[80,1152]{1,0:T(8,128)(2,1)S(1)}, bf16[80,1152]{1,0:T(8,128)(2,1)S(1)}, u32[]{:S(2)}, u32[]{:S(2)}) %collective-permute-start.8) | collective-permute-done | bytes 184352 | tf_op jit(solution)/shard_map/ppermute | solution.py:30
  59.8 2.0 %collective-permute-done.7.refs_4_ = bf16[80,1152]{1,0:T(8,128)(2,1)S(1)} collective-permute-done((bf16[80,1152]{1,0:T(8,128)(2,1)S(1)}, bf16[80,1152]{1,0:T(8,128)(2,1)S(1)}, u32[]{:S(2)}, u32[]{:S(2)}) %collective-permute-start.7) | collective-permute-done | bytes 184352 | tf_op jit(solution)/shard_map/ppermute | solution.py:30
  67.5 2.8 %shard_map.122 = (f32[8,48,128]{2,1,0:T(8,128)S(1)}, bf16[8,48,128]{2,1,0:T(8,128)(2,1)S(1)}, bf16[8,48,128]{2,1,0:T(8,128)(2,1)S(1)}, bf16[8,48,128]{2,1,0:T(8,128)(2,1)S(1)}) custom-call(s32[1]{0:T(128)} %bitcast.3.y_ref, bf16[80,1152]{1,0:T(8,128)(2,1)S(1)} %get-tuple-element.45.refs_0_, bf16[80,1152]{1,0:T(8,128)(2,1)} %collective-permute-done.9.refs_1_, ...), custom_call_target="tpu_custom_call" | custom-call | tf_op jit(solution)/shard_map/pallas_call | solution.py:245
  70.3 1.6 %collective-permute-start.13 = (bf16[8,48,128]{2,1,0:T(8,128)(2,1)S(1)}, bf16[8,48,128]{2,1,0:T(8,128)(2,1)S(1)}, u32[]{:S(2)}, u32[]{:S(2)}) collective-permute-start(bf16[8,48,128]{2,1,0:T(8,128)(2,1)S(1)} %get-tuple-element.54), channel_id=1, source_target_pairs={{0,1},{1,2},{2,3},{3,0},{4,5},{5,6},{6,7},{7,4},{8,9},{9,10},{10,1... | collective-permute-start | bytes 294920 | tf_op jit(solution)/shard_map/ppermute | solution.py:34
  71.8 2.7 %collective-permute-start.14 = (bf16[8,48,128]{2,1,0:T(8,128)(2,1)S(1)}, bf16[8,48,128]{2,1,0:T(8,128)(2,1)S(1)}, u32[]{:S(2)}, u32[]{:S(2)}) collective-permute-start(bf16[8,48,128]{2,1,0:T(8,128)(2,1)S(1)} %get-tuple-element.55), channel_id=1, source_target_pairs={{0,2},{1,3},{2,0},{3,1},{4,6},{5,7},{6,4},{7,5},{8,10},{9,11},{10,... | collective-permute-start | bytes 294920 | tf_op jit(solution)/shard_map/ppermute | solution.py:34
  74.5 1.5 %collective-permute-start.15 = (bf16[8,48,128]{2,1,0:T(8,128)(2,1)S(1)}, bf16[8,48,128]{2,1,0:T(8,128)(2,1)S(1)}, u32[]{:S(2)}, u32[]{:S(2)}) collective-permute-start(bf16[8,48,128]{2,1,0:T(8,128)(2,1)S(1)} %get-tuple-element.56), channel_id=1, source_target_pairs={{0,3},{1,0},{2,1},{3,2},{4,7},{5,4},{6,5},{7,6},{8,11},{9,8},{10,9... | collective-permute-start | bytes 294920 | tf_op jit(solution)/shard_map/ppermute | solution.py:34
  76.0 2.6 %collective-permute-start.16 = (bf16[224,1152]{1,0:T(8,128)(2,1)S(1)}, bf16[224,1152]{1,0:T(8,128)(2,1)S(1)}, u32[]{:S(2)}, u32[]{:S(2)}) collective-permute-start(bf16[224,1152]{1,0:T(8,128)(2,1)S(1)} %slice.38), channel_id=1, source_target_pairs={{0,64},{64,128},{128,192},{192,0},{1,65},{65,129},{129,193},{193,1... | collective-permute-start | bytes 1548296 | tf_op jit(solution)/shard_map/ppermute | solution.py:30
  80.1 9.1 %collective-permute-done.16.refs_6_ = bf16[224,1152]{1,0:T(8,128)(2,1)S(1)} collective-permute-done((bf16[224,1152]{1,0:T(8,128)(2,1)S(1)}, bf16[224,1152]{1,0:T(8,128)(2,1)S(1)}, u32[]{:S(2)}, u32[]{:S(2)}) %collective-permute-start.16) | collective-permute-done | bytes 516128 | tf_op jit(solution)/shard_map/ppermute | solution.py:30
  89.2 5.2 %collective-permute-done.17.refs_7_ = bf16[208,1152]{1,0:T(8,128)(2,1)} collective-permute-done((bf16[208,1152]{1,0:T(8,128)(2,1)S(1)}, bf16[208,1152]{1,0:T(8,128)(2,1)}, u32[]{:S(2)}, u32[]{:S(2)}) %collective-permute-start.17) | collective-permute-done | bytes 479264 | tf_op jit(solution)/shard_map/ppermute | solution.py:30
  95.1 6.7 %all-to-all-start.2 = ((bf16[8,48,128]{2,1,0:T(8,128)(2,1)}), bf16[8,48,128]{2,1,0:T(8,128)(2,1)S(1)}, u32[]{:S(2)}, u32[]{:S(2)}) async-start(bf16[8,48,128]{2,1,0:T(8,128)(2,1)} %shard_map.123), calls=%async_computation.2 | async-start | bytes 196608 | tf_op jit(solution)/shard_map/all_to_all | solution.py:408
  102.7 6.0 %shard_map.125 = (bf16[128,1152]{1,0:T(8,128)(2,1)}, bf16[128,1152]{1,0:T(8,128)(2,1)}, bf16[128,1152]{1,0:T(8,128)(2,1)}, bf16[128,1152]{1,0:T(8,128)(2,1)}) custom-call(s32[2]{0:T(128)S(1)} %pad_add_fusion.at_ref.refs_0_, bf16[256,256]{1,0:T(8,128)(2,1)S(1)} %copy-done.10, bf16[32,8,1792]{2,1,0:T(8,128)(2,1)S(1)} %all-to-all-done.1.refs_2_, ...), custom_call_target="tpu_custom_call" | custom-call | flops 1019215872 | bytes 7962624 | tf_op jit(solution)/shard_map/pallas_call | solution.py:350
  108.7 2.1 %all-to-all-done.2.terms_ref = bf16[8,48,128]{2,1,0:T(8,128)(2,1)S(1)} async-done(((bf16[8,48,128]{2,1,0:T(8,128)(2,1)}), bf16[8,48,128]{2,1,0:T(8,128)(2,1)S(1)}, u32[]{:S(2)}, u32[]{:S(2)}) %all-to-all-start.2) | async-done | bytes 98336 | tf_op jit(solution)/shard_map/all_to_all | solution.py:408
  (81 shorter events, 18.4 us)
Async XLA Ops:
  7.7 32.2 %collective-permute-start.1 = (bf16[432,1152]{1,0:T(8,128)(2,1)}, bf16[432,1152]{1,0:T(8,128)(2,1)S(1)}, u32[]{:S(2)}, u32[]{:S(2)}) collective-permute-start(bf16[432,1152]{1,0:T(8,128)(2,1)} %get-tuple-element.38.refs_3_), channel_id=1, source_target_pairs={{0,192},{64,0},{128,64},{192,128},{1,193},{65,1},{129,65},{193,129... | collective-permute-start | bytes 2985992 | tf_op jit(solution)/shard_map/ppermute | solution.py:30
  8.5 31.4 %collective-permute-start = (bf16[432,1152]{1,0:T(8,128)(2,1)}, bf16[432,1152]{1,0:T(8,128)(2,1)S(1)}, u32[]{:S(2)}, u32[]{:S(2)}) collective-permute-start(bf16[432,1152]{1,0:T(8,128)(2,1)} %get-tuple-element.38.refs_3_), channel_id=1, source_target_pairs={{0,64},{64,128},{128,192},{192,0},{1,65},{65,129},{129,193},{193,1... | collective-permute-start | bytes 2985992 | tf_op jit(solution)/shard_map/ppermute | solution.py:30
  13.5 11.5 %collective-permute-start.2 = (bf16[4,80,256]{2,1,0:T(8,128)(2,1)S(1)}, bf16[4,80,256]{2,1,0:T(8,128)(2,1)S(1)}, u32[]{:S(2)}, u32[]{:S(2)}) collective-permute-start(bf16[4,80,256]{2,1,0:T(8,128)(2,1)S(1)} %get-tuple-element.40), channel_id=1, source_target_pairs={{0,32},{32,0},{1,33},{33,1},{2,34},{34,2},{3,35},{35,3},{4,36},{36... | collective-permute-start | bytes 491528 | tf_op jit(solution)/shard_map/ppermute | solution.py:38
  13.5 26.4 %all-to-all-start = ((bf16[32,8,640]{2,1,0:T(8,128)(2,1)}), bf16[32,8,640]{2,1,0:T(8,128)(2,1)S(1)}, u32[]{:S(2)}, u32[]{:S(2)}) async-start(bf16[32,8,640]{2,1,0:T(8,128)(2,1)} %get-tuple-element.37), calls=%async_computation | async-start | bytes 655360 | tf_op jit(solution)/shard_map/all_to_all | solution.py:381
  25.1 10.6 %collective-permute-start.3 = (bf16[160,256]{1,0:T(8,128)(2,1)S(1)}, bf16[160,256]{1,0:T(8,128)(2,1)S(1)}, u32[]{:S(2)}, u32[]{:S(2)}) collective-permute-start(bf16[160,256]{1,0:T(8,128)(2,1)S(1)} %pad_maximum_fusion.1), channel_id=1, source_target_pairs={{0,64},{64,128},{128,192},{192,0},{1,65},{65,129},{129,193},{193,1... | collective-permute-start | bytes 245768 | tf_op jit(solution)/shard_map/ppermute | solution.py:30
  25.2 10.5 %collective-permute-start.4 = (bf16[160,256]{1,0:T(8,128)(2,1)S(1)}, bf16[160,256]{1,0:T(8,128)(2,1)S(1)}, u32[]{:S(2)}, u32[]{:S(2)}) collective-permute-start(bf16[160,256]{1,0:T(8,128)(2,1)S(1)} %pad_maximum_fusion.2), channel_id=1, source_target_pairs={{0,128},{64,192},{128,0},{192,64},{1,129},{65,193},{129,1},{193,65... | collective-permute-start | bytes 245768 | tf_op jit(solution)/shard_map/ppermute | solution.py:30
  26.9 9.5 %collective-permute-start.5 = (bf16[160,256]{1,0:T(8,128)(2,1)S(1)}, bf16[160,256]{1,0:T(8,128)(2,1)S(1)}, u32[]{:S(2)}, u32[]{:S(2)}) collective-permute-start(bf16[160,256]{1,0:T(8,128)(2,1)S(1)} %pad_maximum_fusion.3), channel_id=1, source_target_pairs={{0,192},{64,0},{128,64},{192,128},{1,193},{65,1},{129,65},{193,129... | collective-permute-start | bytes 245768 | tf_op jit(solution)/shard_map/ppermute | solution.py:30
  43.2 51.9 %all-to-all-start.1 = ((bf16[32,8,1792]{2,1,0:T(8,128)(2,1)}), bf16[32,8,1792]{2,1,0:T(8,128)(2,1)S(1)}, u32[]{:S(2)}, u32[]{:S(2)}) async-start(bf16[32,8,1792]{2,1,0:T(8,128)(2,1)} %shard_map.124), calls=%async_computation.1 | async-start | bytes 1835008 | tf_op jit(solution)/shard_map/all_to_all | solution.py:396
  51.3 8.5 %collective-permute-start.8 = (bf16[80,1152]{1,0:T(8,128)(2,1)S(1)}, bf16[80,1152]{1,0:T(8,128)(2,1)S(1)}, u32[]{:S(2)}, u32[]{:S(2)}) collective-permute-start(bf16[80,1152]{1,0:T(8,128)(2,1)S(1)} %get-tuple-element.45.refs_0_), channel_id=1, source_target_pairs={{0,192},{64,0},{128,64},{192,128},{1,193},{65,1},{129,65},{193,129... | collective-permute-start | bytes 552968 | tf_op jit(solution)/shard_map/ppermute | solution.py:30
  52.3 9.5 %collective-permute-start.7 = (bf16[80,1152]{1,0:T(8,128)(2,1)S(1)}, bf16[80,1152]{1,0:T(8,128)(2,1)S(1)}, u32[]{:S(2)}, u32[]{:S(2)}) collective-permute-start(bf16[80,1152]{1,0:T(8,128)(2,1)S(1)} %get-tuple-element.45.refs_0_), channel_id=1, source_target_pairs={{0,128},{64,192},{128,0},{192,64},{1,129},{65,193},{129,1},{193,65... | collective-permute-start | bytes 552968 | tf_op jit(solution)/shard_map/ppermute | solution.py:30
  55.8 6.6 %collective-permute-start.6 = (bf16[80,1152]{1,0:T(8,128)(2,1)S(1)}, bf16[80,1152]{1,0:T(8,128)(2,1)}, u32[]{:S(2)}, u32[]{:S(2)}) collective-permute-start(bf16[80,1152]{1,0:T(8,128)(2,1)S(1)} %get-tuple-element.45.refs_0_), channel_id=1, source_target_pairs={{0,64},{64,128},{128,192},{192,0},{1,65},{65,129},{129,193},{193,1... | collective-permute-start | bytes 552968 | tf_op jit(solution)/shard_map/ppermute | solution.py:30
  62.4 2.1 %collective-permute-start.10 = (bf16[80,1152]{1,0:T(8,128)(2,1)}, bf16[80,1152]{1,0:T(8,128)(2,1)}, u32[]{:S(2)}, u32[]{:S(2)}) collective-permute-start(bf16[80,1152]{1,0:T(8,128)(2,1)} %collective-permute-done.6.refs_2_), channel_id=1, source_target_pairs={{0,32},{32,0},{1,33},{33,1},{2,34},{34,2},{3,35},{35,3},{4,36},{36... | collective-permute-start | bytes 552968 | tf_op jit(solution)/shard_map/ppermute | solution.py:38
  63.0 1.8 %collective-permute-start.12 = (bf16[80,1152]{1,0:T(8,128)(2,1)S(1)}, bf16[80,1152]{1,0:T(8,128)(2,1)}, u32[]{:S(2)}, u32[]{:S(2)}) collective-permute-start(bf16[80,1152]{1,0:T(8,128)(2,1)S(1)} %collective-permute-done.8.refs_6_), channel_id=1, source_target_pairs={{0,32},{32,0},{1,33},{33,1},{2,34},{34,2},{3,35},{35,3},{4,36},{36... | collective-permute-start | bytes 552968 | tf_op jit(solution)/shard_map/ppermute | solution.py:38
  70.3 8.4 %collective-permute-start.13 = (bf16[8,48,128]{2,1,0:T(8,128)(2,1)S(1)}, bf16[8,48,128]{2,1,0:T(8,128)(2,1)S(1)}, u32[]{:S(2)}, u32[]{:S(2)}) collective-permute-start(bf16[8,48,128]{2,1,0:T(8,128)(2,1)S(1)} %get-tuple-element.54), channel_id=1, source_target_pairs={{0,1},{1,2},{2,3},{3,0},{4,5},{5,6},{6,7},{7,4},{8,9},{9,10},{10,1... | collective-permute-start | bytes 294920 | tf_op jit(solution)/shard_map/ppermute | solution.py:34
  71.8 7.7 %collective-permute-start.14 = (bf16[8,48,128]{2,1,0:T(8,128)(2,1)S(1)}, bf16[8,48,128]{2,1,0:T(8,128)(2,1)S(1)}, u32[]{:S(2)}, u32[]{:S(2)}) collective-permute-start(bf16[8,48,128]{2,1,0:T(8,128)(2,1)S(1)} %get-tuple-element.55), channel_id=1, source_target_pairs={{0,2},{1,3},{2,0},{3,1},{4,6},{5,7},{6,4},{7,5},{8,10},{9,11},{10,... | collective-permute-start | bytes 294920 | tf_op jit(solution)/shard_map/ppermute | solution.py:34
  74.5 5.1 %collective-permute-start.15 = (bf16[8,48,128]{2,1,0:T(8,128)(2,1)S(1)}, bf16[8,48,128]{2,1,0:T(8,128)(2,1)S(1)}, u32[]{:S(2)}, u32[]{:S(2)}) collective-permute-start(bf16[8,48,128]{2,1,0:T(8,128)(2,1)S(1)} %get-tuple-element.56), channel_id=1, source_target_pairs={{0,3},{1,0},{2,1},{3,2},{4,7},{5,4},{6,5},{7,6},{8,11},{9,8},{10,9... | collective-permute-start | bytes 294920 | tf_op jit(solution)/shard_map/ppermute | solution.py:34
  76.0 13.2 %collective-permute-start.16 = (bf16[224,1152]{1,0:T(8,128)(2,1)S(1)}, bf16[224,1152]{1,0:T(8,128)(2,1)S(1)}, u32[]{:S(2)}, u32[]{:S(2)}) collective-permute-start(bf16[224,1152]{1,0:T(8,128)(2,1)S(1)} %slice.38), channel_id=1, source_target_pairs={{0,64},{64,128},{128,192},{192,0},{1,65},{65,129},{129,193},{193,1... | collective-permute-start | bytes 1548296 | tf_op jit(solution)/shard_map/ppermute | solution.py:30
  78.6 23.1 %collective-permute-start.18 = (bf16[432,1152]{1,0:T(8,128)(2,1)}, bf16[432,1152]{1,0:T(8,128)(2,1)}, u32[]{:S(2)}, u32[]{:S(2)}) collective-permute-start(bf16[432,1152]{1,0:T(8,128)(2,1)} %get-tuple-element.38.refs_3_), channel_id=1, source_target_pairs={{0,32},{32,0},{1,33},{33,1},{2,34},{34,2},{3,35},{35,3},{4,36},{36... | collective-permute-start | bytes 2985992 | tf_op jit(solution)/shard_map/ppermute | solution.py:38
  78.6 23.1 %collective-permute-start.19 = (bf16[432,1152]{1,0:T(8,128)(2,1)S(1)}, bf16[432,1152]{1,0:T(8,128)(2,1)}, u32[]{:S(2)}, u32[]{:S(2)}) collective-permute-start(bf16[432,1152]{1,0:T(8,128)(2,1)S(1)} %collective-permute-done.refs_4_), channel_id=1, source_target_pairs={{0,32},{32,0},{1,33},{33,1},{2,34},{34,2},{3,35},{35,3},{4,36},{36... | collective-permute-start | bytes 2985992 | tf_op jit(solution)/shard_map/ppermute | solution.py:38
  79.6 22.2 %collective-permute-start.20 = (bf16[432,1152]{1,0:T(8,128)(2,1)S(1)}, bf16[432,1152]{1,0:T(8,128)(2,1)}, u32[]{:S(2)}, u32[]{:S(2)}) collective-permute-start(bf16[432,1152]{1,0:T(8,128)(2,1)S(1)} %collective-permute-done.1.refs_5_), channel_id=1, source_target_pairs={{0,32},{32,0},{1,33},{33,1},{2,34},{34,2},{3,35},{35,3},{4,36},{36... | collective-permute-start | bytes 2985992 | tf_op jit(solution)/shard_map/ppermute | solution.py:38
  79.6 14.8 %collective-permute-start.17 = (bf16[208,1152]{1,0:T(8,128)(2,1)S(1)}, bf16[208,1152]{1,0:T(8,128)(2,1)}, u32[]{:S(2)}, u32[]{:S(2)}) collective-permute-start(bf16[208,1152]{1,0:T(8,128)(2,1)S(1)} %slice.39), channel_id=1, source_target_pairs={{0,192},{64,0},{128,64},{192,128},{1,193},{65,1},{129,65},{193,129... | collective-permute-start | bytes 1437704 | tf_op jit(solution)/shard_map/ppermute | solution.py:30
  89.2 12.6 %collective-permute-start.21 = (bf16[224,1152]{1,0:T(8,128)(2,1)S(1)}, bf16[224,1152]{1,0:T(8,128)(2,1)}, u32[]{:S(2)}, u32[]{:S(2)}) collective-permute-start(bf16[224,1152]{1,0:T(8,128)(2,1)S(1)} %collective-permute-done.16.refs_6_), channel_id=1, source_target_pairs={{0,32},{32,0},{1,33},{33,1},{2,34},{34,2},{3,35},{35,3},{4,36},{36... | collective-permute-start | bytes 1548296 | tf_op jit(solution)/shard_map/ppermute | solution.py:38
  94.4 7.4 %collective-permute-start.22 = (bf16[208,1152]{1,0:T(8,128)(2,1)}, bf16[208,1152]{1,0:T(8,128)(2,1)}, u32[]{:S(2)}, u32[]{:S(2)}) collective-permute-start(bf16[208,1152]{1,0:T(8,128)(2,1)} %collective-permute-done.17.refs_7_), channel_id=1, source_target_pairs={{0,32},{32,0},{1,33},{33,1},{2,34},{34,2},{3,35},{35,3},{4,36},{36... | collective-permute-start | bytes 1437704 | tf_op jit(solution)/shard_map/ppermute | solution.py:38
  95.1 15.7 %all-to-all-start.2 = ((bf16[8,48,128]{2,1,0:T(8,128)(2,1)}), bf16[8,48,128]{2,1,0:T(8,128)(2,1)S(1)}, u32[]{:S(2)}, u32[]{:S(2)}) async-start(bf16[8,48,128]{2,1,0:T(8,128)(2,1)} %shard_map.123), calls=%async_computation.2 | async-start | bytes 196608 | tf_op jit(solution)/shard_map/all_to_all | solution.py:408
  (20 other events, 45.2 us)

commit v5 on v4

v5 whole, which is shorter than its diff:
```python
import jax
import jax.numpy as jnp
from jax import lax
from jax.experimental import pallas as pl
from jax.experimental.pallas import tpu as pltpu
from jax.sharding import Mesh, PartitionSpec as P

DP = ("x", "core")
CTX = ("z", "y")
BF16 = jnp.bfloat16
F32 = jnp.float32
VMEM = pl.BlockSpec(memory_space=pltpu.VMEM)
SMEM = pl.BlockSpec(memory_space=pltpu.SMEM)
HBM = pl.BlockSpec(memory_space=pltpu.HBM)
PARAMS = pltpu.CompilerParams(vmem_limit_bytes=32 << 20)

WIDTH = 1152
MERGE = 4
TOKENS = 20
SLOTS = 32
SHARD = 144
OWN = 36
QUARTER = 288
SAVED_WIDE = 384
SAVED_ROWS = 16
FIRST = 32
ROWS_HALF = 1792
TERM_ROWS = 48
REST = 5


def over_x(array, step):
    return lax.ppermute(array, "x", [(i, (i + step) % 4) for i in range(4)])


def over_y(array, step):
    return lax.ppermute(array, "y", [(i, (i + step) % 4) for i in range(4)])


def over_core(array):
    return lax.ppermute(array, "core", [(0, 1), (1, 0)])


def iota(shape, dim):
    return lax.broadcasted_iota(jnp.int32, shape, dim)


def onehot(condition):
    return jnp.where(condition, 1.0, 0.0).astype(BF16)


def matmul(a, b):
    return jnp.dot(a, b, preferred_element_type=F32)


def matmul_tn(a, b):
    return lax.dot_general(a, b, (((0,), (0,)), ((), ())), preferred_element_type=F32)


def quotient(value, by):
    return jnp.floor((value + 0.5) * (1.0 / by))


def message_kernel(
    slot_ref, saved_hbm, early, middle, late, message_ref, table_ref, stacked, saved_ref, sem
):
    fetch = pltpu.make_async_copy(saved_hbm, saved_ref, sem.at[3])
    fetch.start()
    stack = [
        pltpu.make_async_copy(ref, stacked.at[pl.ds(m * SHARD, SHARD)], sem.at[m])
        for m, ref in enumerate((early, middle, late))
    ]
    for copy in stack:
        copy.start()
    source = slot_ref[...].astype(F32)
    sender = quotient(source, TOKENS)
    place = source - TOKENS * sender
    both = jnp.where(iota((8, SLOTS), 0) == 0, sender, place).astype(BF16)
    repeat = onehot(iota((SLOTS, SLOTS * MERGE), 1) // MERGE == iota((SLOTS, SLOTS * MERGE), 0))
    wide = matmul(both, repeat)
    sender, place = wide[0:1], wide[1:2]
    count = MERGE * SLOTS
    row, column = iota((count, count), 0), iota((count, count), 1)
    match = (sender == (row // MERGE).astype(F32)) & (row % MERGE == column % MERGE)
    tag = jnp.sum(jnp.where(match, place + 1.0, 0.0), axis=1, keepdims=True)
    tag = jnp.broadcast_to(tag, (count, SAVED_WIDE - QUARTER))
    match = onehot(match)
    fetch.wait()
    sorted_rows = matmul(match, saved_ref[...])
    for y in range(4):
        blocks = [sorted_rows[:, OWN * c : OWN * (c + 1)] for c in range(y, SLOTS, 4)]
        message = jnp.concatenate(blocks + [tag], axis=1).astype(BF16)
        for z in range(8):
            message_ref[4 * z + y] = message[SAVED_ROWS * z : SAVED_ROWS * (z + 1)]
    row, column = iota((2 * count, count), 0), iota((2 * count, count), 1)
    match = (sender == (row // 8).astype(F32)) & (row % MERGE == column % MERGE)
    table_ref[:, :count] = onehot(match & (row % 8 < MERGE))
    table_ref[:, count:] = onehot(match & (row % 8 >= MERGE))
    for copy in stack:
        copy.wait()


def make_message(slot, saved, projections):
    return pl.pallas_call(
        message_kernel,
        out_shape=(
            jax.ShapeDtypeStruct((SLOTS, SAVED_ROWS, SAVED_WIDE), BF16),
            jax.ShapeDtypeStruct((8 * SLOTS, 2 * MERGE * SLOTS), BF16),
            jax.ShapeDtypeStruct((3 * SHARD, WIDTH), BF16),
        ),
        in_specs=[VMEM] + [HBM] * 4,
        out_specs=(VMEM, VMEM, HBM),
        scratch_shapes=[
            pltpu.VMEM((MERGE * SLOTS, WIDTH), BF16),
            pltpu.SemaphoreType.DMA((4,)),
        ],
        compiler_params=PARAMS,
    )(slot, saved, *projections)


def rows_kernel(early_ref, middle_ref, late_ref, rows_ref, shares_ref, sums):
    used = MERGE * TOKENS
    for j in range(MERGE):
        at = slice(j * WIDTH, (j + 1) * WIDTH)
        to = slice(j * TOKENS, (j + 1) * TOKENS)
        late = late_ref[:, at].astype(F32)
        middle = late + middle_ref[:, at].astype(F32)
        sums[to, 2 * WIDTH : 3 * WIDTH] = late
        sums[to, WIDTH : 2 * WIDTH] = middle
        sums[to, :WIDTH] = middle + early_ref[:, at].astype(F32)
    rows_ref[...] = jnp.zeros_like(rows_ref)
    rows_ref[FIRST : FIRST + used, : 3 * WIDTH] = sums[...].astype(BF16)
    early = sums[:, :WIDTH]
    main = [early[:, d * SHARD : d * SHARD + 128] for d in range(8)]
    rest = [early[:, d * SHARD + 128 : (d + 1) * SHARD] for d in range(8)]
    shares_ref[...] = jnp.concatenate(main + rest, axis=1).astype(BF16)


def make_rows(early, middle, late):
    return pl.pallas_call(
        rows_kernel,
        out_shape=(
            jax.ShapeDtypeStruct((128, 2 * ROWS_HALF), BF16),
            jax.ShapeDtypeStruct((MERGE * TOKENS, WIDTH), BF16),
        ),
        in_specs=[VMEM] * 3,
        out_specs=(VMEM,) * 2,
        scratch_shapes=[pltpu.VMEM((MERGE * TOKENS, 3 * WIDTH), F32)],
        compiler_params=PARAMS,
    )(early, middle, late)


def place_key(column):
    j = sum((column >= k * TOKENS).astype(jnp.int32) for k in range(1, MERGE))
    return column - TOKENS * j + 1 + 32 * j


def pack_kernel(at_ref, arrived_ref, rows_ref, packed_ref):
    arrived = arrived_ref[...].astype(F32).reshape(SLOTS * SAVED_ROWS, SAVED_WIDE).astype(BF16)
    shape = (8 * SLOTS, SLOTS * SAVED_ROWS)
    row, column = iota(shape, 0), iota(shape, 1)
    mine = MERGE * at_ref[2]
    spread = onehot((row // 8 == column // SAVED_ROWS) & (column % SAVED_ROWS == mine))
    asked = matmul(spread, arrived[:, SAVED_WIDE - 128 :])
    row, column = iota((8 * SLOTS, 128), 0), iota((8 * SLOTS, 128), 1)
    inside = (column >= FIRST) & (column < FIRST + MERGE * TOKENS)
    key = place_key(column - FIRST).astype(F32)
    match = inside & (asked + (32 * (row % MERGE)).astype(F32) == key)
    packed = matmul(onehot(match & (row % 8 < MERGE)), rows_ref[:, :ROWS_HALF])
    packed = packed + matmul(onehot(match & (row % 8 >= MERGE)), rows_ref[:, ROWS_HALF:])
    packed_ref[...] = packed.reshape(SLOTS, 8, ROWS_HALF).astype(BF16)


def pack(at, arrived, rows):
    return pl.pallas_call(
        pack_kernel,
        out_shape=jax.ShapeDtypeStruct((SLOTS, 8, ROWS_HALF), BF16),
        in_specs=[SMEM, VMEM, VMEM],
        out_specs=VMEM,
        compiler_params=PARAMS,
    )(at, arrived, rows)


def gradient_kernel(at_ref, arrived_ref, *refs):
    shares, (keep_ref, give_ref, product, terms) = refs[:4], refs[4:]
    x, core, y = at_ref[0], at_ref[1], at_ref[2]
    used = MERGE * TOKENS
    arrived = arrived_ref[...].astype(F32).reshape(SLOTS * SAVED_ROWS, SAVED_WIDE)
    row = iota((SLOTS * SAVED_ROWS, 128), 0)
    behind = (y + 4 - row // MERGE % 4) % 4
    tag = arrived[:, SAVED_WIDE - 128 :] + (32 * (row % MERGE) + 128 * behind).astype(F32)
    column = iota((1, 4 * used), 1)
    block = sum((column >= k * used).astype(jnp.int32) for k in range(1, 4))
    key = (place_key(column - used * block) + 128 * block).astype(F32)
    match = onehot(tag[:, 127:128] == key)
    saved = matmul_tn(arrived.astype(BF16), match)[:QUARTER].astype(BF16)
    product[...] = matmul(saved, jnp.concatenate([ref[...] for ref in shares], axis=0))

    line = iota((1, QUARTER), 1).astype(F32)
    block = quotient(line, OWN)
    inside = line - OWN * block
    group = quotient(inside, 8)
    to = 8 * REST * (inside - 8 * group) + REST * block + group
    order = onehot(iota((8 * 8 * REST, QUARTER), 0).astype(F32) == to)
    rest = matmul(order, product[:, 8 * 128 :].astype(BF16))
    at = iota((8 * REST, 128), 1) // 16
    fill = jnp.zeros((TERM_ROWS - OWN - REST, 128), F32)
    for d in range(8):
        folded = jnp.zeros((8 * REST, 128), F32)
        for b in range(8):
            part = rest[8 * REST * b : 8 * REST * (b + 1)]
            if b != d:
                part = pltpu.roll(part, 16 * (b - d) % 128, 1)
            folded = jnp.where(at == b, part, folded)
        step = lax.rem(d // 2 + 4 - x, 4)
        side = lax.rem(d % 2 + core, 2)
        for z in range(8):
            main = product[OWN * z : OWN * (z + 1), 128 * d : 128 * (d + 1)]
            parts = [main, folded[REST * z : REST * (z + 1)], fill]
            terms[side, step, z] = jnp.concatenate(parts, axis=0)
    keep_ref[...] = terms[0]
    give_ref[...] = terms[1].astype(BF16)


def gradient(at, arrived, shares):
    shape = (4, 8, TERM_ROWS, 128)
    return pl.pallas_call(
        gradient_kernel,
        out_shape=(jax.ShapeDtypeStruct(shape, F32), jax.ShapeDtypeStruct(shape, BF16)),
        in_specs=[SMEM] + [VMEM] * 5,
        out_specs=(VMEM,) * 2,
        scratch_shapes=[pltpu.VMEM((QUARTER, WIDTH), F32), pltpu.VMEM((2, *shape), F32)],
        compiler_params=PARAMS,
    )(at, arrived, *shares)


def core_kernel(keep_ref, given_ref, *out_refs):
    for step, out in enumerate(out_refs):
        out[...] = (keep_ref[step] + given_ref[step].astype(F32)).astype(out.dtype)


def sum_core(keep, given):
    shape = keep.shape[1:]
    return pl.pallas_call(
        core_kernel,
        out_shape=[jax.ShapeDtypeStruct(shape, F32)] + [jax.ShapeDtypeStruct(shape, BF16)] * 3,
        in_specs=[VMEM] * 2,
        out_specs=[VMEM] * 4,
        compiler_params=PARAMS,
    )(keep, given)


def sum_kernel(own_ref, first, second, third, out_ref):
    total = own_ref[...]
    for ref in (first, second, third):
        total = total + ref[...].astype(F32)
    out_ref[...] = total.astype(BF16)


def sum_x(own, parts):
    return pl.pallas_call(
        sum_kernel,
        out_shape=jax.ShapeDtypeStruct(own.shape, BF16),
        in_specs=[VMEM] * 4,
        out_specs=VMEM,
        compiler_params=PARAMS,
    )(own, *parts)


def total_kernel(terms_ref, out_ref):
    total = terms_ref[0].astype(F32)
    for c in range(1, 8):
        total = total + terms_ref[c].astype(F32)
    rest = jnp.concatenate(
        [jnp.broadcast_to(total[OWN + a : OWN + a + 1], (8, 128)) for a in range(REST)], axis=0
    )[:OWN]
    line, column = iota((OWN, 128), 0), iota((OWN, 128), 1)
    rest = jnp.where(line % 8 == column // 16, rest, 0.0)
    for shift in (64, 32, 16):
        rest = rest + pltpu.roll(rest, shift, 1)
    out_ref[:, :128] = total[:OWN]
    out_ref[:, 128:] = rest[:, : SHARD - 128]


def add_up(terms):
    return pl.pallas_call(
        total_kernel,
        out_shape=jax.ShapeDtypeStruct((OWN, SHARD), F32),
        in_specs=[VMEM],
        out_specs=VMEM,
        compiler_params=PARAMS,
    )(terms)


def context_kernel(cut, at_ref, table_ref, landed_ref, *refs):
    pieces = refs[:10]
    early_out, middle_out, late_out, stream_out, weight, sem = refs[10:]
    x, core = at_ref[0], at_ref[1]
    copies = ([], [], [])

    def put(ref, first, rows, m, inside, of_x, of_core):
        base = pl.multiple_of((2 * of_x + of_core) * SHARD + inside, 16)
        copies[m].append(
            pltpu.make_async_copy(
                ref.at[pl.ds(first, rows)], weight.at[m, pl.ds(base, rows)], sem.at[m]
            )
        )

    for index, of_core in ((0, core), (5, 1 - core)):
        for k, step in enumerate((0, 3, 1)):
            for m in range(3):
                put(pieces[index + k], m * SHARD, SHARD, m, 0, lax.rem(x + step, 4), of_core)
        of_x = lax.rem(x + 2, 4)
        for ref, start, stop in ((pieces[index + 3], 0, cut), (pieces[index + 4], cut, 3 * SHARD)):
            for m in range(3):
                low, high = max(start, m * SHARD), min(stop, (m + 1) * SHARD)
                if low < high:
                    put(ref, low - start, high - low, m, low - m * SHARD, of_x, of_core)
    for m in range(3):
        for copy in copies[m]:
            copy.start()
    landed = landed_ref[...].astype(F32).reshape(8 * SLOTS, ROWS_HALF).astype(BF16)
    placed = matmul_tn(table_ref[...], landed).astype(BF16)
    half = MERGE * SLOTS
    placed = jnp.concatenate([placed[:half], placed[half:, : 3 * WIDTH - ROWS_HALF]], axis=1)
    stream_out[...] = placed[:, :WIDTH]
    for m, out in enumerate((early_out, middle_out, late_out)):
        for copy in copies[m]:
            copy.wait()
        out[...] = lax.dot_general(
            placed[:, m * WIDTH : (m + 1) * WIDTH],
            weight[m],
            (((1,), (1,)), ((), ())),
            preferred_element_type=F32,
        ).astype(BF16)


def contexts(at, table, landed, pieces, cut):
    rows = MERGE * SLOTS
    out = jax.ShapeDtypeStruct((rows, WIDTH), BF16)
    return pl.pallas_call(
        lambda *refs: context_kernel(cut, *refs),
        out_shape=(out,) * 4,
        in_specs=[SMEM, VMEM, VMEM] + [HBM] * 10,
        out_specs=(VMEM,) * 4,
        scratch_shapes=[
            pltpu.VMEM((3, WIDTH, WIDTH), BF16),
            pltpu.SemaphoreType.DMA((3,)),
        ],
        compiler_params=PARAMS,
        cost_estimate=pl.CostEstimate(
            flops=6 * rows * WIDTH * WIDTH, bytes_accessed=6 * WIDTH * WIDTH, transcendentals=0
        ),
    )(at, table, landed, *pieces)


def local(
    injected_early,
    injected_middle,
    injected_late,
    slot_source,
    saved_early,
    projection_early,
    projection_middle,
    projection_late,
):
    at = jnp.stack([lax.axis_index(name) for name in ("x", "core", "y")]).astype(jnp.int32)

    projections = (projection_early, projection_middle, projection_late)
    message, table, stacked = make_message(slot_source, saved_early[0], projections)
    arrived = lax.all_to_all(message, CTX, 0, 0, tiled=True)

    cut = 224
    from_left, from_right = over_x(stacked, 1), over_x(stacked, 3)
    rows, share = make_rows(injected_early[0], injected_middle[0], injected_late[0])
    shares = [share] + [over_y(share, step) for step in (1, 2, 3)]
    arrived, from_left, from_right, shares = lax.optimization_barrier(
        (arrived, from_left, from_right, shares)
    )

    landed = lax.all_to_all(pack(at, arrived, rows), CTX, 0, 0, tiled=True)

    far_left, far_right = over_x(from_left[:cut], 1), over_x(from_right[cut:], 3)

    keep, give = gradient(at, arrived, shares)
    given = over_core(give)
    given, far_left, far_right = lax.optimization_barrier((given, far_left, far_right))
    mine, *parts = sum_core(keep, given)
    parts = [over_x(part, step) for step, part in zip((1, 2, 3), parts)]
    terms = sum_x(mine, parts)
    terms, landed = lax.optimization_barrier((terms, landed))
    weights = add_up(lax.all_to_all(terms, "z", 0, 0, tiled=True))

    pieces = (stacked, from_left, from_right, far_left, far_right)
    pieces = pieces + tuple(over_core(piece) for piece in pieces)
    context_early, context_middle, context_late, stream = contexts(at, table, landed, pieces, cut)
    return context_early[None], context_middle[None], context_late[None], stream[None], weights


def solution(mesh):
    fine = Mesh(mesh.devices.reshape(4, 2, 8, 4), ("x", "core", "z", "y"))
    rows = P(DP, CTX, None)
    return jax.shard_map(
        local,
        mesh=fine,
        in_specs=(rows, rows, rows, P(DP, CTX), rows, P(DP, None), P(DP, None), P(DP, None)),
        out_specs=(rows, rows, rows, rows, P(CTX, DP)),
        check_vma=False,
    )
```

time: 113 us -> 98.2 us (0.87)
  starting transfers between devices: 46.5 us -> 38.4 us
  local copies, waits for them, and re-layouts: 11 us -> 7.13 us
  waiting for transfers between devices: 37.4 us -> 34.7 us
    ppermute x3, waiting for transfers between devices: 0.44 us -> 11.1 us  [over_y(): return lax.ppermute(array, 'y', [(i, (i + step) % 4) for i in range(4)])]
    ppermute x10 -> x7, waiting for transfers between devices: 30 us -> 20.6 us  [over_x(): return lax.ppermute(array, 'x', [(i, (i + step) % 4) for i in range(4)])]
    ppermute x10 -> x7, starting transfers between devices: 13 us -> 8.04 us  [over_x(): return lax.ppermute(array, 'x', [(i, (i + step) % 4) for i in range(4)])]
    unnamed x36 -> x20, local copies, waits for them, and re-layouts: 10.9 us -> 7.05 us
    all_to_all x1, waiting for transfers between devices: 3.55 us -> 0.01 us  [local(): arrived = lax.all_to_all(message, CTX, 0, 0, tiled=True)]
    all_to_all x1, starting transfers between devices: 8.05 us -> 6.3 us  [local(): landed = lax.all_to_all(pack(at, arrived, rows), CTX, 0, 0, tiled=True)]
    ppermute x10 -> x6, waiting for transfers between devices: 1.34 us -> 0.02 us  [over_core(): return lax.ppermute(array, 'core', [(0, 1), (1, 0)])]
  transfers between devices with their start and end apart: 26 -> 19, of which waited for: 13 -> 8; matrix products, arithmetic and copies ran while one was open for 0% -> 0% of each run, Pallas kernels for 10% -> 11%
where the time goes in v5:
time: 98.2 us; the launch traced here: 96.6 us
  starting transfers between devices  38.4 us (39%)
  waiting for transfers between devices  34.7 us (35%)
  Pallas kernels  15.5 us (16%)
  local copies, waits for them, and re-layouts  7.13 us (7%)
    ppermute x7, waiting for transfers between devices, over_x(): return lax.ppermute(array, 'x', [(i, (i + step) % 4) for i in range(4)])  20.6 us
    all_to_all x1, starting transfers between devices, local(): arrived = lax.all_to_all(message, CTX, 0, 0, tiled=True)  11.6 us
    ppermute x3, waiting for transfers between devices, over_y(): return lax.ppermute(array, 'y', [(i, (i + step) % 4) for i in range(4)])  11.1 us
    ppermute x7, starting transfers between devices, over_x(): return lax.ppermute(array, 'x', [(i, (i + step) % 4) for i in range(4)])  8.04 us
    all_to_all x1, starting transfers between devices, local(): weights = add_up(lax.all_to_all(terms, 'z', 0, 0, tiled=True))  7.11 us
    unnamed x20, local copies, waits for them, and re-layouts  7.05 us
    all_to_all x1, starting transfers between devices, local(): landed = lax.all_to_all(pack(at, arrived, rows), CTX, 0, 0, tiled=True)  6.3 us
    pallas_call x1, Pallas kernels, contexts(): pl.pallas_call(lambda *refs: context_kernel(cut, *refs), out_shape=(out,)...  6 us
  transfers between devices with their start and end apart: 19, of which 8 were waited for; matrix products, arithmetic and copies ran while one was open for 0% of the time, Pallas kernels for 11%

profile of v5, /device:TPU:6, one launch (start us, length us, event | category | flops | bytes accessed | tf_op | source)
XLA Modules:
  0.0 96.6 jit_solution(2150184840049465081)
XLA Ops:
  1.3 1.0 %copy-done = bf16[144,1152]{1,0:T(8,128)(2,1)S(1)} copy-done((bf16[144,1152]{1,0:T(8,128)(2,1)S(1)}, bf16[144,1152]{1,0:T(8,128)(2,1)}, u32[]{:S(2)}) %copy-start) | copy-done | bytes 331800
  2.3 1.0 %copy-done.1 = bf16[144,1152]{1,0:T(8,128)(2,1)S(1)} copy-done((bf16[144,1152]{1,0:T(8,128)(2,1)S(1)}, bf16[144,1152]{1,0:T(8,128)(2,1)}, u32[]{:S(2)}) %copy-start.1) | copy-done | bytes 331800
  3.2 1.0 %copy-done.2 = bf16[144,1152]{1,0:T(8,128)(2,1)S(1)} copy-done((bf16[144,1152]{1,0:T(8,128)(2,1)S(1)}, bf16[144,1152]{1,0:T(8,128)(2,1)}, u32[]{:S(2)}) %copy-start.2) | copy-done | bytes 331800
  4.2 1.0 copy-done.3
  5.2 1.8 %shard_map.119 = (bf16[32,16,384]{2,1,0:T(8,128)(2,1)}, bf16[256,256]{1,0:T(8,128)(2,1)S(1)}, bf16[432,1152]{1,0:T(8,128)(2,1)}) custom-call(s32[1,32]{1,0:T(1,128)S(1)} %copy-done.9, bf16[128,1152]{1,0:T(8,128)(2,1)S(1)} %bitcast.11, bf16[144,1152]{1,0:T(8,128)(2,1)S(1)} %copy-done, bf16[144,1152]{1,0:T(8,128)(2,1)S(1)} %copy-done.1, ...), custom_call_target="tpu_custom_call" | custom-call | tf_op jit(solution)/shard_map/pallas_call | solution.py:104
  8.5 2.4 %collective-permute-start = (bf16[432,1152]{1,0:T(8,128)(2,1)}, bf16[432,1152]{1,0:T(8,128)(2,1)S(1)}, u32[]{:S(2)}, u32[]{:S(2)}) collective-permute-start(bf16[432,1152]{1,0:T(8,128)(2,1)} %get-tuple-element.34.refs_3_), channel_id=1, source_target_pairs={{0,64},{64,128},{128,192},{192,0},{1,65},{65,129},{129,193},{193,1... | collective-permute-start | bytes 2985992 | tf_op jit(solution)/shard_map/ppermute | solution.py:33
  10.9 11.6 %all-to-all-start = ((bf16[32,16,384]{2,1,0:T(8,128)(2,1)}), bf16[32,16,384]{2,1,0:T(8,128)(2,1)S(1)}, u32[]{:S(2)}, u32[]{:S(2)}) async-start(bf16[32,16,384]{2,1,0:T(8,128)(2,1)} %get-tuple-element.33), calls=%async_computation | async-start | bytes 786432 | tf_op jit(solution)/shard_map/all_to_all | solution.py:371
  24.4 1.0 shard_map.120
  25.3 3.0 %collective-permute-start.4 = (bf16[80,1152]{1,0:T(8,128)(2,1)}, bf16[80,1152]{1,0:T(8,128)(2,1)S(1)}, u32[]{:S(2)}, u32[]{:S(2)}) collective-permute-start(bf16[80,1152]{1,0:T(8,128)(2,1)} %get-tuple-element.37.refs_0_), channel_id=1, source_target_pairs={{0,3},{1,0},{2,1},{3,2},{4,7},{5,4},{6,5},{7,6},{8,11},{9,8},{10,9... | collective-permute-start | bytes 552968 | tf_op jit(solution)/shard_map/ppermute | solution.py:37
  30.1 7.5 %collective-permute-done.4.refs_3_ = bf16[80,1152]{1,0:T(8,128)(2,1)S(1)} collective-permute-done((bf16[80,1152]{1,0:T(8,128)(2,1)}, bf16[80,1152]{1,0:T(8,128)(2,1)S(1)}, u32[]{:S(2)}, u32[]{:S(2)}) %collective-permute-start.4) | collective-permute-done | bytes 184352 | tf_op jit(solution)/shard_map/ppermute | solution.py:37
  38.6 2.6 %collective-permute-done.2.refs_1_ = bf16[80,1152]{1,0:T(8,128)(2,1)} collective-permute-done((bf16[80,1152]{1,0:T(8,128)(2,1)}, bf16[80,1152]{1,0:T(8,128)(2,1)}, u32[]{:S(2)}, u32[]{:S(2)}) %collective-permute-start.2) | collective-permute-done | bytes 184352 | tf_op jit(solution)/shard_map/ppermute | solution.py:37
  41.2 2.4 %shard_map.124 = bf16[32,8,1792]{2,1,0:T(8,128)(2,1)} custom-call(s32[3]{0:T(128)S(1)} %pad_add_fusion.at_ref.refs_0_, bf16[32,16,384]{2,1,0:T(8,128)(2,1)S(1)} %all-to-all-done.arrived_ref, bf16[128,3584]{1,0:T(8,128)(2,1)S(1)} %get-tuple-element.50.rows_ref), custom_call_target="tpu_custom_call" | custom-call | tf_op jit(solution)/shard_map/pallas_call | solution.py:175
  43.6 6.3 %all-to-all-start.1 = ((bf16[32,8,1792]{2,1,0:T(8,128)(2,1)}), bf16[32,8,1792]{2,1,0:T(8,128)(2,1)S(1)}, u32[]{:S(2)}, u32[]{:S(2)}) async-start(bf16[32,8,1792]{2,1,0:T(8,128)(2,1)} %shard_map.124), calls=%async_computation.1 | async-start | bytes 1835008 | tf_op jit(solution)/shard_map/all_to_all | solution.py:381
  49.9 2.8 %shard_map.121 = (f32[4,8,48,128]{3,2,1,0:T(8,128)S(1)}, bf16[4,8,48,128]{3,2,1,0:T(8,128)(2,1)S(1)}) custom-call(s32[3]{0:T(128)S(1)} %pad_add_fusion.at_ref.refs_0_, bf16[32,16,384]{2,1,0:T(8,128)(2,1)S(1)} %all-to-all-done.arrived_ref, bf16[80,1152]{1,0:T(8,128)(2,1)} %get-tuple-element.37.refs_0_, bf16[80,1152]{1,0:T(8,128)(2,1)} %collective-permute-done.2.refs_1_, ...), custom_call_target="tpu_custom_call" | custom-call | tf_op jit(solution)/shard_map/pallas_call | solution.py:227
  53.3 1.8 %collective-permute-start.7 = (bf16[208,1152]{1,0:T(8,128)(2,1)S(1)}, bf16[208,1152]{1,0:T(8,128)(2,1)}, u32[]{:S(2)}, u32[]{:S(2)}) collective-permute-start(bf16[208,1152]{1,0:T(8,128)(2,1)S(1)} %slice.7), channel_id=1, source_target_pairs={{0,192},{64,0},{128,64},{192,128},{1,193},{65,1},{129,65},{193,129... | collective-permute-start | bytes 1437704 | tf_op jit(solution)/shard_map/ppermute | solution.py:33
  55.6 12.2 %collective-permute-done.7.refs_7_ = bf16[208,1152]{1,0:T(8,128)(2,1)} collective-permute-done((bf16[208,1152]{1,0:T(8,128)(2,1)S(1)}, bf16[208,1152]{1,0:T(8,128)(2,1)}, u32[]{:S(2)}, u32[]{:S(2)}) %collective-permute-start.7) | collective-permute-done | bytes 479264 | tf_op jit(solution)/shard_map/ppermute | solution.py:33
  67.9 1.0 %collective-permute-start.8 = (bf16[8,48,128]{2,1,0:T(8,128)(2,1)S(1)}, bf16[8,48,128]{2,1,0:T(8,128)(2,1)S(1)}, u32[]{:S(2)}, u32[]{:S(2)}) collective-permute-start(bf16[8,48,128]{2,1,0:T(8,128)(2,1)S(1)} %get-tuple-element.47), channel_id=1, source_target_pairs={{0,64},{64,128},{128,192},{192,0},{1,65},{65,129},{129,193},{193,1... | collective-permute-start | bytes 294920 | tf_op jit(solution)/shard_map/ppermute | solution.py:33
  68.9 1.6 %collective-permute-start.9 = (bf16[8,48,128]{2,1,0:T(8,128)(2,1)S(1)}, bf16[8,48,128]{2,1,0:T(8,128)(2,1)S(1)}, u32[]{:S(2)}, u32[]{:S(2)}) collective-permute-start(bf16[8,48,128]{2,1,0:T(8,128)(2,1)S(1)} %get-tuple-element.48), channel_id=1, source_target_pairs={{0,128},{64,192},{128,0},{192,64},{1,129},{65,193},{129,1},{193,65... | collective-permute-start | bytes 294920 | tf_op jit(solution)/shard_map/ppermute | solution.py:33
  70.5 2.6 %collective-permute-done.8.first = bf16[8,48,128]{2,1,0:T(8,128)(2,1)S(1)} collective-permute-done((bf16[8,48,128]{2,1,0:T(8,128)(2,1)S(1)}, bf16[8,48,128]{2,1,0:T(8,128)(2,1)S(1)}, u32[]{:S(2)}, u32[]{:S(2)}) %collective-permute-start.8) | collective-permute-done | bytes 98336 | tf_op jit(solution)/shard_map/ppermute | solution.py:33
  73.1 1.9 %collective-permute-done.9.second = bf16[8,48,128]{2,1,0:T(8,128)(2,1)S(1)} collective-permute-done((bf16[8,48,128]{2,1,0:T(8,128)(2,1)S(1)}, bf16[8,48,128]{2,1,0:T(8,128)(2,1)S(1)}, u32[]{:S(2)}, u32[]{:S(2)}) %collective-permute-start.9) | collective-permute-done | bytes 98336 | tf_op jit(solution)/shard_map/ppermute | solution.py:33
  75.0 3.9 %collective-permute-done.10.third = bf16[8,48,128]{2,1,0:T(8,128)(2,1)S(1)} collective-permute-done((bf16[8,48,128]{2,1,0:T(8,128)(2,1)S(1)}, bf16[8,48,128]{2,1,0:T(8,128)(2,1)S(1)}, u32[]{:S(2)}, u32[]{:S(2)}) %collective-permute-start.10) | collective-permute-done | bytes 98336 | tf_op jit(solution)/shard_map/ppermute | solution.py:33
  79.6 7.1 %all-to-all-start.2 = ((bf16[8,48,128]{2,1,0:T(8,128)(2,1)}), bf16[8,48,128]{2,1,0:T(8,128)(2,1)S(1)}, u32[]{:S(2)}, u32[]{:S(2)}) async-start(bf16[8,48,128]{2,1,0:T(8,128)(2,1)} %shard_map.123), calls=%async_computation.2 | async-start | bytes 196608 | tf_op jit(solution)/shard_map/all_to_all | solution.py:392
  86.8 6.0 %shard_map.125 = (bf16[128,1152]{1,0:T(8,128)(2,1)}, bf16[128,1152]{1,0:T(8,128)(2,1)}, bf16[128,1152]{1,0:T(8,128)(2,1)}, bf16[128,1152]{1,0:T(8,128)(2,1)}) custom-call(s32[3]{0:T(128)S(1)} %pad_add_fusion.at_ref.refs_0_, bf16[256,256]{1,0:T(8,128)(2,1)S(1)} %copy-done.8, bf16[32,8,1792]{2,1,0:T(8,128)(2,1)S(1)} %all-to-all-done.1.refs_2_, ...), custom_call_target="tpu_custom_call" | custom-call | flops 1019215872 | bytes 7962624 | tf_op jit(solution)/shard_map/pallas_call | solution.py:341
  92.8 3.0 %all-to-all-done.2.terms_ref = bf16[8,48,128]{2,1,0:T(8,128)(2,1)S(1)} async-done(((bf16[8,48,128]{2,1,0:T(8,128)(2,1)}), bf16[8,48,128]{2,1,0:T(8,128)(2,1)S(1)}, u32[]{:S(2)}, u32[]{:S(2)}) %all-to-all-start.2) | async-done | bytes 98336 | tf_op jit(solution)/shard_map/all_to_all | solution.py:392
  (45 shorter events, 9.4 us)
Async XLA Ops:
  1.3 1.0 %copy-start = (bf16[144,1152]{1,0:T(8,128)(2,1)S(1)}, bf16[144,1152]{1,0:T(8,128)(2,1)}, u32[]{:S(2)}) copy-start(bf16[144,1152]{1,0:T(8,128)(2,1)} %early.1) | copy-start | bytes 995332
  2.3 1.0 %copy-start.1 = (bf16[144,1152]{1,0:T(8,128)(2,1)S(1)}, bf16[144,1152]{1,0:T(8,128)(2,1)}, u32[]{:S(2)}) copy-start(bf16[144,1152]{1,0:T(8,128)(2,1)} %middle.1) | copy-start | bytes 995332
  3.2 1.0 %copy-start.2 = (bf16[144,1152]{1,0:T(8,128)(2,1)S(1)}, bf16[144,1152]{1,0:T(8,128)(2,1)}, u32[]{:S(2)}) copy-start(bf16[144,1152]{1,0:T(8,128)(2,1)} %late.1) | copy-start | bytes 995332
  7.6 33.6 %collective-permute-start.1 = (bf16[432,1152]{1,0:T(8,128)(2,1)}, bf16[432,1152]{1,0:T(8,128)(2,1)S(1)}, u32[]{:S(2)}, u32[]{:S(2)}) collective-permute-start(bf16[432,1152]{1,0:T(8,128)(2,1)} %get-tuple-element.34.refs_3_), channel_id=1, source_target_pairs={{0,192},{64,0},{128,64},{192,128},{1,193},{65,1},{129,65},{193,129... | collective-permute-start | bytes 2985992 | tf_op jit(solution)/shard_map/ppermute | solution.py:33
  8.5 32.7 %collective-permute-start = (bf16[432,1152]{1,0:T(8,128)(2,1)}, bf16[432,1152]{1,0:T(8,128)(2,1)S(1)}, u32[]{:S(2)}, u32[]{:S(2)}) collective-permute-start(bf16[432,1152]{1,0:T(8,128)(2,1)} %get-tuple-element.34.refs_3_), channel_id=1, source_target_pairs={{0,64},{64,128},{128,192},{192,0},{1,65},{65,129},{129,193},{193,1... | collective-permute-start | bytes 2985992 | tf_op jit(solution)/shard_map/ppermute | solution.py:33
  10.9 11.6 %copy-start.4 = (bf16[1,20,4608]{2,1,0:T(8,128)(2,1)S(1)}, bf16[1,20,4608]{2,1,0:T(8,128)(2,1)}, u32[]{:S(2)}) copy-start(bf16[1,20,4608]{2,1,0:T(8,128)(2,1)} %param.8) | copy-start | bytes 552964
  10.9 30.3 %all-to-all-start = ((bf16[32,16,384]{2,1,0:T(8,128)(2,1)}), bf16[32,16,384]{2,1,0:T(8,128)(2,1)S(1)}, u32[]{:S(2)}, u32[]{:S(2)}) async-start(bf16[32,16,384]{2,1,0:T(8,128)(2,1)} %get-tuple-element.33), calls=%async_computation | async-start | bytes 786432 | tf_op jit(solution)/shard_map/all_to_all | solution.py:371
  25.3 12.3 %collective-permute-start.4 = (bf16[80,1152]{1,0:T(8,128)(2,1)}, bf16[80,1152]{1,0:T(8,128)(2,1)S(1)}, u32[]{:S(2)}, u32[]{:S(2)}) collective-permute-start(bf16[80,1152]{1,0:T(8,128)(2,1)} %get-tuple-element.37.refs_0_), channel_id=1, source_target_pairs={{0,3},{1,0},{2,1},{3,2},{4,7},{5,4},{6,5},{7,6},{8,11},{9,8},{10,9... | collective-permute-start | bytes 552968 | tf_op jit(solution)/shard_map/ppermute | solution.py:37
  28.3 10.2 %collective-permute-start.3 = (bf16[80,1152]{1,0:T(8,128)(2,1)}, bf16[80,1152]{1,0:T(8,128)(2,1)}, u32[]{:S(2)}, u32[]{:S(2)}) collective-permute-start(bf16[80,1152]{1,0:T(8,128)(2,1)} %get-tuple-element.37.refs_0_), channel_id=1, source_target_pairs={{0,2},{1,3},{2,0},{3,1},{4,6},{5,7},{6,4},{7,5},{8,10},{9,11},{10,... | collective-permute-start | bytes 552968 | tf_op jit(solution)/shard_map/ppermute | solution.py:37
  29.2 12.0 %collective-permute-start.2 = (bf16[80,1152]{1,0:T(8,128)(2,1)}, bf16[80,1152]{1,0:T(8,128)(2,1)}, u32[]{:S(2)}, u32[]{:S(2)}) collective-permute-start(bf16[80,1152]{1,0:T(8,128)(2,1)} %get-tuple-element.37.refs_0_), channel_id=1, source_target_pairs={{0,1},{1,2},{2,3},{3,0},{4,5},{5,6},{6,7},{7,4},{8,9},{9,10},{10,1... | collective-permute-start | bytes 552968 | tf_op jit(solution)/shard_map/ppermute | solution.py:37
  43.6 36.0 %all-to-all-start.1 = ((bf16[32,8,1792]{2,1,0:T(8,128)(2,1)}), bf16[32,8,1792]{2,1,0:T(8,128)(2,1)S(1)}, u32[]{:S(2)}, u32[]{:S(2)}) async-start(bf16[32,8,1792]{2,1,0:T(8,128)(2,1)} %shard_map.124), calls=%async_computation.1 | async-start | bytes 1835008 | tf_op jit(solution)/shard_map/all_to_all | solution.py:381
  52.7 2.9 %collective-permute-start.5 = (bf16[4,8,48,128]{3,2,1,0:T(8,128)(2,1)S(1)}, bf16[4,8,48,128]{3,2,1,0:T(8,128)(2,1)S(1)}, u32[]{:S(2)}, u32[]{:S(2)}) collective-permute-start(bf16[4,8,48,128]{3,2,1,0:T(8,128)(2,1)S(1)} %get-tuple-element.42), channel_id=1, source_target_pairs={{0,32},{32,0},{1,33},{33,1},{2,34},{34,2},{3,35},{35,3},{4,36},{36... | collective-permute-start | bytes 1179656 | tf_op jit(solution)/shard_map/ppermute | solution.py:41
  52.8 14.9 %collective-permute-start.6 = (bf16[224,1152]{1,0:T(8,128)(2,1)S(1)}, bf16[224,1152]{1,0:T(8,128)(2,1)}, u32[]{:S(2)}, u32[]{:S(2)}) collective-permute-start(bf16[224,1152]{1,0:T(8,128)(2,1)S(1)} %slice.6), channel_id=1, source_target_pairs={{0,64},{64,128},{128,192},{192,0},{1,65},{65,129},{129,193},{193,1... | collective-permute-start | bytes 1548296 | tf_op jit(solution)/shard_map/ppermute | solution.py:33
  53.3 14.5 %collective-permute-start.7 = (bf16[208,1152]{1,0:T(8,128)(2,1)S(1)}, bf16[208,1152]{1,0:T(8,128)(2,1)}, u32[]{:S(2)}, u32[]{:S(2)}) collective-permute-start(bf16[208,1152]{1,0:T(8,128)(2,1)S(1)} %slice.7), channel_id=1, source_target_pairs={{0,192},{64,0},{128,64},{192,128},{1,193},{65,1},{129,65},{193,129... | collective-permute-start | bytes 1437704 | tf_op jit(solution)/shard_map/ppermute | solution.py:33
  55.1 31.7 %collective-permute-start.11 = (bf16[432,1152]{1,0:T(8,128)(2,1)}, bf16[432,1152]{1,0:T(8,128)(2,1)}, u32[]{:S(2)}, u32[]{:S(2)}) collective-permute-start(bf16[432,1152]{1,0:T(8,128)(2,1)} %get-tuple-element.34.refs_3_), channel_id=1, source_target_pairs={{0,32},{32,0},{1,33},{33,1},{2,34},{34,2},{3,35},{35,3},{4,36},{36... | collective-permute-start | bytes 2985992 | tf_op jit(solution)/shard_map/ppermute | solution.py:41
  55.1 31.7 %collective-permute-start.12 = (bf16[432,1152]{1,0:T(8,128)(2,1)S(1)}, bf16[432,1152]{1,0:T(8,128)(2,1)}, u32[]{:S(2)}, u32[]{:S(2)}) collective-permute-start(bf16[432,1152]{1,0:T(8,128)(2,1)S(1)} %collective-permute-done.refs_4_), channel_id=1, source_target_pairs={{0,32},{32,0},{1,33},{33,1},{2,34},{34,2},{3,35},{35,3},{4,36},{36... | collective-permute-start | bytes 2985992 | tf_op jit(solution)/shard_map/ppermute | solution.py:41
  55.6 31.2 %collective-permute-start.13 = (bf16[432,1152]{1,0:T(8,128)(2,1)S(1)}, bf16[432,1152]{1,0:T(8,128)(2,1)}, u32[]{:S(2)}, u32[]{:S(2)}) collective-permute-start(bf16[432,1152]{1,0:T(8,128)(2,1)S(1)} %collective-permute-done.1.refs_5_), channel_id=1, source_target_pairs={{0,32},{32,0},{1,33},{33,1},{2,34},{34,2},{3,35},{35,3},{4,36},{36... | collective-permute-start | bytes 2985992 | tf_op jit(solution)/shard_map/ppermute | solution.py:41
  67.9 5.2 %collective-permute-start.8 = (bf16[8,48,128]{2,1,0:T(8,128)(2,1)S(1)}, bf16[8,48,128]{2,1,0:T(8,128)(2,1)S(1)}, u32[]{:S(2)}, u32[]{:S(2)}) collective-permute-start(bf16[8,48,128]{2,1,0:T(8,128)(2,1)S(1)} %get-tuple-element.47), channel_id=1, source_target_pairs={{0,64},{64,128},{128,192},{192,0},{1,65},{65,129},{129,193},{193,1... | collective-permute-start | bytes 294920 | tf_op jit(solution)/shard_map/ppermute | solution.py:33
  68.9 6.1 %collective-permute-start.9 = (bf16[8,48,128]{2,1,0:T(8,128)(2,1)S(1)}, bf16[8,48,128]{2,1,0:T(8,128)(2,1)S(1)}, u32[]{:S(2)}, u32[]{:S(2)}) collective-permute-start(bf16[8,48,128]{2,1,0:T(8,128)(2,1)S(1)} %get-tuple-element.48), channel_id=1, source_target_pairs={{0,128},{64,192},{128,0},{192,64},{1,129},{65,193},{129,1},{193,65... | collective-permute-start | bytes 294920 | tf_op jit(solution)/shard_map/ppermute | solution.py:33
  73.1 5.8 %collective-permute-start.10 = (bf16[8,48,128]{2,1,0:T(8,128)(2,1)S(1)}, bf16[8,48,128]{2,1,0:T(8,128)(2,1)S(1)}, u32[]{:S(2)}, u32[]{:S(2)}) collective-permute-start(bf16[8,48,128]{2,1,0:T(8,128)(2,1)S(1)} %get-tuple-element.49), channel_id=1, source_target_pairs={{0,192},{64,0},{128,64},{192,128},{1,193},{65,1},{129,65},{193,129... | collective-permute-start | bytes 294920 | tf_op jit(solution)/shard_map/ppermute | solution.py:33
  75.0 11.7 %collective-permute-start.14 = (bf16[224,1152]{1,0:T(8,128)(2,1)}, bf16[224,1152]{1,0:T(8,128)(2,1)}, u32[]{:S(2)}, u32[]{:S(2)}) collective-permute-start(bf16[224,1152]{1,0:T(8,128)(2,1)} %collective-permute-done.6.refs_6_), channel_id=1, source_target_pairs={{0,32},{32,0},{1,33},{33,1},{2,34},{34,2},{3,35},{35,3},{4,36},{36... | collective-permute-start | bytes 1548296 | tf_op jit(solution)/shard_map/ppermute | solution.py:41
  78.9 7.8 %collective-permute-start.15 = (bf16[208,1152]{1,0:T(8,128)(2,1)}, bf16[208,1152]{1,0:T(8,128)(2,1)}, u32[]{:S(2)}, u32[]{:S(2)}) collective-permute-start(bf16[208,1152]{1,0:T(8,128)(2,1)} %collective-permute-done.7.refs_7_), channel_id=1, source_target_pairs={{0,32},{32,0},{1,33},{33,1},{2,34},{34,2},{3,35},{35,3},{4,36},{36... | collective-permute-start | bytes 1437704 | tf_op jit(solution)/shard_map/ppermute | solution.py:41
  79.6 7.2 %copy-start.8 = (bf16[256,256]{1,0:T(8,128)(2,1)S(1)}, bf16[256,256]{1,0:T(8,128)(2,1)}, u32[]{:S(2)}) copy-start(bf16[256,256]{1,0:T(8,128)(2,1)} %copy-done.7) | copy-start | bytes 393220
  79.6 16.1 %all-to-all-start.2 = ((bf16[8,48,128]{2,1,0:T(8,128)(2,1)}), bf16[8,48,128]{2,1,0:T(8,128)(2,1)S(1)}, u32[]{:S(2)}, u32[]{:S(2)}) async-start(bf16[8,48,128]{2,1,0:T(8,128)(2,1)} %shard_map.123), calls=%async_computation.2 | async-start | bytes 196608 | tf_op jit(solution)/shard_map/all_to_all | solution.py:392
  (5 other events, 4.2 us)

commit v6 on v5

--- a/solution.py
+++ b/solution.py
@@ -12,13 +12,19 @@
 VMEM = pl.BlockSpec(memory_space=pltpu.VMEM)
 SMEM = pl.BlockSpec(memory_space=pltpu.SMEM)
 HBM = pl.BlockSpec(memory_space=pltpu.HBM)
-PARAMS = pltpu.CompilerParams(vmem_limit_bytes=32 << 20)
+PARAMS = pltpu.CompilerParams(vmem_limit_bytes=16 << 20)
+
+
+def cost(mib):
+    return pl.CostEstimate(flops=0, bytes_accessed=mib << 20, transcendentals=0)
+
 
 WIDTH = 1152
 MERGE = 4
 TOKENS = 20
 SLOTS = 32
 SHARD = 144
+CUT = 224
 OWN = 36
 QUARTER = 288
 SAVED_WIDE = 384
@@ -61,17 +67,24 @@
     return jnp.floor((value + 0.5) * (1.0 / by))
 
 
-def message_kernel(
-    slot_ref, saved_hbm, early, middle, late, message_ref, table_ref, stacked, saved_ref, sem
+def first_kernel(
+    slot_ref,
+    *refs,
 ):
-    fetch = pltpu.make_async_copy(saved_hbm, saved_ref, sem.at[3])
-    fetch.start()
+    inputs, outputs, (saved_ref, rows_in, sums, sem) = refs[:7], refs[7:12], refs[12:]
+    message_ref, table_ref, stacked_ref, rows_ref, shares_ref = outputs
+    fetch_saved = pltpu.make_async_copy(inputs[0], saved_ref, sem.at[0])
+    fetch_rows = [
+        pltpu.make_async_copy(ref, rows_in.at[m], sem.at[1 + m])
+        for m, ref in enumerate(inputs[1:4])
+    ]
     stack = [
-        pltpu.make_async_copy(ref, stacked.at[pl.ds(m * SHARD, SHARD)], sem.at[m])
-        for m, ref in enumerate((early, middle, late))
+        pltpu.make_async_copy(ref, stacked_ref.at[pl.ds(m * SHARD, SHARD)], sem.at[4 + m])
+        for m, ref in enumerate(inputs[4:7])
     ]
-    for copy in stack:
+    for copy in (fetch_saved, *fetch_rows, *stack):
         copy.start()
+
     source = slot_ref[...].astype(F32)
     sender = quotient(source, TOKENS)
     place = source - TOKENS * sender
@@ -80,74 +93,64 @@
     wide = matmul(both, repeat)
     sender, place = wide[0:1], wide[1:2]
     count = MERGE * SLOTS
+    row, column = iota((2 * count, count), 0), iota((2 * count, count), 1)
+    match = (sender == (row // 8).astype(F32)) & (row % MERGE == column % MERGE)
+    table_ref[:, :count] = onehot(match & (row % 8 < MERGE))
+    table_ref[:, count:] = onehot(match & (row % 8 >= MERGE))
     row, column = iota((count, count), 0), iota((count, count), 1)
     match = (sender == (row // MERGE).astype(F32)) & (row % MERGE == column % MERGE)
     tag = jnp.sum(jnp.where(match, place + 1.0, 0.0), axis=1, keepdims=True)
     tag = jnp.broadcast_to(tag, (count, SAVED_WIDE - QUARTER))
     match = onehot(match)
-    fetch.wait()
+    fetch_saved.wait()
     sorted_rows = matmul(match, saved_ref[...])
     for y in range(4):
         blocks = [sorted_rows[:, OWN * c : OWN * (c + 1)] for c in range(y, SLOTS, 4)]
         message = jnp.concatenate(blocks + [tag], axis=1).astype(BF16)
         for z in range(8):
             message_ref[4 * z + y] = message[SAVED_ROWS * z : SAVED_ROWS * (z + 1)]
-    row, column = iota((2 * count, count), 0), iota((2 * count, count), 1)
-    match = (sender == (row // 8).astype(F32)) & (row % MERGE == column % MERGE)
-    table_ref[:, :count] = onehot(match & (row % 8 < MERGE))
-    table_ref[:, count:] = onehot(match & (row % 8 >= MERGE))
-    for copy in stack:
+
+    used = MERGE * TOKENS
+    rows_ref[...] = jnp.zeros_like(rows_ref)
+    for copy in fetch_rows:
         copy.wait()
-
-
-def make_message(slot, saved, projections):
-    return pl.pallas_call(
-        message_kernel,
-        out_shape=(
-            jax.ShapeDtypeStruct((SLOTS, SAVED_ROWS, SAVED_WIDE), BF16),
-            jax.ShapeDtypeStruct((8 * SLOTS, 2 * MERGE * SLOTS), BF16),
-            jax.ShapeDtypeStruct((3 * SHARD, WIDTH), BF16),
-        ),
-        in_specs=[VMEM] + [HBM] * 4,
-        out_specs=(VMEM, VMEM, HBM),
-        scratch_shapes=[
-            pltpu.VMEM((MERGE * SLOTS, WIDTH), BF16),
-            pltpu.SemaphoreType.DMA((4,)),
-        ],
-        compiler_params=PARAMS,
-    )(slot, saved, *projections)
-
-
-def rows_kernel(early_ref, middle_ref, late_ref, rows_ref, shares_ref, sums):
-    used = MERGE * TOKENS
     for j in range(MERGE):
         at = slice(j * WIDTH, (j + 1) * WIDTH)
         to = slice(j * TOKENS, (j + 1) * TOKENS)
-        late = late_ref[:, at].astype(F32)
-        middle = late + middle_ref[:, at].astype(F32)
+        late = rows_in[2, :, at].astype(F32)
+        middle = late + rows_in[1, :, at].astype(F32)
         sums[to, 2 * WIDTH : 3 * WIDTH] = late
         sums[to, WIDTH : 2 * WIDTH] = middle
-        sums[to, :WIDTH] = middle + early_ref[:, at].astype(F32)
-    rows_ref[...] = jnp.zeros_like(rows_ref)
+        sums[to, :WIDTH] = middle + rows_in[0, :, at].astype(F32)
     rows_ref[FIRST : FIRST + used, : 3 * WIDTH] = sums[...].astype(BF16)
     early = sums[:, :WIDTH]
     main = [early[:, d * SHARD : d * SHARD + 128] for d in range(8)]
     rest = [early[:, d * SHARD + 128 : (d + 1) * SHARD] for d in range(8)]
     shares_ref[...] = jnp.concatenate(main + rest, axis=1).astype(BF16)
-
-
-def make_rows(early, middle, late):
-    return pl.pallas_call(
-        rows_kernel,
+    for copy in stack:
+        copy.wait()
+
+
+def first(slot, saved, injected, projections):
+    return pl.pallas_call(
+        first_kernel,
         out_shape=(
+            jax.ShapeDtypeStruct((SLOTS, SAVED_ROWS, SAVED_WIDE), BF16),
+            jax.ShapeDtypeStruct((8 * SLOTS, 2 * MERGE * SLOTS), BF16),
+            jax.ShapeDtypeStruct((3 * SHARD, WIDTH), BF16),
             jax.ShapeDtypeStruct((128, 2 * ROWS_HALF), BF16),
             jax.ShapeDtypeStruct((MERGE * TOKENS, WIDTH), BF16),
         ),
-        in_specs=[VMEM] * 3,
-        out_specs=(VMEM,) * 2,
-        scratch_shapes=[pltpu.VMEM((MERGE * TOKENS, 3 * WIDTH), F32)],
-        compiler_params=PARAMS,
-    )(early, middle, late)
+        in_specs=[VMEM] + [HBM] * 7,
+        out_specs=(VMEM,) * 5,
+        scratch_shapes=[
+            pltpu.VMEM((MERGE * SLOTS, WIDTH), BF16),
+            pltpu.VMEM((3, TOKENS, MERGE * WIDTH), BF16),
+            pltpu.VMEM((MERGE * TOKENS, 3 * WIDTH), F32),
+            pltpu.SemaphoreType.DMA((7,)),
+        ],
+        cost_estimate=cost(8),
+    )(slot, saved, *injected, *projections)
 
 
 def place_key(column):
@@ -178,6 +181,7 @@
         in_specs=[SMEM, VMEM, VMEM],
         out_specs=VMEM,
         compiler_params=PARAMS,
+        cost_estimate=cost(40),
     )(at, arrived, rows)
 
 
@@ -231,6 +235,7 @@
         out_specs=(VMEM,) * 2,
         scratch_shapes=[pltpu.VMEM((QUARTER, WIDTH), F32), pltpu.VMEM((2, *shape), F32)],
         compiler_params=PARAMS,
+        cost_estimate=cost(40),
     )(at, arrived, *shares)
 
 
@@ -292,41 +297,33 @@
     )(terms)
 
 
-def context_kernel(cut, at_ref, table_ref, landed_ref, *refs):
-    pieces = refs[:10]
-    early_out, middle_out, late_out, stream_out, weight, sem = refs[10:]
+def context_kernel(at_ref, table_ref, landed_ref, *refs):
+    pieces, outs, (stream_out, weight, sem) = refs[:10], refs[10:13], refs[13:]
     x, core = at_ref[0], at_ref[1]
-    copies = ([], [], [])
-
-    def put(ref, first, rows, m, inside, of_x, of_core):
-        base = pl.multiple_of((2 * of_x + of_core) * SHARD + inside, 16)
-        copies[m].append(
-            pltpu.make_async_copy(
-                ref.at[pl.ds(first, rows)], weight.at[m, pl.ds(base, rows)], sem.at[m]
-            )
-        )
-
-    for index, of_core in ((0, core), (5, 1 - core)):
-        for k, step in enumerate((0, 3, 1)):
-            for m in range(3):
-                put(pieces[index + k], m * SHARD, SHARD, m, 0, lax.rem(x + step, 4), of_core)
-        of_x = lax.rem(x + 2, 4)
-        for ref, start, stop in ((pieces[index + 3], 0, cut), (pieces[index + 4], cut, 3 * SHARD)):
-            for m in range(3):
-                low, high = max(start, m * SHARD), min(stop, (m + 1) * SHARD)
-                if low < high:
-                    put(ref, low - start, high - low, m, low - m * SHARD, of_x, of_core)
+    copies = []
     for m in range(3):
-        for copy in copies[m]:
-            copy.start()
+        for k, ref in enumerate(pieces):
+            of_core = core if k < 5 else 1 - core
+            of_x = lax.rem(x + (0, 3, 1, 2, 2)[k % 5], 4)
+            start = CUT if k % 5 == 4 else 0
+            stop = CUT if k % 5 == 3 else 3 * SHARD
+            low, high = max(start, m * SHARD), min(stop, (m + 1) * SHARD)
+            if low < high:
+                base = pl.multiple_of((2 * of_x + of_core) * SHARD + low - m * SHARD, 16)
+                from_ref = ref.at[pl.ds(low - start, high - low)]
+                to_ref = weight.at[m, pl.ds(base, high - low)]
+                copies.append((m, pltpu.make_async_copy(from_ref, to_ref, sem.at[m])))
+    for _, copy in copies:
+        copy.start()
     landed = landed_ref[...].astype(F32).reshape(8 * SLOTS, ROWS_HALF).astype(BF16)
     placed = matmul_tn(table_ref[...], landed).astype(BF16)
     half = MERGE * SLOTS
     placed = jnp.concatenate([placed[:half], placed[half:, : 3 * WIDTH - ROWS_HALF]], axis=1)
     stream_out[...] = placed[:, :WIDTH]
-    for m, out in enumerate((early_out, middle_out, late_out)):
-        for copy in copies[m]:
-            copy.wait()
+    for m, out in enumerate(outs):
+        for of_m, copy in copies:
+            if of_m == m:
+                copy.wait()
         out[...] = lax.dot_general(
             placed[:, m * WIDTH : (m + 1) * WIDTH],
             weight[m],
@@ -335,11 +332,10 @@
         ).astype(BF16)
 
 
-def contexts(at, table, landed, pieces, cut):
-    rows = MERGE * SLOTS
-    out = jax.ShapeDtypeStruct((rows, WIDTH), BF16)
-    return pl.pallas_call(
-        lambda *refs: context_kernel(cut, *refs),
+def contexts(at, table, landed, pieces):
+    out = jax.ShapeDtypeStruct((MERGE * SLOTS, WIDTH), BF16)
+    return pl.pallas_call(
+        context_kernel,
         out_shape=(out,) * 4,
         in_specs=[SMEM, VMEM, VMEM] + [HBM] * 10,
         out_specs=(VMEM,) * 4,
@@ -347,10 +343,8 @@
             pltpu.VMEM((3, WIDTH, WIDTH), BF16),
             pltpu.SemaphoreType.DMA((3,)),
         ],
-        compiler_params=PARAMS,
-        cost_estimate=pl.CostEstimate(
-            flops=6 * rows * WIDTH * WIDTH, bytes_accessed=6 * WIDTH * WIDTH, transcendentals=0
-        ),
+        compiler_params=pltpu.CompilerParams(vmem_limit_bytes=58 << 20),
+        cost_estimate=cost(24),
     )(at, table, landed, *pieces)
 
 
@@ -366,34 +360,36 @@
 ):
     at = jnp.stack([lax.axis_index(name) for name in ("x", "core", "y")]).astype(jnp.int32)
 
-    projections = (projection_early, projection_middle, projection_late)
-    message, table, stacked = make_message(slot_source, saved_early[0], projections)
+    message, table, stacked, rows, share = first(
+        slot_source,
+        saved_early[0],
+        (injected_early[0], injected_middle[0], injected_late[0]),
+        (projection_early, projection_middle, projection_late),
+    )
     arrived = lax.all_to_all(message, CTX, 0, 0, tiled=True)
 
-    cut = 224
     from_left, from_right = over_x(stacked, 1), over_x(stacked, 3)
-    rows, share = make_rows(injected_early[0], injected_middle[0], injected_late[0])
     shares = [share] + [over_y(share, step) for step in (1, 2, 3)]
-    arrived, from_left, from_right, shares = lax.optimization_barrier(
-        (arrived, from_left, from_right, shares)
+    once_more = from_left[:CUT], from_right[CUT:]
+    arrived, shares, from_left, from_right, once_more = lax.optimization_barrier(
+        (arrived, shares, from_left, from_right, once_more)
     )
 
     landed = lax.all_to_all(pack(at, arrived, rows), CTX, 0, 0, tiled=True)
 
-    far_left, far_right = over_x(from_left[:cut], 1), over_x(from_right[cut:], 3)
-
+    far = over_x(once_more[0], 1), over_x(once_more[1], 3)
     keep, give = gradient(at, arrived, shares)
-    given = over_core(give)
-    given, far_left, far_right = lax.optimization_barrier((given, far_left, far_right))
-    mine, *parts = sum_core(keep, given)
+    mine, *parts = sum_core(keep, over_core(give))
     parts = [over_x(part, step) for step, part in zip((1, 2, 3), parts)]
+    parts, far = lax.optimization_barrier((parts, far))
     terms = sum_x(mine, parts)
+
+    pieces = (stacked, from_left, from_right, *far)
+    terms, pieces = lax.optimization_barrier((terms, pieces))
+    pieces = pieces + tuple(over_core(piece) for piece in pieces)
     terms, landed = lax.optimization_barrier((terms, landed))
     weights = add_up(lax.all_to_all(terms, "z", 0, 0, tiled=True))
-
-    pieces = (stacked, from_left, from_right, far_left, far_right)
-    pieces = pieces + tuple(over_core(piece) for piece in pieces)
-    context_early, context_middle, context_late, stream = contexts(at, table, landed, pieces, cut)
+    context_early, context_middle, context_late, stream = contexts(at, table, landed, pieces)
     return context_early[None], context_middle[None], context_late[None], stream[None], weights
 
 

time: 98.2 us -> 88 us (0.90); the launches traced: 96.6 us -> 87.5 us
  waiting for transfers between devices: 34.7 us -> 25.4 us
  local copies, waits for them, and re-layouts: 7.13 us -> 3.56 us
  starting transfers between devices: 38.4 us -> 40.7 us
  Pallas kernels: 15.5 us -> 17 us
    ppermute x3, waiting for transfers between devices: 11.1 us -> 3.6 us  [over_y(): return lax.ppermute(array, 'y', [(i, (i + step) % 4) for i in range(4)])]
    unnamed x20 -> x18, local copies, waits for them, and re-layouts: 7.05 us -> 0.78 us
    slice x2, local copies, waits for them, and re-layouts: 0.08 us -> 2.78 us  [local(): once_more = (from_left[:CUT], from_right[CUT:])]
    pallas_call x3 -> x2, Pallas kernels: 8.75 us -> 10.7 us  [the longest x1 6.77 us: contexts(): pl.pallas_call(context_kernel, out_shape=(out,) * 4, in_specs=[SMEM, VMEM...]
    all_to_all x1, starting transfers between devices: 6.3 us -> 7.91 us  [local(): landed = lax.all_to_all(pack(at, arrived, rows), CTX, 0, 0, tiled=True)]
    all_to_all x1, waiting for transfers between devices: 2.97 us -> 1.42 us  [local(): weights = add_up(lax.all_to_all(terms, 'z', 0, 0, tiled=True))]
    ppermute x7, waiting for transfers between devices: 20.6 us -> 19.4 us  [over_x(): return lax.ppermute(array, 'x', [(i, (i + step) % 4) for i in range(4)])]
  transfers between devices with their start and end apart: 19 -> 19, of which waited for: 8 -> 9; matrix products, arithmetic and copies ran while one was open for 0% -> 3% of each run, Pallas kernels for 11% -> 11%
where the time goes in v6:
time: 88 us; the launch traced here: 87.5 us
  starting transfers between devices  40.7 us (46%)
  waiting for transfers between devices  25.4 us (29%)
  Pallas kernels  17 us (19%)
  local copies, waits for them, and re-layouts  3.56 us (4%)
    ppermute x7, waiting for transfers between devices, over_x(): return lax.ppermute(array, 'x', [(i, (i + step) % 4) for i in range(4)])  19.4 us
    all_to_all x1, starting transfers between devices, local(): arrived = lax.all_to_all(message, CTX, 0, 0, tiled=True)  11.6 us
    ppermute x7, starting transfers between devices, over_x(): return lax.ppermute(array, 'x', [(i, (i + step) % 4) for i in range(4)])  8.7 us
    all_to_all x1, starting transfers between devices, local(): landed = lax.all_to_all(pack(at, arrived, rows), CTX, 0, 0, tiled=True)  7.91 us
    pallas_call x1, Pallas kernels, contexts(): pl.pallas_call(context_kernel, out_shape=(out,) * 4, in_specs=[SMEM, VMEM...  6.77 us
    all_to_all x1, starting transfers between devices, local(): weights = add_up(lax.all_to_all(terms, 'z', 0, 0, tiled=True))  6.55 us
    ppermute x3, starting transfers between devices, over_y(): return lax.ppermute(array, 'y', [(i, (i + step) % 4) for i in range(4)])  4.79 us
    pallas_call x1, Pallas kernels, first(): pl.pallas_call(first_kernel, out_shape=(jax.ShapeDtypeStruct((SLOTS, SAVE...  3.97 us
  transfers between devices with their start and end apart: 19, of which 9 were waited for; matrix products, arithmetic and copies ran while one was open for 3% of the time, Pallas kernels for 11%

profile of v6, /device:TPU:6, one launch (start us, length us, event | category | flops | bytes accessed | tf_op | source)
XLA Modules:
  0.0 87.5 jit_solution(12608202785841429661)
XLA Ops:
  0.6 4.0 %shard_map.119 = (bf16[32,16,384]{2,1,0:T(8,128)(2,1)}, bf16[256,256]{1,0:T(8,128)(2,1)}, bf16[432,1152]{1,0:T(8,128)(2,1)}, bf16[128,3584]{1,0:T(8,128)(2,1)}, bf16[80,1152]{1,0:T(8,128)(2,1)}) custom-call(s32[1,32]{1,0:T(1,128)} %slot_ref.1, bf16[128,1152]{1,0:T(8,128)(2,1)} %bitcast.11, bf16[20,4608]{1,0:T(8,128)(2,1)} %bitcast.12, ...), custom_call_target="tpu_custom_call" | custom-call | bytes 8388608 | tf_op jit(solution)/shard_map/pallas_call | solution.py:135
  4.6 0.9 %collective-permute-start.4 = (bf16[432,1152]{1,0:T(8,128)(2,1)}, bf16[432,1152]{1,0:T(8,128)(2,1)}, u32[]{:S(2)}, u32[]{:S(2)}) collective-permute-start(bf16[432,1152]{1,0:T(8,128)(2,1)} %get-tuple-element.69.refs_0_), channel_id=1, source_target_pairs={{0,192},{64,0},{128,64},{192,128},{1,193},{65,1},{129,65},{193,129... | collective-permute-start | bytes 2985992 | tf_op jit(solution)/shard_map/ppermute | solution.py:39
  5.5 2.4 %collective-permute-start.3 = (bf16[432,1152]{1,0:T(8,128)(2,1)}, bf16[432,1152]{1,0:T(8,128)(2,1)S(1)}, u32[]{:S(2)}, u32[]{:S(2)}) collective-permute-start(bf16[432,1152]{1,0:T(8,128)(2,1)} %get-tuple-element.69.refs_0_), channel_id=1, source_target_pairs={{0,64},{64,128},{128,192},{192,0},{1,65},{65,129},{129,193},{193,1... | collective-permute-start | bytes 2985992 | tf_op jit(solution)/shard_map/ppermute | solution.py:39
  7.9 11.6 %all-to-all-start = ((bf16[32,16,384]{2,1,0:T(8,128)(2,1)}), bf16[32,16,384]{2,1,0:T(8,128)(2,1)S(1)}, u32[]{:S(2)}, u32[]{:S(2)}) async-start(bf16[32,16,384]{2,1,0:T(8,128)(2,1)} %get-tuple-element.43), calls=%async_computation | async-start | bytes 786432 | tf_op jit(solution)/shard_map/all_to_all | solution.py:369
  19.6 3.1 %collective-permute-start.2 = (bf16[80,1152]{1,0:T(8,128)(2,1)S(1)}, bf16[80,1152]{1,0:T(8,128)(2,1)S(1)}, u32[]{:S(2)}, u32[]{:S(2)}) collective-permute-start(bf16[80,1152]{1,0:T(8,128)(2,1)S(1)} %copy-done.1), channel_id=1, source_target_pairs={{0,3},{1,0},{2,1},{3,2},{4,7},{5,4},{6,5},{7,6},{8,11},{9,8},{10,9... | collective-permute-start | bytes 552968 | tf_op jit(solution)/shard_map/ppermute | solution.py:43
  22.6 0.9 collective-permute-start.1
  23.5 0.9 collective-permute-start
  24.4 5.5 %collective-permute-done.4.refs_2_ = bf16[432,1152]{1,0:T(8,128)(2,1)} collective-permute-done((bf16[432,1152]{1,0:T(8,128)(2,1)}, bf16[432,1152]{1,0:T(8,128)(2,1)}, u32[]{:S(2)}, u32[]{:S(2)}) %collective-permute-start.4) | collective-permute-done | bytes 995360 | tf_op jit(solution)/shard_map/ppermute | solution.py:39
  30.0 1.9 %slice.9 = bf16[208,1152]{1,0:T(8,128)(2,1)} slice(bf16[432,1152]{1,0:T(8,128)(2,1)} %collective-permute-done.4.refs_2_), slice={[224:432], [0:1152]} | slice | bytes 958464 | tf_op jit(solution)/shard_map/slice | solution.py:373
  31.9 0.9 %slice.8 = bf16[224,1152]{1,0:T(8,128)(2,1)} slice(bf16[432,1152]{1,0:T(8,128)(2,1)S(1)} %collective-permute-done.3.refs_1_), slice={[0:224], [0:1152]} | slice | bytes 1032192 | tf_op jit(solution)/shard_map/slice | solution.py:373
  33.9 2.5 %collective-permute-done.refs_1_ = bf16[80,1152]{1,0:T(8,128)(2,1)S(1)} collective-permute-done((bf16[80,1152]{1,0:T(8,128)(2,1)S(1)}, bf16[80,1152]{1,0:T(8,128)(2,1)S(1)}, u32[]{:S(2)}, u32[]{:S(2)}) %collective-permute-start) | collective-permute-done | bytes 184352 | tf_op jit(solution)/shard_map/ppermute | solution.py:43
  36.4 2.4 %shard_map.123 = bf16[32,8,1792]{2,1,0:T(8,128)(2,1)} custom-call(s32[3]{0:T(128)S(1)} %pad_add_fusion.at_ref, bf16[32,16,384]{2,1,0:T(8,128)(2,1)S(1)} %all-to-all-done.arrived_ref, bf16[128,3584]{1,0:T(8,128)(2,1)S(1)} %copy-done), custom_call_target="tpu_custom_call" | custom-call | bytes 41943040 | tf_op jit(solution)/shard_map/pallas_call | solution.py:178
  38.8 7.9 %all-to-all-start.1 = ((bf16[32,8,1792]{2,1,0:T(8,128)(2,1)}), bf16[32,8,1792]{2,1,0:T(8,128)(2,1)S(1)}, u32[]{:S(2)}, u32[]{:S(2)}) async-start(bf16[32,8,1792]{2,1,0:T(8,128)(2,1)} %shard_map.123), calls=%async_computation.1 | async-start | bytes 1835008 | tf_op jit(solution)/shard_map/all_to_all | solution.py:378
  46.7 1.0 %collective-permute-start.9 = (bf16[224,1152]{1,0:T(8,128)(2,1)}, bf16[224,1152]{1,0:T(8,128)(2,1)S(1)}, u32[]{:S(2)}, u32[]{:S(2)}) collective-permute-start(bf16[224,1152]{1,0:T(8,128)(2,1)} %slice.8), channel_id=1, source_target_pairs={{0,64},{64,128},{128,192},{192,0},{1,65},{65,129},{129,193},{193,1... | collective-permute-start | bytes 1548296 | tf_op jit(solution)/shard_map/ppermute | solution.py:39
  47.8 2.2 %shard_map.120 = (f32[4,8,48,128]{3,2,1,0:T(8,128)S(1)}, bf16[4,8,48,128]{3,2,1,0:T(8,128)(2,1)S(1)}) custom-call(s32[3]{0:T(128)S(1)} %pad_add_fusion.at_ref, bf16[32,16,384]{2,1,0:T(8,128)(2,1)S(1)} %all-to-all-done.arrived_ref, bf16[80,1152]{1,0:T(8,128)(2,1)S(1)} %copy-done.1, bf16[80,1152]{1,0:T(8,128)(2,1)S(1)} %collective-permute-done.refs_1_, ...), custom_call_target="tpu_custom_call" | custom-call | bytes 41943040 | tf_op jit(solution)/shard_map/pallas_call | solution.py:231
  50.1 1.1 %collective-permute-start.10 = (bf16[208,1152]{1,0:T(8,128)(2,1)S(1)}, bf16[208,1152]{1,0:T(8,128)(2,1)}, u32[]{:S(2)}, u32[]{:S(2)}) collective-permute-start(bf16[208,1152]{1,0:T(8,128)(2,1)S(1)} %copy-done.8), channel_id=1, source_target_pairs={{0,192},{64,0},{128,64},{192,128},{1,193},{65,1},{129,65},{193,129... | collective-permute-start | bytes 1437704 | tf_op jit(solution)/shard_map/ppermute | solution.py:39
  51.9 1.7 %collective-permute-start.6 = (bf16[8,48,128]{2,1,0:T(8,128)(2,1)S(1)}, bf16[8,48,128]{2,1,0:T(8,128)(2,1)S(1)}, u32[]{:S(2)}, u32[]{:S(2)}) collective-permute-start(bf16[8,48,128]{2,1,0:T(8,128)(2,1)S(1)} %get-tuple-element.54), channel_id=1, source_target_pairs={{0,64},{64,128},{128,192},{192,0},{1,65},{65,129},{129,193},{193,1... | collective-permute-start | bytes 294920 | tf_op jit(solution)/shard_map/ppermute | solution.py:39
  53.6 1.5 %collective-permute-start.7 = (bf16[8,48,128]{2,1,0:T(8,128)(2,1)S(1)}, bf16[8,48,128]{2,1,0:T(8,128)(2,1)S(1)}, u32[]{:S(2)}, u32[]{:S(2)}) collective-permute-start(bf16[8,48,128]{2,1,0:T(8,128)(2,1)S(1)} %get-tuple-element.55), channel_id=1, source_target_pairs={{0,128},{64,192},{128,0},{192,64},{1,129},{65,193},{129,1},{193,65... | collective-permute-start | bytes 294920 | tf_op jit(solution)/shard_map/ppermute | solution.py:39
  55.1 12.3 %collective-permute-done.10.refs_4_ = bf16[208,1152]{1,0:T(8,128)(2,1)} collective-permute-done((bf16[208,1152]{1,0:T(8,128)(2,1)S(1)}, bf16[208,1152]{1,0:T(8,128)(2,1)}, u32[]{:S(2)}, u32[]{:S(2)}) %collective-permute-start.10) | collective-permute-done | bytes 479264 | tf_op jit(solution)/shard_map/ppermute | solution.py:39
  67.4 1.5 %collective-permute-done.8.third = bf16[8,48,128]{2,1,0:T(8,128)(2,1)S(1)} collective-permute-done((bf16[8,48,128]{2,1,0:T(8,128)(2,1)S(1)}, bf16[8,48,128]{2,1,0:T(8,128)(2,1)S(1)}, u32[]{:S(2)}, u32[]{:S(2)}) %collective-permute-start.8) | collective-permute-done | bytes 98336 | tf_op jit(solution)/shard_map/ppermute | solution.py:39
  71.1 6.5 %all-to-all-start.2 = ((bf16[8,48,128]{2,1,0:T(8,128)(2,1)}), bf16[8,48,128]{2,1,0:T(8,128)(2,1)S(1)}, u32[]{:S(2)}, u32[]{:S(2)}) async-start(bf16[8,48,128]{2,1,0:T(8,128)(2,1)} %shard_map.122), calls=%async_computation.2 | async-start | bytes 196608 | tf_op jit(solution)/shard_map/all_to_all | solution.py:391
  78.5 6.8 %shard_map.124 = (bf16[128,1152]{1,0:T(8,128)(2,1)}, bf16[128,1152]{1,0:T(8,128)(2,1)}, bf16[128,1152]{1,0:T(8,128)(2,1)}, bf16[128,1152]{1,0:T(8,128)(2,1)}) custom-call(s32[3]{0:T(128)} %copy-done.2, bf16[256,256]{1,0:T(8,128)(2,1)} %get-tuple-element.42.table_ref, bf16[32,8,1792]{2,1,0:T(8,128)(2,1)} %copy-done.3, ...), custom_call_target="tpu_custom_call" | custom-call | bytes 25165824 | tf_op jit(solution)/shard_map/pallas_call | solution.py:337
  85.3 1.4 %all-to-all-done.2.terms_ref = bf16[8,48,128]{2,1,0:T(8,128)(2,1)S(1)} async-done(((bf16[8,48,128]{2,1,0:T(8,128)(2,1)}), bf16[8,48,128]{2,1,0:T(8,128)(2,1)S(1)}, u32[]{:S(2)}, u32[]{:S(2)}) %all-to-all-start.2) | async-done | bytes 98336 | tf_op jit(solution)/shard_map/all_to_all | solution.py:391
  86.7 0.8 shard_map.125
  (42 shorter events, 4.9 us)
Async XLA Ops:
  4.6 25.4 %collective-permute-start.4 = (bf16[432,1152]{1,0:T(8,128)(2,1)}, bf16[432,1152]{1,0:T(8,128)(2,1)}, u32[]{:S(2)}, u32[]{:S(2)}) collective-permute-start(bf16[432,1152]{1,0:T(8,128)(2,1)} %get-tuple-element.69.refs_0_), channel_id=1, source_target_pairs={{0,192},{64,0},{128,64},{192,128},{1,193},{65,1},{129,65},{193,129... | collective-permute-start | bytes 2985992 | tf_op jit(solution)/shard_map/ppermute | solution.py:39
  5.5 26.3 %collective-permute-start.3 = (bf16[432,1152]{1,0:T(8,128)(2,1)}, bf16[432,1152]{1,0:T(8,128)(2,1)S(1)}, u32[]{:S(2)}, u32[]{:S(2)}) collective-permute-start(bf16[432,1152]{1,0:T(8,128)(2,1)} %get-tuple-element.69.refs_0_), channel_id=1, source_target_pairs={{0,64},{64,128},{128,192},{192,0},{1,65},{65,129},{129,193},{193,1... | collective-permute-start | bytes 2985992 | tf_op jit(solution)/shard_map/ppermute | solution.py:39
  7.9 11.6 %copy-start.1 = (bf16[80,1152]{1,0:T(8,128)(2,1)S(1)}, bf16[80,1152]{1,0:T(8,128)(2,1)}, u32[]{:S(2)}) copy-start(bf16[80,1152]{1,0:T(8,128)(2,1)} %get-tuple-element.47.refs_0_) | copy-start | bytes 552964
  7.9 28.4 %all-to-all-start = ((bf16[32,16,384]{2,1,0:T(8,128)(2,1)}), bf16[32,16,384]{2,1,0:T(8,128)(2,1)S(1)}, u32[]{:S(2)}, u32[]{:S(2)}) async-start(bf16[32,16,384]{2,1,0:T(8,128)(2,1)} %get-tuple-element.43), calls=%async_computation | async-start | bytes 786432 | tf_op jit(solution)/shard_map/all_to_all | solution.py:369
  19.6 13.5 %collective-permute-start.2 = (bf16[80,1152]{1,0:T(8,128)(2,1)S(1)}, bf16[80,1152]{1,0:T(8,128)(2,1)S(1)}, u32[]{:S(2)}, u32[]{:S(2)}) collective-permute-start(bf16[80,1152]{1,0:T(8,128)(2,1)S(1)} %copy-done.1), channel_id=1, source_target_pairs={{0,3},{1,0},{2,1},{3,2},{4,7},{5,4},{6,5},{7,6},{8,11},{9,8},{10,9... | collective-permute-start | bytes 552968 | tf_op jit(solution)/shard_map/ppermute | solution.py:43
  22.6 11.3 %collective-permute-start.1 = (bf16[80,1152]{1,0:T(8,128)(2,1)S(1)}, bf16[80,1152]{1,0:T(8,128)(2,1)S(1)}, u32[]{:S(2)}, u32[]{:S(2)}) collective-permute-start(bf16[80,1152]{1,0:T(8,128)(2,1)S(1)} %copy-done.1), channel_id=1, source_target_pairs={{0,2},{1,3},{2,0},{3,1},{4,6},{5,7},{6,4},{7,5},{8,10},{9,11},{10,... | collective-permute-start | bytes 552968 | tf_op jit(solution)/shard_map/ppermute | solution.py:43
  23.5 12.9 %collective-permute-start = (bf16[80,1152]{1,0:T(8,128)(2,1)S(1)}, bf16[80,1152]{1,0:T(8,128)(2,1)S(1)}, u32[]{:S(2)}, u32[]{:S(2)}) collective-permute-start(bf16[80,1152]{1,0:T(8,128)(2,1)S(1)} %copy-done.1), channel_id=1, source_target_pairs={{0,1},{1,2},{2,3},{3,0},{4,5},{5,6},{6,7},{7,4},{8,9},{9,10},{10,1... | collective-permute-start | bytes 552968 | tf_op jit(solution)/shard_map/ppermute | solution.py:43
  24.4 23.3 %copy-start.2 = (s32[3]{0:T(128)}, s32[3]{0:T(128)S(1)}, u32[]{:S(2)}) copy-start(s32[3]{0:T(128)S(1)} %pad_add_fusion.at_ref) | copy-start | bytes 40
  24.4 11.9 %copy-start = (bf16[128,3584]{1,0:T(8,128)(2,1)S(1)}, bf16[128,3584]{1,0:T(8,128)(2,1)}, u32[]{:S(2)}) copy-start(bf16[128,3584]{1,0:T(8,128)(2,1)} %get-tuple-element.67.rows_ref) | copy-start | bytes 2752516
  38.8 32.3 %all-to-all-start.1 = ((bf16[32,8,1792]{2,1,0:T(8,128)(2,1)}), bf16[32,8,1792]{2,1,0:T(8,128)(2,1)S(1)}, u32[]{:S(2)}, u32[]{:S(2)}) async-start(bf16[32,8,1792]{2,1,0:T(8,128)(2,1)} %shard_map.123), calls=%async_computation.1 | async-start | bytes 1835008 | tf_op jit(solution)/shard_map/all_to_all | solution.py:378
  46.7 22.2 %collective-permute-start.9 = (bf16[224,1152]{1,0:T(8,128)(2,1)}, bf16[224,1152]{1,0:T(8,128)(2,1)S(1)}, u32[]{:S(2)}, u32[]{:S(2)}) collective-permute-start(bf16[224,1152]{1,0:T(8,128)(2,1)} %slice.8), channel_id=1, source_target_pairs={{0,64},{64,128},{128,192},{192,0},{1,65},{65,129},{129,193},{193,1... | collective-permute-start | bytes 1548296 | tf_op jit(solution)/shard_map/ppermute | solution.py:39
  50.0 19.7 %copy-start.5 = (bf16[432,1152]{1,0:T(8,128)(2,1)S(1)}, bf16[432,1152]{1,0:T(8,128)(2,1)}, u32[]{:S(2)}) copy-start(bf16[432,1152]{1,0:T(8,128)(2,1)} %copy-done.4) | copy-start | bytes 2985988
  50.0 1.8 %collective-permute-start.5 = (bf16[4,8,48,128]{3,2,1,0:T(8,128)(2,1)S(1)}, bf16[4,8,48,128]{3,2,1,0:T(8,128)(2,1)S(1)}, u32[]{:S(2)}, u32[]{:S(2)}) collective-permute-start(bf16[4,8,48,128]{3,2,1,0:T(8,128)(2,1)S(1)} %get-tuple-element.52), channel_id=1, source_target_pairs={{0,32},{32,0},{1,33},{33,1},{2,34},{34,2},{3,35},{35,3},{4,36},{36... | collective-permute-start | bytes 1179656 | tf_op jit(solution)/shard_map/ppermute | solution.py:47
  50.1 17.3 %collective-permute-start.10 = (bf16[208,1152]{1,0:T(8,128)(2,1)S(1)}, bf16[208,1152]{1,0:T(8,128)(2,1)}, u32[]{:S(2)}, u32[]{:S(2)}) collective-permute-start(bf16[208,1152]{1,0:T(8,128)(2,1)S(1)} %copy-done.8), channel_id=1, source_target_pairs={{0,192},{64,0},{128,64},{192,128},{1,193},{65,1},{129,65},{193,129... | collective-permute-start | bytes 1437704 | tf_op jit(solution)/shard_map/ppermute | solution.py:39
  51.9 15.5 %collective-permute-start.6 = (bf16[8,48,128]{2,1,0:T(8,128)(2,1)S(1)}, bf16[8,48,128]{2,1,0:T(8,128)(2,1)S(1)}, u32[]{:S(2)}, u32[]{:S(2)}) collective-permute-start(bf16[8,48,128]{2,1,0:T(8,128)(2,1)S(1)} %get-tuple-element.54), channel_id=1, source_target_pairs={{0,64},{64,128},{128,192},{192,0},{1,65},{65,129},{129,193},{193,1... | collective-permute-start | bytes 294920 | tf_op jit(solution)/shard_map/ppermute | solution.py:39
  53.6 13.8 %collective-permute-start.7 = (bf16[8,48,128]{2,1,0:T(8,128)(2,1)S(1)}, bf16[8,48,128]{2,1,0:T(8,128)(2,1)S(1)}, u32[]{:S(2)}, u32[]{:S(2)}) collective-permute-start(bf16[8,48,128]{2,1,0:T(8,128)(2,1)S(1)} %get-tuple-element.55), channel_id=1, source_target_pairs={{0,128},{64,192},{128,0},{192,64},{1,129},{65,193},{129,1},{193,65... | collective-permute-start | bytes 294920 | tf_op jit(solution)/shard_map/ppermute | solution.py:39
  55.1 13.8 %collective-permute-start.8 = (bf16[8,48,128]{2,1,0:T(8,128)(2,1)S(1)}, bf16[8,48,128]{2,1,0:T(8,128)(2,1)S(1)}, u32[]{:S(2)}, u32[]{:S(2)}) collective-permute-start(bf16[8,48,128]{2,1,0:T(8,128)(2,1)S(1)} %get-tuple-element.56), channel_id=1, source_target_pairs={{0,192},{64,0},{128,64},{192,128},{1,193},{65,1},{129,65},{193,129... | collective-permute-start | bytes 294920 | tf_op jit(solution)/shard_map/ppermute | solution.py:39
  68.9 8.8 %copy-start.6 = (bf16[224,1152]{1,0:T(8,128)(2,1)}, bf16[224,1152]{1,0:T(8,128)(2,1)S(1)}, u32[]{:S(2)}) copy-start(bf16[224,1152]{1,0:T(8,128)(2,1)S(1)} %collective-permute-done.9.refs_3_) | copy-start | bytes 1548292
  69.6 8.1 %collective-permute-start.11 = (bf16[432,1152]{1,0:T(8,128)(2,1)}, bf16[432,1152]{1,0:T(8,128)(2,1)}, u32[]{:S(2)}, u32[]{:S(2)}) collective-permute-start(bf16[432,1152]{1,0:T(8,128)(2,1)} %get-tuple-element.69.refs_0_), channel_id=1, source_target_pairs={{0,32},{32,0},{1,33},{33,1},{2,34},{34,2},{3,35},{35,3},{4,36},{36... | collective-permute-start | bytes 2985992 | tf_op jit(solution)/shard_map/ppermute | solution.py:47
  69.6 8.1 %collective-permute-start.12 = (bf16[432,1152]{1,0:T(8,128)(2,1)S(1)}, bf16[432,1152]{1,0:T(8,128)(2,1)}, u32[]{:S(2)}, u32[]{:S(2)}) collective-permute-start(bf16[432,1152]{1,0:T(8,128)(2,1)S(1)} %copy-done.5), channel_id=1, source_target_pairs={{0,32},{32,0},{1,33},{33,1},{2,34},{34,2},{3,35},{35,3},{4,36},{36... | collective-permute-start | bytes 2985992 | tf_op jit(solution)/shard_map/ppermute | solution.py:47
  70.2 7.6 %collective-permute-start.13 = (bf16[432,1152]{1,0:T(8,128)(2,1)}, bf16[432,1152]{1,0:T(8,128)(2,1)}, u32[]{:S(2)}, u32[]{:S(2)}) collective-permute-start(bf16[432,1152]{1,0:T(8,128)(2,1)} %collective-permute-done.4.refs_2_), channel_id=1, source_target_pairs={{0,32},{32,0},{1,33},{33,1},{2,34},{34,2},{3,35},{35,3},{4,36},{36... | collective-permute-start | bytes 2985992 | tf_op jit(solution)/shard_map/ppermute | solution.py:47
  70.2 7.5 %collective-permute-start.14 = (bf16[224,1152]{1,0:T(8,128)(2,1)S(1)}, bf16[224,1152]{1,0:T(8,128)(2,1)S(1)}, u32[]{:S(2)}, u32[]{:S(2)}) collective-permute-start(bf16[224,1152]{1,0:T(8,128)(2,1)S(1)} %collective-permute-done.9.refs_3_), channel_id=1, source_target_pairs={{0,32},{32,0},{1,33},{33,1},{2,34},{34,2},{3,35},{35,3},{4,36},{36... | collective-permute-start | bytes 1548296 | tf_op jit(solution)/shard_map/ppermute | solution.py:47
  70.7 7.0 %collective-permute-start.15 = (bf16[208,1152]{1,0:T(8,128)(2,1)}, bf16[208,1152]{1,0:T(8,128)(2,1)}, u32[]{:S(2)}, u32[]{:S(2)}) collective-permute-start(bf16[208,1152]{1,0:T(8,128)(2,1)} %collective-permute-done.10.refs_4_), channel_id=1, source_target_pairs={{0,32},{32,0},{1,33},{33,1},{2,34},{34,2},{3,35},{35,3},{4,36},{36... | collective-permute-start | bytes 1437704 | tf_op jit(solution)/shard_map/ppermute | solution.py:47
  71.1 15.6 %all-to-all-start.2 = ((bf16[8,48,128]{2,1,0:T(8,128)(2,1)}), bf16[8,48,128]{2,1,0:T(8,128)(2,1)S(1)}, u32[]{:S(2)}, u32[]{:S(2)}) async-start(bf16[8,48,128]{2,1,0:T(8,128)(2,1)} %shard_map.122), calls=%async_computation.2 | async-start | bytes 196608 | tf_op jit(solution)/shard_map/all_to_all | solution.py:391
  (4 other events, 17.8 us)

commit v7 on v6

--- a/solution.py
+++ b/solution.py
@@ -67,23 +67,12 @@
     return jnp.floor((value + 0.5) * (1.0 / by))
 
 
-def first_kernel(
-    slot_ref,
-    *refs,
-):
-    inputs, outputs, (saved_ref, rows_in, sums, sem) = refs[:7], refs[7:12], refs[12:]
-    message_ref, table_ref, stacked_ref, rows_ref, shares_ref = outputs
-    fetch_saved = pltpu.make_async_copy(inputs[0], saved_ref, sem.at[0])
-    fetch_rows = [
-        pltpu.make_async_copy(ref, rows_in.at[m], sem.at[1 + m])
-        for m, ref in enumerate(inputs[1:4])
-    ]
-    stack = [
-        pltpu.make_async_copy(ref, stacked_ref.at[pl.ds(m * SHARD, SHARD)], sem.at[4 + m])
-        for m, ref in enumerate(inputs[4:7])
-    ]
-    for copy in (fetch_saved, *fetch_rows, *stack):
-        copy.start()
+def first_kernel(slot_hbm, saved_hbm, message_ref, table_ref, slot_ref, saved_ref, sem):
+    fetch_slot = pltpu.make_async_copy(slot_hbm, slot_ref, sem.at[0])
+    fetch_saved = pltpu.make_async_copy(saved_hbm, saved_ref, sem.at[1])
+    fetch_slot.start()
+    fetch_saved.start()
+    fetch_slot.wait()
 
     source = slot_ref[...].astype(F32)
     sender = quotient(source, TOKENS)
@@ -110,47 +99,80 @@
         for z in range(8):
             message_ref[4 * z + y] = message[SAVED_ROWS * z : SAVED_ROWS * (z + 1)]
 
-    used = MERGE * TOKENS
-    rows_ref[...] = jnp.zeros_like(rows_ref)
-    for copy in fetch_rows:
-        copy.wait()
-    for j in range(MERGE):
-        at = slice(j * WIDTH, (j + 1) * WIDTH)
-        to = slice(j * TOKENS, (j + 1) * TOKENS)
-        late = rows_in[2, :, at].astype(F32)
-        middle = late + rows_in[1, :, at].astype(F32)
-        sums[to, 2 * WIDTH : 3 * WIDTH] = late
-        sums[to, WIDTH : 2 * WIDTH] = middle
-        sums[to, :WIDTH] = middle + rows_in[0, :, at].astype(F32)
-    rows_ref[FIRST : FIRST + used, : 3 * WIDTH] = sums[...].astype(BF16)
-    early = sums[:, :WIDTH]
-    main = [early[:, d * SHARD : d * SHARD + 128] for d in range(8)]
-    rest = [early[:, d * SHARD + 128 : (d + 1) * SHARD] for d in range(8)]
-    shares_ref[...] = jnp.concatenate(main + rest, axis=1).astype(BF16)
-    for copy in stack:
-        copy.wait()
-
-
-def first(slot, saved, injected, projections):
+
+def first(slot, saved):
     return pl.pallas_call(
         first_kernel,
         out_shape=(
             jax.ShapeDtypeStruct((SLOTS, SAVED_ROWS, SAVED_WIDE), BF16),
             jax.ShapeDtypeStruct((8 * SLOTS, 2 * MERGE * SLOTS), BF16),
-            jax.ShapeDtypeStruct((3 * SHARD, WIDTH), BF16),
-            jax.ShapeDtypeStruct((128, 2 * ROWS_HALF), BF16),
-            jax.ShapeDtypeStruct((MERGE * TOKENS, WIDTH), BF16),
         ),
-        in_specs=[VMEM] + [HBM] * 7,
-        out_specs=(VMEM,) * 5,
+        in_specs=[HBM] * 2,
+        out_specs=(VMEM,) * 2,
         scratch_shapes=[
-            pltpu.VMEM((MERGE * SLOTS, WIDTH), BF16),
-            pltpu.VMEM((3, TOKENS, MERGE * WIDTH), BF16),
-            pltpu.VMEM((MERGE * TOKENS, 3 * WIDTH), F32),
-            pltpu.SemaphoreType.DMA((7,)),
+            pltpu.VMEM(slot.shape, jnp.int32),
+            pltpu.VMEM(saved.shape, BF16),
+            pltpu.SemaphoreType.DMA((2,)),
         ],
+        compiler_params=pltpu.CompilerParams(vmem_limit_bytes=58 << 20),
         cost_estimate=cost(8),
-    )(slot, saved, *injected, *projections)
+    )(slot, saved)
+
+
+def stack_kernel(early_ref, middle_ref, late_ref, stacked_ref):
+    for m, ref in enumerate((early_ref, middle_ref, late_ref)):
+        stacked_ref[m * SHARD : (m + 1) * SHARD] = ref[...]
+
+
+def stack(projections):
+    return pl.pallas_call(
+        stack_kernel,
+        out_shape=jax.ShapeDtypeStruct((3 * SHARD, WIDTH), BF16),
+        in_specs=[VMEM] * 3,
+        out_specs=VMEM,
+        compiler_params=pltpu.CompilerParams(vmem_limit_bytes=8 << 20),
+        cost_estimate=cost(4),
+    )(*projections)
+
+
+def add_down(refs, sums, at):
+    early_ref, middle_ref, late_ref = refs
+    for j in range(MERGE):
+        columns = slice(j * WIDTH, (j + 1) * WIDTH)
+        to = slice(j * TOKENS, (j + 1) * TOKENS)
+        late = late_ref[:, columns].astype(F32)
+        middle = late + middle_ref[:, columns].astype(F32)
+        sums[to, :WIDTH] = middle + early_ref[:, columns].astype(F32)
+        if at > WIDTH:
+            sums[to, 2 * WIDTH :] = late
+            sums[to, WIDTH : 2 * WIDTH] = middle
+
+
+def share_kernel(early_ref, middle_ref, late_ref, shares_ref, sums):
+    add_down((early_ref, middle_ref, late_ref), sums, WIDTH)
+    early = sums[...]
+    main = [early[:, d * SHARD : d * SHARD + 128] for d in range(8)]
+    rest = [early[:, d * SHARD + 128 : (d + 1) * SHARD] for d in range(8)]
+    shares_ref[...] = jnp.concatenate(main + rest, axis=1).astype(BF16)
+
+
+def rows_kernel(early_ref, middle_ref, late_ref, rows_ref, sums):
+    used = MERGE * TOKENS
+    add_down((early_ref, middle_ref, late_ref), sums, 3 * WIDTH)
+    rows_ref[...] = jnp.zeros_like(rows_ref)
+    rows_ref[FIRST : FIRST + used, : 3 * WIDTH] = sums[...].astype(BF16)
+
+
+def from_injected(kernel, injected, shape, width):
+    return pl.pallas_call(
+        kernel,
+        out_shape=jax.ShapeDtypeStruct(shape, BF16),
+        in_specs=[VMEM] * 3,
+        out_specs=VMEM,
+        scratch_shapes=[pltpu.VMEM((MERGE * TOKENS, width), F32)],
+        compiler_params=PARAMS,
+        cost_estimate=cost(4),
+    )(*injected)
 
 
 def place_key(column):
@@ -313,12 +335,16 @@
                 from_ref = ref.at[pl.ds(low - start, high - low)]
                 to_ref = weight.at[m, pl.ds(base, high - low)]
                 copies.append((m, pltpu.make_async_copy(from_ref, to_ref, sem.at[m])))
-    for _, copy in copies:
-        copy.start()
+    for m, copy in copies:
+        if m == 0:
+            copy.start()
     landed = landed_ref[...].astype(F32).reshape(8 * SLOTS, ROWS_HALF).astype(BF16)
     placed = matmul_tn(table_ref[...], landed).astype(BF16)
     half = MERGE * SLOTS
     placed = jnp.concatenate([placed[:half], placed[half:, : 3 * WIDTH - ROWS_HALF]], axis=1)
+    for m, copy in copies:
+        if m > 0:
+            copy.start()
     stream_out[...] = placed[:, :WIDTH]
     for m, out in enumerate(outs):
         for of_m, copy in copies:
@@ -343,7 +369,7 @@
             pltpu.VMEM((3, WIDTH, WIDTH), BF16),
             pltpu.SemaphoreType.DMA((3,)),
         ],
-        compiler_params=pltpu.CompilerParams(vmem_limit_bytes=58 << 20),
+        compiler_params=pltpu.CompilerParams(vmem_limit_bytes=32 << 20),
         cost_estimate=cost(24),
     )(at, table, landed, *pieces)
 
@@ -360,23 +386,25 @@
 ):
     at = jnp.stack([lax.axis_index(name) for name in ("x", "core", "y")]).astype(jnp.int32)
 
-    message, table, stacked, rows, share = first(
-        slot_source,
-        saved_early[0],
-        (injected_early[0], injected_middle[0], injected_late[0]),
-        (projection_early, projection_middle, projection_late),
-    )
+    projections = (projection_early, projection_middle, projection_late)
+    message, table = first(slot_source, saved_early[0])
+    message, projections = lax.optimization_barrier((message, projections))
+    stacked = stack(projections)
     arrived = lax.all_to_all(message, CTX, 0, 0, tiled=True)
 
     from_left, from_right = over_x(stacked, 1), over_x(stacked, 3)
+    injected = injected_early[0], injected_middle[0], injected_late[0]
+    share = from_injected(share_kernel, injected, (MERGE * TOKENS, WIDTH), WIDTH)
+    rows = from_injected(rows_kernel, injected, (128, 2 * ROWS_HALF), 3 * WIDTH)
     shares = [share] + [over_y(share, step) for step in (1, 2, 3)]
     once_more = from_left[:CUT], from_right[CUT:]
+    arrived, shares = lax.optimization_barrier((arrived, shares))
+
+    landed = lax.all_to_all(pack(at, arrived, rows), CTX, 0, 0, tiled=True)
+
     arrived, shares, from_left, from_right, once_more = lax.optimization_barrier(
         (arrived, shares, from_left, from_right, once_more)
     )
-
-    landed = lax.all_to_all(pack(at, arrived, rows), CTX, 0, 0, tiled=True)
-
     far = over_x(once_more[0], 1), over_x(once_more[1], 3)
     keep, give = gradient(at, arrived, shares)
     mine, *parts = sum_core(keep, over_core(give))

time: 88 us -> 85 us (0.966)
  local copies, waits for them, and re-layouts: 3.56 us -> 1.14 us
  waiting for transfers between devices: 25.4 us -> 27.1 us
  starting transfers between devices: 40.7 us -> 39.5 us
  Pallas kernels: 17 us -> 15.9 us
    ppermute x3, waiting for transfers between devices: 3.6 us -> 10.6 us  [over_y(): return lax.ppermute(array, 'y', [(i, (i + step) % 4) for i in range(4)])]
    ppermute x7, waiting for transfers between devices: 19.4 us -> 13.2 us  [over_x(): return lax.ppermute(array, 'x', [(i, (i + step) % 4) for i in range(4)])]
    pallas_call x1, Pallas kernels: 3.97 us -> 2.29 us  [first(): pl.pallas_call(first_kernel, out_shape=(jax.ShapeDtypeStruct((SLOTS, SAVE...]
    slice x2, local copies, waits for them, and re-layouts: 2.78 us -> 1.11 us  [local(): once_more = (from_left[:CUT], from_right[CUT:])]
    all_to_all x1, starting transfers between devices: 7.91 us -> 6.39 us  [local(): landed = lax.all_to_all(pack(at, arrived, rows), CTX, 0, 0, tiled=True)]
    all_to_all x1, waiting for transfers between devices: 1.42 us -> 2.63 us  [local(): weights = add_up(lax.all_to_all(terms, 'z', 0, 0, tiled=True))]
  transfers between devices with their start and end apart: 19 -> 19, of which waited for: 9 -> 7; matrix products, arithmetic and copies ran while one was open for 3% -> 1% of each run, Pallas kernels for 11% -> 15%
where the time goes in v7:
time: 85 us; the launch traced here: 84.5 us
  starting transfers between devices  39.5 us (46%)
  waiting for transfers between devices  27.1 us (32%)
  Pallas kernels  15.9 us (19%)
  local copies, waits for them, and re-layouts  1.14 us (1%)
  between operations  0.86 us (1%)
    ppermute x7, waiting for transfers between devices, over_x(): return lax.ppermute(array, 'x', [(i, (i + step) % 4) for i in range(4)])  13.2 us
    all_to_all x1, starting transfers between devices, local(): arrived = lax.all_to_all(message, CTX, 0, 0, tiled=True)  11.6 us
    ppermute x3, waiting for transfers between devices, over_y(): return lax.ppermute(array, 'y', [(i, (i + step) % 4) for i in range(4)])  10.6 us
    ppermute x7, starting transfers between devices, over_x(): return lax.ppermute(array, 'x', [(i, (i + step) % 4) for i in range(4)])  9.27 us
    all_to_all x1, starting transfers between devices, local(): landed = lax.all_to_all(pack(at, arrived, rows), CTX, 0, 0, tiled=True)  6.39 us
    pallas_call x1, Pallas kernels, contexts(): pl.pallas_call(context_kernel, out_shape=(out,) * 4, in_specs=[SMEM, VMEM...  6.34 us
    all_to_all x1, starting transfers between devices, local(): weights = add_up(lax.all_to_all(terms, 'z', 0, 0, tiled=True))  6.27 us
    ppermute x3, starting transfers between devices, over_y(): return lax.ppermute(array, 'y', [(i, (i + step) % 4) for i in range(4)])  4.79 us
  transfers between devices with their start and end apart: 19, of which 7 were waited for; matrix products, arithmetic and copies ran while one was open for 1% of the time, Pallas kernels for 15%

profile of v7, /device:TPU:6, one launch (start us, length us, event | category | flops | bytes accessed | tf_op | source)
XLA Modules:
  0.0 84.5 jit_solution(7063503947854482616)
XLA Ops:
  0.6 2.3 %shard_map.119 = (bf16[32,16,384]{2,1,0:T(8,128)(2,1)}, bf16[256,256]{1,0:T(8,128)(2,1)}) custom-call(s32[1,32]{1,0:T(1,128)} %slot_hbm.1, bf16[128,1152]{1,0:T(8,128)(2,1)} %bitcast.17), custom_call_target="tpu_custom_call" | custom-call | bytes 8388608 | tf_op jit(solution)/shard_map/pallas_call | solution.py:104
  3.0 11.6 %all-to-all-start = ((bf16[32,16,384]{2,1,0:T(8,128)(2,1)}), bf16[32,16,384]{2,1,0:T(8,128)(2,1)S(1)}, u32[]{:S(2)}, u32[]{:S(2)}) async-start(bf16[32,16,384]{2,1,0:T(8,128)(2,1)} %get-tuple-element.50), calls=%async_computation | async-start | bytes 786432 | tf_op jit(solution)/shard_map/all_to_all | solution.py:393
  14.8 0.9 %collective-permute-start.4 = (bf16[432,1152]{1,0:T(8,128)(2,1)S(1)}, bf16[432,1152]{1,0:T(8,128)(2,1)}, u32[]{:S(2)}, u32[]{:S(2)}) collective-permute-start(bf16[432,1152]{1,0:T(8,128)(2,1)S(1)} %shard_map.121.refs_0_), channel_id=1, source_target_pairs={{0,192},{64,0},{128,64},{192,128},{1,193},{65,1},{129,65},{193,129... | collective-permute-start | bytes 2985992 | tf_op jit(solution)/shard_map/ppermute | solution.py:39
  15.7 2.4 %collective-permute-start.3 = (bf16[432,1152]{1,0:T(8,128)(2,1)S(1)}, bf16[432,1152]{1,0:T(8,128)(2,1)S(1)}, u32[]{:S(2)}, u32[]{:S(2)}) collective-permute-start(bf16[432,1152]{1,0:T(8,128)(2,1)S(1)} %shard_map.121.refs_0_), channel_id=1, source_target_pairs={{0,64},{64,128},{128,192},{192,0},{1,65},{65,129},{129,193},{193,1... | collective-permute-start | bytes 2985992 | tf_op jit(solution)/shard_map/ppermute | solution.py:39
  18.3 3.1 %collective-permute-start.2 = (bf16[80,1152]{1,0:T(8,128)(2,1)S(1)}, bf16[80,1152]{1,0:T(8,128)(2,1)}, u32[]{:S(2)}, u32[]{:S(2)}) collective-permute-start(bf16[80,1152]{1,0:T(8,128)(2,1)S(1)} %shard_map.120.refs_0_), channel_id=1, source_target_pairs={{0,3},{1,0},{2,1},{3,2},{4,7},{5,4},{6,5},{7,6},{8,11},{9,8},{10,9... | collective-permute-start | bytes 552968 | tf_op jit(solution)/shard_map/ppermute | solution.py:43
  21.4 0.9 %collective-permute-start.1 = (bf16[80,1152]{1,0:T(8,128)(2,1)S(1)}, bf16[80,1152]{1,0:T(8,128)(2,1)}, u32[]{:S(2)}, u32[]{:S(2)}) collective-permute-start(bf16[80,1152]{1,0:T(8,128)(2,1)S(1)} %shard_map.120.refs_0_), channel_id=1, source_target_pairs={{0,2},{1,3},{2,0},{3,1},{4,6},{5,7},{6,4},{7,5},{8,10},{9,11},{10,... | collective-permute-start | bytes 552968 | tf_op jit(solution)/shard_map/ppermute | solution.py:43
  22.2 0.9 %collective-permute-start = (bf16[80,1152]{1,0:T(8,128)(2,1)S(1)}, bf16[80,1152]{1,0:T(8,128)(2,1)}, u32[]{:S(2)}, u32[]{:S(2)}) collective-permute-start(bf16[80,1152]{1,0:T(8,128)(2,1)S(1)} %shard_map.120.refs_0_), channel_id=1, source_target_pairs={{0,1},{1,2},{2,3},{3,0},{4,5},{5,6},{6,7},{7,4},{8,9},{9,10},{10,1... | collective-permute-start | bytes 552968 | tf_op jit(solution)/shard_map/ppermute | solution.py:43
  23.4 6.8 %collective-permute-done.2.refs_3_ = bf16[80,1152]{1,0:T(8,128)(2,1)} collective-permute-done((bf16[80,1152]{1,0:T(8,128)(2,1)S(1)}, bf16[80,1152]{1,0:T(8,128)(2,1)}, u32[]{:S(2)}, u32[]{:S(2)}) %collective-permute-start.2) | collective-permute-done | bytes 184352 | tf_op jit(solution)/shard_map/ppermute | solution.py:43
  30.2 1.2 %collective-permute-done.1.refs_2_ = bf16[80,1152]{1,0:T(8,128)(2,1)} collective-permute-done((bf16[80,1152]{1,0:T(8,128)(2,1)S(1)}, bf16[80,1152]{1,0:T(8,128)(2,1)}, u32[]{:S(2)}, u32[]{:S(2)}) %collective-permute-start.1) | collective-permute-done | bytes 184352 | tf_op jit(solution)/shard_map/ppermute | solution.py:43
  31.3 2.6 %collective-permute-done.refs_1_ = bf16[80,1152]{1,0:T(8,128)(2,1)} collective-permute-done((bf16[80,1152]{1,0:T(8,128)(2,1)S(1)}, bf16[80,1152]{1,0:T(8,128)(2,1)}, u32[]{:S(2)}, u32[]{:S(2)}) %collective-permute-start) | collective-permute-done | bytes 184352 | tf_op jit(solution)/shard_map/ppermute | solution.py:43
  33.9 2.4 %shard_map.126 = bf16[32,8,1792]{2,1,0:T(8,128)(2,1)} custom-call(s32[3]{0:T(128)S(1)} %pad_add_fusion.at_ref, bf16[32,16,384]{2,1,0:T(8,128)(2,1)S(1)} %all-to-all-done.arrived_ref, bf16[128,3584]{1,0:T(8,128)(2,1)S(1)} %shard_map.125.rows_ref), custom_call_target="tpu_custom_call" | custom-call | bytes 41943040 | tf_op jit(solution)/shard_map/pallas_call | solution.py:200
  36.3 6.4 %all-to-all-start.1 = ((bf16[32,8,1792]{2,1,0:T(8,128)(2,1)}), bf16[32,8,1792]{2,1,0:T(8,128)(2,1)S(1)}, u32[]{:S(2)}, u32[]{:S(2)}) async-start(bf16[32,8,1792]{2,1,0:T(8,128)(2,1)} %shard_map.126), calls=%async_computation.1 | async-start | bytes 1835008 | tf_op jit(solution)/shard_map/all_to_all | solution.py:403
  42.7 1.1 %slice.9 = bf16[208,1152]{1,0:T(8,128)(2,1)S(1)} slice(bf16[432,1152]{1,0:T(8,128)(2,1)} %collective-permute-done.4.refs_2_), slice={[224:432], [0:1152]} | slice | bytes 958464 | tf_op jit(solution)/shard_map/slice | solution.py:400
  44.2 2.8 %shard_map.122 = (f32[4,8,48,128]{3,2,1,0:T(8,128)S(1)}, bf16[4,8,48,128]{3,2,1,0:T(8,128)(2,1)S(1)}) custom-call(s32[3]{0:T(128)S(1)} %pad_add_fusion.at_ref, bf16[32,16,384]{2,1,0:T(8,128)(2,1)S(1)} %all-to-all-done.arrived_ref, bf16[80,1152]{1,0:T(8,128)(2,1)S(1)} %shard_map.120.refs_0_, bf16[80,1152]{1,0:T(8,128)(2,1)} %collective-permute-done.refs_1_, ...), custom_call_target="tpu_custom_call" | custom-call | bytes 41943040 | tf_op jit(solution)/shard_map/pallas_call | solution.py:253
  47.1 1.8 %collective-permute-start.10 = (bf16[208,1152]{1,0:T(8,128)(2,1)S(1)}, bf16[208,1152]{1,0:T(8,128)(2,1)}, u32[]{:S(2)}, u32[]{:S(2)}) collective-permute-start(bf16[208,1152]{1,0:T(8,128)(2,1)S(1)} %slice.9), channel_id=1, source_target_pairs={{0,192},{64,0},{128,64},{192,128},{1,193},{65,1},{129,65},{193,129... | collective-permute-start | bytes 1437704 | tf_op jit(solution)/shard_map/ppermute | solution.py:39
  49.0 1.6 %collective-permute-start.6 = (bf16[8,48,128]{2,1,0:T(8,128)(2,1)S(1)}, bf16[8,48,128]{2,1,0:T(8,128)(2,1)S(1)}, u32[]{:S(2)}, u32[]{:S(2)}) collective-permute-start(bf16[8,48,128]{2,1,0:T(8,128)(2,1)S(1)} %get-tuple-element.67), channel_id=1, source_target_pairs={{0,64},{64,128},{128,192},{192,0},{1,65},{65,129},{129,193},{193,1... | collective-permute-start | bytes 294920 | tf_op jit(solution)/shard_map/ppermute | solution.py:39
  50.6 2.2 %collective-permute-start.7 = (bf16[8,48,128]{2,1,0:T(8,128)(2,1)S(1)}, bf16[8,48,128]{2,1,0:T(8,128)(2,1)S(1)}, u32[]{:S(2)}, u32[]{:S(2)}) collective-permute-start(bf16[8,48,128]{2,1,0:T(8,128)(2,1)S(1)} %get-tuple-element.68), channel_id=1, source_target_pairs={{0,128},{64,192},{128,0},{192,64},{1,129},{65,193},{129,1},{193,65... | collective-permute-start | bytes 294920 | tf_op jit(solution)/shard_map/ppermute | solution.py:39
  52.8 11.6 %collective-permute-done.10.refs_4_ = bf16[208,1152]{1,0:T(8,128)(2,1)} collective-permute-done((bf16[208,1152]{1,0:T(8,128)(2,1)S(1)}, bf16[208,1152]{1,0:T(8,128)(2,1)}, u32[]{:S(2)}, u32[]{:S(2)}) %collective-permute-start.10) | collective-permute-done | bytes 479264 | tf_op jit(solution)/shard_map/ppermute | solution.py:39
  64.4 1.5 %collective-permute-done.8.third = bf16[8,48,128]{2,1,0:T(8,128)(2,1)S(1)} collective-permute-done((bf16[8,48,128]{2,1,0:T(8,128)(2,1)S(1)}, bf16[8,48,128]{2,1,0:T(8,128)(2,1)S(1)}, u32[]{:S(2)}, u32[]{:S(2)}) %collective-permute-start.8) | collective-permute-done | bytes 98336 | tf_op jit(solution)/shard_map/ppermute | solution.py:39
  67.6 0.7 all-to-all-done.1.landed_ref
  68.3 6.3 %all-to-all-start.2 = ((bf16[8,48,128]{2,1,0:T(8,128)(2,1)}), bf16[8,48,128]{2,1,0:T(8,128)(2,1)S(1)}, u32[]{:S(2)}, u32[]{:S(2)}) async-start(bf16[8,48,128]{2,1,0:T(8,128)(2,1)} %shard_map.124), calls=%async_computation.2 | async-start | bytes 196608 | tf_op jit(solution)/shard_map/all_to_all | solution.py:419
  74.7 6.3 %shard_map.127 = (bf16[128,1152]{1,0:T(8,128)(2,1)}, bf16[128,1152]{1,0:T(8,128)(2,1)}, bf16[128,1152]{1,0:T(8,128)(2,1)}, bf16[128,1152]{1,0:T(8,128)(2,1)}) custom-call(s32[3]{0:T(128)S(1)} %pad_add_fusion.at_ref, bf16[256,256]{1,0:T(8,128)(2,1)S(1)} %copy-done.6, bf16[32,8,1792]{2,1,0:T(8,128)(2,1)S(1)} %all-to-all-done.1.landed_ref, ...), custom_call_target="tpu_custom_call" | custom-call | bytes 25165824 | tf_op jit(solution)/shard_map/pallas_call | solution.py:363
  81.0 2.6 %all-to-all-done.2.terms_ref = bf16[8,48,128]{2,1,0:T(8,128)(2,1)S(1)} async-done(((bf16[8,48,128]{2,1,0:T(8,128)(2,1)}), bf16[8,48,128]{2,1,0:T(8,128)(2,1)S(1)}, u32[]{:S(2)}, u32[]{:S(2)}) %all-to-all-start.2) | async-done | bytes 98336 | tf_op jit(solution)/shard_map/all_to_all | solution.py:419
  83.7 0.8 shard_map.128
  (41 shorter events, 2.9 us)
Async XLA Ops:
  0.6 14.0 %copy-start.5 = (bf16[144,1152]{1,0:T(8,128)(2,1)S(1)}, bf16[144,1152]{1,0:T(8,128)(2,1)}, u32[]{:S(2)}) copy-start(bf16[144,1152]{1,0:T(8,128)(2,1)} %late_ref) | copy-start | bytes 995332
  2.9 11.7 %copy-start.3 = (bf16[144,1152]{1,0:T(8,128)(2,1)S(1)}, bf16[144,1152]{1,0:T(8,128)(2,1)}, u32[]{:S(2)}) copy-start(bf16[144,1152]{1,0:T(8,128)(2,1)} %early_ref) | copy-start | bytes 995332
  3.0 11.7 %copy-start.4 = (bf16[144,1152]{1,0:T(8,128)(2,1)S(1)}, bf16[144,1152]{1,0:T(8,128)(2,1)}, u32[]{:S(2)}) copy-start(bf16[144,1152]{1,0:T(8,128)(2,1)} %middle_ref) | copy-start | bytes 995332
  3.0 31.0 %all-to-all-start = ((bf16[32,16,384]{2,1,0:T(8,128)(2,1)}), bf16[32,16,384]{2,1,0:T(8,128)(2,1)S(1)}, u32[]{:S(2)}, u32[]{:S(2)}) async-start(bf16[32,16,384]{2,1,0:T(8,128)(2,1)} %get-tuple-element.50), calls=%async_computation | async-start | bytes 786432 | tf_op jit(solution)/shard_map/all_to_all | solution.py:393
  14.6 3.4 %copy-start = (bf16[1,20,4608]{2,1,0:T(8,128)(2,1)S(1)}, bf16[1,20,4608]{2,1,0:T(8,128)(2,1)}, u32[]{:S(2)}) copy-start(bf16[1,20,4608]{2,1,0:T(8,128)(2,1)} %param.8) | copy-start | bytes 552964
  14.8 28.0 %collective-permute-start.4 = (bf16[432,1152]{1,0:T(8,128)(2,1)S(1)}, bf16[432,1152]{1,0:T(8,128)(2,1)}, u32[]{:S(2)}, u32[]{:S(2)}) collective-permute-start(bf16[432,1152]{1,0:T(8,128)(2,1)S(1)} %shard_map.121.refs_0_), channel_id=1, source_target_pairs={{0,192},{64,0},{128,64},{192,128},{1,193},{65,1},{129,65},{193,129... | collective-permute-start | bytes 2985992 | tf_op jit(solution)/shard_map/ppermute | solution.py:39
  15.7 28.1 %collective-permute-start.3 = (bf16[432,1152]{1,0:T(8,128)(2,1)S(1)}, bf16[432,1152]{1,0:T(8,128)(2,1)S(1)}, u32[]{:S(2)}, u32[]{:S(2)}) collective-permute-start(bf16[432,1152]{1,0:T(8,128)(2,1)S(1)} %shard_map.121.refs_0_), channel_id=1, source_target_pairs={{0,64},{64,128},{128,192},{192,0},{1,65},{65,129},{129,193},{193,1... | collective-permute-start | bytes 2985992 | tf_op jit(solution)/shard_map/ppermute | solution.py:39
  18.3 11.9 %collective-permute-start.2 = (bf16[80,1152]{1,0:T(8,128)(2,1)S(1)}, bf16[80,1152]{1,0:T(8,128)(2,1)}, u32[]{:S(2)}, u32[]{:S(2)}) collective-permute-start(bf16[80,1152]{1,0:T(8,128)(2,1)S(1)} %shard_map.120.refs_0_), channel_id=1, source_target_pairs={{0,3},{1,0},{2,1},{3,2},{4,7},{5,4},{6,5},{7,6},{8,11},{9,8},{10,9... | collective-permute-start | bytes 552968 | tf_op jit(solution)/shard_map/ppermute | solution.py:43
  21.4 10.0 %collective-permute-start.1 = (bf16[80,1152]{1,0:T(8,128)(2,1)S(1)}, bf16[80,1152]{1,0:T(8,128)(2,1)}, u32[]{:S(2)}, u32[]{:S(2)}) collective-permute-start(bf16[80,1152]{1,0:T(8,128)(2,1)S(1)} %shard_map.120.refs_0_), channel_id=1, source_target_pairs={{0,2},{1,3},{2,0},{3,1},{4,6},{5,7},{6,4},{7,5},{8,10},{9,11},{10,... | collective-permute-start | bytes 552968 | tf_op jit(solution)/shard_map/ppermute | solution.py:43
  22.2 11.7 %collective-permute-start = (bf16[80,1152]{1,0:T(8,128)(2,1)S(1)}, bf16[80,1152]{1,0:T(8,128)(2,1)}, u32[]{:S(2)}, u32[]{:S(2)}) collective-permute-start(bf16[80,1152]{1,0:T(8,128)(2,1)S(1)} %shard_map.120.refs_0_), channel_id=1, source_target_pairs={{0,1},{1,2},{2,3},{3,0},{4,5},{5,6},{6,7},{7,4},{8,9},{9,10},{10,1... | collective-permute-start | bytes 552968 | tf_op jit(solution)/shard_map/ppermute | solution.py:43
  36.3 32.0 %all-to-all-start.1 = ((bf16[32,8,1792]{2,1,0:T(8,128)(2,1)}), bf16[32,8,1792]{2,1,0:T(8,128)(2,1)S(1)}, u32[]{:S(2)}, u32[]{:S(2)}) async-start(bf16[32,8,1792]{2,1,0:T(8,128)(2,1)} %shard_map.126), calls=%async_computation.1 | async-start | bytes 1835008 | tf_op jit(solution)/shard_map/all_to_all | solution.py:403
  43.8 22.1 %collective-permute-start.9 = (bf16[224,1152]{1,0:T(8,128)(2,1)S(1)}, bf16[224,1152]{1,0:T(8,128)(2,1)}, u32[]{:S(2)}, u32[]{:S(2)}) collective-permute-start(bf16[224,1152]{1,0:T(8,128)(2,1)S(1)} %slice.8), channel_id=1, source_target_pairs={{0,64},{64,128},{128,192},{192,0},{1,65},{65,129},{129,193},{193,1... | collective-permute-start | bytes 1548296 | tf_op jit(solution)/shard_map/ppermute | solution.py:39
  47.0 1.9 %collective-permute-start.5 = (bf16[4,8,48,128]{3,2,1,0:T(8,128)(2,1)S(1)}, bf16[4,8,48,128]{3,2,1,0:T(8,128)(2,1)S(1)}, u32[]{:S(2)}, u32[]{:S(2)}) collective-permute-start(bf16[4,8,48,128]{3,2,1,0:T(8,128)(2,1)S(1)} %get-tuple-element.65), channel_id=1, source_target_pairs={{0,32},{32,0},{1,33},{33,1},{2,34},{34,2},{3,35},{35,3},{4,36},{36... | collective-permute-start | bytes 1179656 | tf_op jit(solution)/shard_map/ppermute | solution.py:47
  47.1 17.3 %collective-permute-start.10 = (bf16[208,1152]{1,0:T(8,128)(2,1)S(1)}, bf16[208,1152]{1,0:T(8,128)(2,1)}, u32[]{:S(2)}, u32[]{:S(2)}) collective-permute-start(bf16[208,1152]{1,0:T(8,128)(2,1)S(1)} %slice.9), channel_id=1, source_target_pairs={{0,192},{64,0},{128,64},{192,128},{1,193},{65,1},{129,65},{193,129... | collective-permute-start | bytes 1437704 | tf_op jit(solution)/shard_map/ppermute | solution.py:39
  49.0 15.4 %collective-permute-start.6 = (bf16[8,48,128]{2,1,0:T(8,128)(2,1)S(1)}, bf16[8,48,128]{2,1,0:T(8,128)(2,1)S(1)}, u32[]{:S(2)}, u32[]{:S(2)}) collective-permute-start(bf16[8,48,128]{2,1,0:T(8,128)(2,1)S(1)} %get-tuple-element.67), channel_id=1, source_target_pairs={{0,64},{64,128},{128,192},{192,0},{1,65},{65,129},{129,193},{193,1... | collective-permute-start | bytes 294920 | tf_op jit(solution)/shard_map/ppermute | solution.py:39
  50.6 13.8 %collective-permute-start.7 = (bf16[8,48,128]{2,1,0:T(8,128)(2,1)S(1)}, bf16[8,48,128]{2,1,0:T(8,128)(2,1)S(1)}, u32[]{:S(2)}, u32[]{:S(2)}) collective-permute-start(bf16[8,48,128]{2,1,0:T(8,128)(2,1)S(1)} %get-tuple-element.68), channel_id=1, source_target_pairs={{0,128},{64,192},{128,0},{192,64},{1,129},{65,193},{129,1},{193,65... | collective-permute-start | bytes 294920 | tf_op jit(solution)/shard_map/ppermute | solution.py:39
  52.8 13.2 %collective-permute-start.8 = (bf16[8,48,128]{2,1,0:T(8,128)(2,1)S(1)}, bf16[8,48,128]{2,1,0:T(8,128)(2,1)S(1)}, u32[]{:S(2)}, u32[]{:S(2)}) collective-permute-start(bf16[8,48,128]{2,1,0:T(8,128)(2,1)S(1)} %get-tuple-element.69), channel_id=1, source_target_pairs={{0,192},{64,0},{128,64},{192,128},{1,193},{65,1},{129,65},{193,129... | collective-permute-start | bytes 294920 | tf_op jit(solution)/shard_map/ppermute | solution.py:39
  66.6 8.1 %copy-start.6 = (bf16[256,256]{1,0:T(8,128)(2,1)S(1)}, bf16[256,256]{1,0:T(8,128)(2,1)}, u32[]{:S(2)}) copy-start(bf16[256,256]{1,0:T(8,128)(2,1)} %get-tuple-element.48.table_ref) | copy-start | bytes 393220
  66.6 8.0 %collective-permute-start.11 = (bf16[432,1152]{1,0:T(8,128)(2,1)S(1)}, bf16[432,1152]{1,0:T(8,128)(2,1)}, u32[]{:S(2)}, u32[]{:S(2)}) collective-permute-start(bf16[432,1152]{1,0:T(8,128)(2,1)S(1)} %shard_map.121.refs_0_), channel_id=1, source_target_pairs={{0,32},{32,0},{1,33},{33,1},{2,34},{34,2},{3,35},{35,3},{4,36},{36... | collective-permute-start | bytes 2985992 | tf_op jit(solution)/shard_map/ppermute | solution.py:47
  66.6 8.0 %collective-permute-start.12 = (bf16[432,1152]{1,0:T(8,128)(2,1)S(1)}, bf16[432,1152]{1,0:T(8,128)(2,1)}, u32[]{:S(2)}, u32[]{:S(2)}) collective-permute-start(bf16[432,1152]{1,0:T(8,128)(2,1)S(1)} %collective-permute-done.3.refs_1_), channel_id=1, source_target_pairs={{0,32},{32,0},{1,33},{33,1},{2,34},{34,2},{3,35},{35,3},{4,36},{36... | collective-permute-start | bytes 2985992 | tf_op jit(solution)/shard_map/ppermute | solution.py:47
  67.1 7.5 %collective-permute-start.13 = (bf16[432,1152]{1,0:T(8,128)(2,1)}, bf16[432,1152]{1,0:T(8,128)(2,1)}, u32[]{:S(2)}, u32[]{:S(2)}) collective-permute-start(bf16[432,1152]{1,0:T(8,128)(2,1)} %collective-permute-done.4.refs_2_), channel_id=1, source_target_pairs={{0,32},{32,0},{1,33},{33,1},{2,34},{34,2},{3,35},{35,3},{4,36},{36... | collective-permute-start | bytes 2985992 | tf_op jit(solution)/shard_map/ppermute | solution.py:47
  67.1 7.5 %collective-permute-start.14 = (bf16[224,1152]{1,0:T(8,128)(2,1)}, bf16[224,1152]{1,0:T(8,128)(2,1)}, u32[]{:S(2)}, u32[]{:S(2)}) collective-permute-start(bf16[224,1152]{1,0:T(8,128)(2,1)} %collective-permute-done.9.refs_3_), channel_id=1, source_target_pairs={{0,32},{32,0},{1,33},{33,1},{2,34},{34,2},{3,35},{35,3},{4,36},{36... | collective-permute-start | bytes 1548296 | tf_op jit(solution)/shard_map/ppermute | solution.py:47
  67.6 7.0 %collective-permute-start.15 = (bf16[208,1152]{1,0:T(8,128)(2,1)}, bf16[208,1152]{1,0:T(8,128)(2,1)}, u32[]{:S(2)}, u32[]{:S(2)}) collective-permute-start(bf16[208,1152]{1,0:T(8,128)(2,1)} %collective-permute-done.10.refs_4_), channel_id=1, source_target_pairs={{0,32},{32,0},{1,33},{33,1},{2,34},{34,2},{3,35},{35,3},{4,36},{36... | collective-permute-start | bytes 1437704 | tf_op jit(solution)/shard_map/ppermute | solution.py:47
  68.3 15.3 %all-to-all-start.2 = ((bf16[8,48,128]{2,1,0:T(8,128)(2,1)}), bf16[8,48,128]{2,1,0:T(8,128)(2,1)S(1)}, u32[]{:S(2)}, u32[]{:S(2)}) async-start(bf16[8,48,128]{2,1,0:T(8,128)(2,1)} %shard_map.124), calls=%async_computation.2 | async-start | bytes 196608 | tf_op jit(solution)/shard_map/all_to_all | solution.py:419
  (2 other events, 6.8 us)

commit v8 on v7

--- a/solution.py
+++ b/solution.py
@@ -67,25 +67,45 @@
     return jnp.floor((value + 0.5) * (1.0 / by))
 
 
-def first_kernel(slot_hbm, saved_hbm, message_ref, table_ref, slot_ref, saved_ref, sem):
+def patch_slots(slot):
+    source = slot.astype(F32)
+    sender = quotient(source, TOKENS)
+    place = source - TOKENS * sender
+    both = jnp.where(iota((8, SLOTS), 0) == 0, sender, place).astype(BF16)
+    repeat = onehot(iota((SLOTS, SLOTS * MERGE), 1) // MERGE == iota((SLOTS, SLOTS * MERGE), 0))
+    wide = matmul(both, repeat)
+    return wide[0:1], wide[1:2]
+
+
+def table_kernel(slot_ref, table_ref):
+    sender, _ = patch_slots(slot_ref[...])
+    count = MERGE * SLOTS
+    row, column = iota((2 * count, count), 0), iota((2 * count, count), 1)
+    match = (sender == (row // 8).astype(F32)) & (row % MERGE == column % MERGE)
+    table_ref[:, :count] = onehot(match & (row % 8 < MERGE))
+    table_ref[:, count:] = onehot(match & (row % 8 >= MERGE))
+
+
+def make_table(slot):
+    return pl.pallas_call(
+        table_kernel,
+        out_shape=jax.ShapeDtypeStruct((8 * SLOTS, 2 * MERGE * SLOTS), BF16),
+        in_specs=[VMEM],
+        out_specs=VMEM,
+        compiler_params=PARAMS,
+        cost_estimate=cost(4),
+    )(slot)
+
+
+def first_kernel(slot_hbm, saved_hbm, message_ref, slot_ref, saved_ref, sem):
     fetch_slot = pltpu.make_async_copy(slot_hbm, slot_ref, sem.at[0])
     fetch_saved = pltpu.make_async_copy(saved_hbm, saved_ref, sem.at[1])
     fetch_slot.start()
     fetch_saved.start()
     fetch_slot.wait()
 
-    source = slot_ref[...].astype(F32)
-    sender = quotient(source, TOKENS)
-    place = source - TOKENS * sender
-    both = jnp.where(iota((8, SLOTS), 0) == 0, sender, place).astype(BF16)
-    repeat = onehot(iota((SLOTS, SLOTS * MERGE), 1) // MERGE == iota((SLOTS, SLOTS * MERGE), 0))
-    wide = matmul(both, repeat)
-    sender, place = wide[0:1], wide[1:2]
+    sender, place = patch_slots(slot_ref[...])
     count = MERGE * SLOTS
-    row, column = iota((2 * count, count), 0), iota((2 * count, count), 1)
-    match = (sender == (row // 8).astype(F32)) & (row % MERGE == column % MERGE)
-    table_ref[:, :count] = onehot(match & (row % 8 < MERGE))
-    table_ref[:, count:] = onehot(match & (row % 8 >= MERGE))
     row, column = iota((count, count), 0), iota((count, count), 1)
     match = (sender == (row // MERGE).astype(F32)) & (row % MERGE == column % MERGE)
     tag = jnp.sum(jnp.where(match, place + 1.0, 0.0), axis=1, keepdims=True)
@@ -103,12 +123,9 @@
 def first(slot, saved):
     return pl.pallas_call(
         first_kernel,
-        out_shape=(
-            jax.ShapeDtypeStruct((SLOTS, SAVED_ROWS, SAVED_WIDE), BF16),
-            jax.ShapeDtypeStruct((8 * SLOTS, 2 * MERGE * SLOTS), BF16),
-        ),
+        out_shape=jax.ShapeDtypeStruct((SLOTS, SAVED_ROWS, SAVED_WIDE), BF16),
         in_specs=[HBM] * 2,
-        out_specs=(VMEM,) * 2,
+        out_specs=VMEM,
         scratch_shapes=[
             pltpu.VMEM(slot.shape, jnp.int32),
             pltpu.VMEM(saved.shape, BF16),
@@ -182,18 +199,24 @@
 
 def pack_kernel(at_ref, arrived_ref, rows_ref, packed_ref):
     arrived = arrived_ref[...].astype(F32).reshape(SLOTS * SAVED_ROWS, SAVED_WIDE).astype(BF16)
-    shape = (8 * SLOTS, SLOTS * SAVED_ROWS)
+    count = MERGE * SLOTS
+    shape = (count, SLOTS * SAVED_ROWS)
     row, column = iota(shape, 0), iota(shape, 1)
     mine = MERGE * at_ref[2]
-    spread = onehot((row // 8 == column // SAVED_ROWS) & (column % SAVED_ROWS == mine))
+    spread = onehot((row // MERGE == column // SAVED_ROWS) & (column % SAVED_ROWS == mine))
     asked = matmul(spread, arrived[:, SAVED_WIDE - 128 :])
-    row, column = iota((8 * SLOTS, 128), 0), iota((8 * SLOTS, 128), 1)
+    row, column = iota((count, 128), 0), iota((count, 128), 1)
     inside = (column >= FIRST) & (column < FIRST + MERGE * TOKENS)
     key = place_key(column - FIRST).astype(F32)
-    match = inside & (asked + (32 * (row % MERGE)).astype(F32) == key)
-    packed = matmul(onehot(match & (row % 8 < MERGE)), rows_ref[:, :ROWS_HALF])
-    packed = packed + matmul(onehot(match & (row % 8 >= MERGE)), rows_ref[:, ROWS_HALF:])
-    packed_ref[...] = packed.reshape(SLOTS, 8, ROWS_HALF).astype(BF16)
+    match = onehot(inside & (asked + (32 * (row % MERGE)).astype(F32) == key))
+    upper = iota((count, ROWS_HALF), 0) % 8 < MERGE
+    left = matmul(match, rows_ref[:, :ROWS_HALF])
+    right = matmul(match, rows_ref[:, ROWS_HALF:])
+    even = jnp.where(upper, left, pltpu.roll(right, MERGE, 0)).astype(BF16)
+    odd = jnp.where(upper, pltpu.roll(left, count - MERGE, 0), right).astype(BF16)
+    for k in range(SLOTS // 2):
+        packed_ref[2 * k] = even[8 * k : 8 * (k + 1)]
+        packed_ref[2 * k + 1] = odd[8 * k : 8 * (k + 1)]
 
 
 def pack(at, arrived, rows):
@@ -387,8 +410,11 @@
     at = jnp.stack([lax.axis_index(name) for name in ("x", "core", "y")]).astype(jnp.int32)
 
     projections = (projection_early, projection_middle, projection_late)
-    message, table = first(slot_source, saved_early[0])
-    message, projections = lax.optimization_barrier((message, projections))
+    message = first(slot_source, saved_early[0])
+    message, projections, slot_source = lax.optimization_barrier(
+        (message, projections, slot_source)
+    )
+    table = make_table(slot_source)
     stacked = stack(projections)
     arrived = lax.all_to_all(message, CTX, 0, 0, tiled=True)
 

time: 85 us -> 84.6 us (level)
    pallas_call x1 -> x2, Pallas kernels: 2.29 us -> 2.46 us  [the longest x1 2.29 us: first(): pl.pallas_call(first_kernel, out_shape=jax.ShapeDtypeStruct((SLOTS, SAVED...]
where the time goes in v8:
time: 84.6 us; the launch traced here: 84.2 us
  starting transfers between devices  39.5 us (47%)
  waiting for transfers between devices  26.9 us (32%)
  Pallas kernels  15.7 us (19%)
  local copies, waits for them, and re-layouts  1.14 us (1%)
  between operations  0.87 us (1%)
    ppermute x7, waiting for transfers between devices, over_x(): return lax.ppermute(array, 'x', [(i, (i + step) % 4) for i in range(4)])  13.2 us
    all_to_all x1, starting transfers between devices, local(): arrived = lax.all_to_all(message, CTX, 0, 0, tiled=True)  11.6 us
    ppermute x3, waiting for transfers between devices, over_y(): return lax.ppermute(array, 'y', [(i, (i + step) % 4) for i in range(4)])  10.6 us
    ppermute x7, starting transfers between devices, over_x(): return lax.ppermute(array, 'x', [(i, (i + step) % 4) for i in range(4)])  9.26 us
    all_to_all x1, starting transfers between devices, local(): landed = lax.all_to_all(pack(at, arrived, rows), CTX, 0, 0, tiled=True)  6.39 us
    pallas_call x1, Pallas kernels, contexts(): pl.pallas_call(context_kernel, out_shape=(out,) * 4, in_specs=[SMEM, VMEM...  6.34 us
    all_to_all x1, starting transfers between devices, local(): weights = add_up(lax.all_to_all(terms, 'z', 0, 0, tiled=True))  6.26 us
    ppermute x3, starting transfers between devices, over_y(): return lax.ppermute(array, 'y', [(i, (i + step) % 4) for i in range(4)])  4.79 us
  transfers between devices with their start and end apart: 19, of which 7 were waited for; matrix products, arithmetic and copies ran while one was open for 1% of the time, Pallas kernels for 15%

profile of v8, /device:TPU:6, one launch (start us, length us, event | category | flops | bytes accessed | tf_op | source)
XLA Modules:
  0.0 84.2 jit_solution(525112868635389659)
XLA Ops:
  0.6 2.3 %shard_map.119 = bf16[32,16,384]{2,1,0:T(8,128)(2,1)} custom-call(s32[1,32]{1,0:T(1,128)} %slot_ref, bf16[128,1152]{1,0:T(8,128)(2,1)} %bitcast.17), custom_call_target="tpu_custom_call" | custom-call | bytes 8388608 | tf_op jit(solution)/shard_map/pallas_call | solution.py:124
  3.0 11.6 %all-to-all-start = ((bf16[32,16,384]{2,1,0:T(8,128)(2,1)}), bf16[32,16,384]{2,1,0:T(8,128)(2,1)S(1)}, u32[]{:S(2)}, u32[]{:S(2)}) async-start(bf16[32,16,384]{2,1,0:T(8,128)(2,1)} %shard_map.119), calls=%async_computation | async-start | bytes 786432 | tf_op jit(solution)/shard_map/all_to_all | solution.py:419
  14.8 0.9 %collective-permute-start.4 = (bf16[432,1152]{1,0:T(8,128)(2,1)S(1)}, bf16[432,1152]{1,0:T(8,128)(2,1)}, u32[]{:S(2)}, u32[]{:S(2)}) collective-permute-start(bf16[432,1152]{1,0:T(8,128)(2,1)S(1)} %shard_map.122.refs_0_), channel_id=1, source_target_pairs={{0,192},{64,0},{128,64},{192,128},{1,193},{65,1},{129,65},{193,129... | collective-permute-start | bytes 2985992 | tf_op jit(solution)/shard_map/ppermute | solution.py:39
  15.7 2.4 %collective-permute-start.3 = (bf16[432,1152]{1,0:T(8,128)(2,1)S(1)}, bf16[432,1152]{1,0:T(8,128)(2,1)S(1)}, u32[]{:S(2)}, u32[]{:S(2)}) collective-permute-start(bf16[432,1152]{1,0:T(8,128)(2,1)S(1)} %shard_map.122.refs_0_), channel_id=1, source_target_pairs={{0,64},{64,128},{128,192},{192,0},{1,65},{65,129},{129,193},{193,1... | collective-permute-start | bytes 2985992 | tf_op jit(solution)/shard_map/ppermute | solution.py:39
  18.3 3.1 %collective-permute-start.2 = (bf16[80,1152]{1,0:T(8,128)(2,1)S(1)}, bf16[80,1152]{1,0:T(8,128)(2,1)}, u32[]{:S(2)}, u32[]{:S(2)}) collective-permute-start(bf16[80,1152]{1,0:T(8,128)(2,1)S(1)} %shard_map.121.refs_0_), channel_id=1, source_target_pairs={{0,3},{1,0},{2,1},{3,2},{4,7},{5,4},{6,5},{7,6},{8,11},{9,8},{10,9... | collective-permute-start | bytes 552968 | tf_op jit(solution)/shard_map/ppermute | solution.py:43
  21.4 0.9 %collective-permute-start.1 = (bf16[80,1152]{1,0:T(8,128)(2,1)S(1)}, bf16[80,1152]{1,0:T(8,128)(2,1)}, u32[]{:S(2)}, u32[]{:S(2)}) collective-permute-start(bf16[80,1152]{1,0:T(8,128)(2,1)S(1)} %shard_map.121.refs_0_), channel_id=1, source_target_pairs={{0,2},{1,3},{2,0},{3,1},{4,6},{5,7},{6,4},{7,5},{8,10},{9,11},{10,... | collective-permute-start | bytes 552968 | tf_op jit(solution)/shard_map/ppermute | solution.py:43
  22.2 0.9 %collective-permute-start = (bf16[80,1152]{1,0:T(8,128)(2,1)S(1)}, bf16[80,1152]{1,0:T(8,128)(2,1)}, u32[]{:S(2)}, u32[]{:S(2)}) collective-permute-start(bf16[80,1152]{1,0:T(8,128)(2,1)S(1)} %shard_map.121.refs_0_), channel_id=1, source_target_pairs={{0,1},{1,2},{2,3},{3,0},{4,5},{5,6},{6,7},{7,4},{8,9},{9,10},{10,1... | collective-permute-start | bytes 552968 | tf_op jit(solution)/shard_map/ppermute | solution.py:43
  23.4 6.8 %collective-permute-done.2.refs_3_ = bf16[80,1152]{1,0:T(8,128)(2,1)} collective-permute-done((bf16[80,1152]{1,0:T(8,128)(2,1)S(1)}, bf16[80,1152]{1,0:T(8,128)(2,1)}, u32[]{:S(2)}, u32[]{:S(2)}) %collective-permute-start.2) | collective-permute-done | bytes 184352 | tf_op jit(solution)/shard_map/ppermute | solution.py:43
  30.2 1.2 %collective-permute-done.1.refs_2_ = bf16[80,1152]{1,0:T(8,128)(2,1)} collective-permute-done((bf16[80,1152]{1,0:T(8,128)(2,1)S(1)}, bf16[80,1152]{1,0:T(8,128)(2,1)}, u32[]{:S(2)}, u32[]{:S(2)}) %collective-permute-start.1) | collective-permute-done | bytes 184352 | tf_op jit(solution)/shard_map/ppermute | solution.py:43
  31.3 2.6 %collective-permute-done.refs_1_ = bf16[80,1152]{1,0:T(8,128)(2,1)} collective-permute-done((bf16[80,1152]{1,0:T(8,128)(2,1)S(1)}, bf16[80,1152]{1,0:T(8,128)(2,1)}, u32[]{:S(2)}, u32[]{:S(2)}) %collective-permute-start) | collective-permute-done | bytes 184352 | tf_op jit(solution)/shard_map/ppermute | solution.py:43
  33.9 2.0 %shard_map.127 = bf16[32,8,1792]{2,1,0:T(8,128)(2,1)} custom-call(s32[3]{0:T(128)S(1)} %pad_add_fusion.at_ref, bf16[32,16,384]{2,1,0:T(8,128)(2,1)S(1)} %all-to-all-done.arrived_ref, bf16[128,3584]{1,0:T(8,128)(2,1)S(1)} %shard_map.126.rows_ref), custom_call_target="tpu_custom_call" | custom-call | bytes 41943040 | tf_op jit(solution)/shard_map/pallas_call | solution.py:223
  36.0 6.4 %all-to-all-start.1 = ((bf16[32,8,1792]{2,1,0:T(8,128)(2,1)}), bf16[32,8,1792]{2,1,0:T(8,128)(2,1)S(1)}, u32[]{:S(2)}, u32[]{:S(2)}) async-start(bf16[32,8,1792]{2,1,0:T(8,128)(2,1)} %shard_map.127), calls=%async_computation.1 | async-start | bytes 1835008 | tf_op jit(solution)/shard_map/all_to_all | solution.py:429
  42.4 1.1 %slice.9 = bf16[208,1152]{1,0:T(8,128)(2,1)S(1)} slice(bf16[432,1152]{1,0:T(8,128)(2,1)} %collective-permute-done.4.refs_2_), slice={[224:432], [0:1152]} | slice | bytes 958464 | tf_op jit(solution)/shard_map/slice | solution.py:426
  43.9 2.8 %shard_map.123 = (f32[4,8,48,128]{3,2,1,0:T(8,128)S(1)}, bf16[4,8,48,128]{3,2,1,0:T(8,128)(2,1)S(1)}) custom-call(s32[3]{0:T(128)S(1)} %pad_add_fusion.at_ref, bf16[32,16,384]{2,1,0:T(8,128)(2,1)S(1)} %all-to-all-done.arrived_ref, bf16[80,1152]{1,0:T(8,128)(2,1)S(1)} %shard_map.121.refs_0_, bf16[80,1152]{1,0:T(8,128)(2,1)} %collective-permute-done.refs_1_, ...), custom_call_target="tpu_custom_call" | custom-call | bytes 41943040 | tf_op jit(solution)/shard_map/pallas_call | solution.py:276
  46.8 1.8 %collective-permute-start.10 = (bf16[208,1152]{1,0:T(8,128)(2,1)S(1)}, bf16[208,1152]{1,0:T(8,128)(2,1)}, u32[]{:S(2)}, u32[]{:S(2)}) collective-permute-start(bf16[208,1152]{1,0:T(8,128)(2,1)S(1)} %slice.9), channel_id=1, source_target_pairs={{0,192},{64,0},{128,64},{192,128},{1,193},{65,1},{129,65},{193,129... | collective-permute-start | bytes 1437704 | tf_op jit(solution)/shard_map/ppermute | solution.py:39
  48.6 1.6 %collective-permute-start.6 = (bf16[8,48,128]{2,1,0:T(8,128)(2,1)S(1)}, bf16[8,48,128]{2,1,0:T(8,128)(2,1)S(1)}, u32[]{:S(2)}, u32[]{:S(2)}) collective-permute-start(bf16[8,48,128]{2,1,0:T(8,128)(2,1)S(1)} %get-tuple-element.65), channel_id=1, source_target_pairs={{0,64},{64,128},{128,192},{192,0},{1,65},{65,129},{129,193},{193,1... | collective-permute-start | bytes 294920 | tf_op jit(solution)/shard_map/ppermute | solution.py:39
  50.3 2.2 %collective-permute-start.7 = (bf16[8,48,128]{2,1,0:T(8,128)(2,1)S(1)}, bf16[8,48,128]{2,1,0:T(8,128)(2,1)S(1)}, u32[]{:S(2)}, u32[]{:S(2)}) collective-permute-start(bf16[8,48,128]{2,1,0:T(8,128)(2,1)S(1)} %get-tuple-element.66), channel_id=1, source_target_pairs={{0,128},{64,192},{128,0},{192,64},{1,129},{65,193},{129,1},{193,65... | collective-permute-start | bytes 294920 | tf_op jit(solution)/shard_map/ppermute | solution.py:39
  52.4 11.6 %collective-permute-done.10.refs_4_ = bf16[208,1152]{1,0:T(8,128)(2,1)} collective-permute-done((bf16[208,1152]{1,0:T(8,128)(2,1)S(1)}, bf16[208,1152]{1,0:T(8,128)(2,1)}, u32[]{:S(2)}, u32[]{:S(2)}) %collective-permute-start.10) | collective-permute-done | bytes 479264 | tf_op jit(solution)/shard_map/ppermute | solution.py:39
  64.1 1.5 %collective-permute-done.8.third = bf16[8,48,128]{2,1,0:T(8,128)(2,1)S(1)} collective-permute-done((bf16[8,48,128]{2,1,0:T(8,128)(2,1)S(1)}, bf16[8,48,128]{2,1,0:T(8,128)(2,1)S(1)}, u32[]{:S(2)}, u32[]{:S(2)}) %collective-permute-start.8) | collective-permute-done | bytes 98336 | tf_op jit(solution)/shard_map/ppermute | solution.py:39
  67.3 0.7 all-to-all-done.1.landed_ref
  68.0 6.3 %all-to-all-start.2 = ((bf16[8,48,128]{2,1,0:T(8,128)(2,1)}), bf16[8,48,128]{2,1,0:T(8,128)(2,1)S(1)}, u32[]{:S(2)}, u32[]{:S(2)}) async-start(bf16[8,48,128]{2,1,0:T(8,128)(2,1)} %shard_map.125), calls=%async_computation.2 | async-start | bytes 196608 | tf_op jit(solution)/shard_map/all_to_all | solution.py:445
  74.5 6.3 %shard_map.128 = (bf16[128,1152]{1,0:T(8,128)(2,1)}, bf16[128,1152]{1,0:T(8,128)(2,1)}, bf16[128,1152]{1,0:T(8,128)(2,1)}, bf16[128,1152]{1,0:T(8,128)(2,1)}) custom-call(s32[3]{0:T(128)S(1)} %pad_add_fusion.at_ref, bf16[256,256]{1,0:T(8,128)(2,1)S(1)} %shard_map.120.table_ref, bf16[32,8,1792]{2,1,0:T(8,128)(2,1)S(1)} %all-to-all-done.1.landed_ref, ...), custom_call_target="tpu_custom_call" | custom-call | bytes 25165824 | tf_op jit(solution)/shard_map/pallas_call | solution.py:386
  80.9 2.5 %all-to-all-done.2.terms_ref = bf16[8,48,128]{2,1,0:T(8,128)(2,1)S(1)} async-done(((bf16[8,48,128]{2,1,0:T(8,128)(2,1)}), bf16[8,48,128]{2,1,0:T(8,128)(2,1)S(1)}, u32[]{:S(2)}, u32[]{:S(2)}) %all-to-all-start.2) | async-done | bytes 98336 | tf_op jit(solution)/shard_map/all_to_all | solution.py:445
  83.3 0.8 shard_map.129
  (42 shorter events, 3.1 us)
Async XLA Ops:
  0.6 14.0 %copy-start.5 = (bf16[144,1152]{1,0:T(8,128)(2,1)S(1)}, bf16[144,1152]{1,0:T(8,128)(2,1)}, u32[]{:S(2)}) copy-start(bf16[144,1152]{1,0:T(8,128)(2,1)} %late_ref) | copy-start | bytes 995332
  2.9 11.7 %copy-start.3 = (bf16[144,1152]{1,0:T(8,128)(2,1)S(1)}, bf16[144,1152]{1,0:T(8,128)(2,1)}, u32[]{:S(2)}) copy-start(bf16[144,1152]{1,0:T(8,128)(2,1)} %early_ref) | copy-start | bytes 995332
  3.0 11.7 %copy-start.4 = (bf16[144,1152]{1,0:T(8,128)(2,1)S(1)}, bf16[144,1152]{1,0:T(8,128)(2,1)}, u32[]{:S(2)}) copy-start(bf16[144,1152]{1,0:T(8,128)(2,1)} %middle_ref) | copy-start | bytes 995332
  3.0 31.0 %all-to-all-start = ((bf16[32,16,384]{2,1,0:T(8,128)(2,1)}), bf16[32,16,384]{2,1,0:T(8,128)(2,1)S(1)}, u32[]{:S(2)}, u32[]{:S(2)}) async-start(bf16[32,16,384]{2,1,0:T(8,128)(2,1)} %shard_map.119), calls=%async_computation | async-start | bytes 786432 | tf_op jit(solution)/shard_map/all_to_all | solution.py:419
  14.6 3.4 %copy-start = (bf16[1,20,4608]{2,1,0:T(8,128)(2,1)S(1)}, bf16[1,20,4608]{2,1,0:T(8,128)(2,1)}, u32[]{:S(2)}) copy-start(bf16[1,20,4608]{2,1,0:T(8,128)(2,1)} %param.8) | copy-start | bytes 552964
  14.8 27.6 %collective-permute-start.4 = (bf16[432,1152]{1,0:T(8,128)(2,1)S(1)}, bf16[432,1152]{1,0:T(8,128)(2,1)}, u32[]{:S(2)}, u32[]{:S(2)}) collective-permute-start(bf16[432,1152]{1,0:T(8,128)(2,1)S(1)} %shard_map.122.refs_0_), channel_id=1, source_target_pairs={{0,192},{64,0},{128,64},{192,128},{1,193},{65,1},{129,65},{193,129... | collective-permute-start | bytes 2985992 | tf_op jit(solution)/shard_map/ppermute | solution.py:39
  15.7 27.8 %collective-permute-start.3 = (bf16[432,1152]{1,0:T(8,128)(2,1)S(1)}, bf16[432,1152]{1,0:T(8,128)(2,1)S(1)}, u32[]{:S(2)}, u32[]{:S(2)}) collective-permute-start(bf16[432,1152]{1,0:T(8,128)(2,1)S(1)} %shard_map.122.refs_0_), channel_id=1, source_target_pairs={{0,64},{64,128},{128,192},{192,0},{1,65},{65,129},{129,193},{193,1... | collective-permute-start | bytes 2985992 | tf_op jit(solution)/shard_map/ppermute | solution.py:39
  18.3 11.9 %collective-permute-start.2 = (bf16[80,1152]{1,0:T(8,128)(2,1)S(1)}, bf16[80,1152]{1,0:T(8,128)(2,1)}, u32[]{:S(2)}, u32[]{:S(2)}) collective-permute-start(bf16[80,1152]{1,0:T(8,128)(2,1)S(1)} %shard_map.121.refs_0_), channel_id=1, source_target_pairs={{0,3},{1,0},{2,1},{3,2},{4,7},{5,4},{6,5},{7,6},{8,11},{9,8},{10,9... | collective-permute-start | bytes 552968 | tf_op jit(solution)/shard_map/ppermute | solution.py:43
  21.4 10.0 %collective-permute-start.1 = (bf16[80,1152]{1,0:T(8,128)(2,1)S(1)}, bf16[80,1152]{1,0:T(8,128)(2,1)}, u32[]{:S(2)}, u32[]{:S(2)}) collective-permute-start(bf16[80,1152]{1,0:T(8,128)(2,1)S(1)} %shard_map.121.refs_0_), channel_id=1, source_target_pairs={{0,2},{1,3},{2,0},{3,1},{4,6},{5,7},{6,4},{7,5},{8,10},{9,11},{10,... | collective-permute-start | bytes 552968 | tf_op jit(solution)/shard_map/ppermute | solution.py:43
  22.2 11.7 %collective-permute-start = (bf16[80,1152]{1,0:T(8,128)(2,1)S(1)}, bf16[80,1152]{1,0:T(8,128)(2,1)}, u32[]{:S(2)}, u32[]{:S(2)}) collective-permute-start(bf16[80,1152]{1,0:T(8,128)(2,1)S(1)} %shard_map.121.refs_0_), channel_id=1, source_target_pairs={{0,1},{1,2},{2,3},{3,0},{4,5},{5,6},{6,7},{7,4},{8,9},{9,10},{10,1... | collective-permute-start | bytes 552968 | tf_op jit(solution)/shard_map/ppermute | solution.py:43
  36.0 32.0 %all-to-all-start.1 = ((bf16[32,8,1792]{2,1,0:T(8,128)(2,1)}), bf16[32,8,1792]{2,1,0:T(8,128)(2,1)S(1)}, u32[]{:S(2)}, u32[]{:S(2)}) async-start(bf16[32,8,1792]{2,1,0:T(8,128)(2,1)} %shard_map.127), calls=%async_computation.1 | async-start | bytes 1835008 | tf_op jit(solution)/shard_map/all_to_all | solution.py:429
  43.5 22.1 %collective-permute-start.9 = (bf16[224,1152]{1,0:T(8,128)(2,1)S(1)}, bf16[224,1152]{1,0:T(8,128)(2,1)}, u32[]{:S(2)}, u32[]{:S(2)}) collective-permute-start(bf16[224,1152]{1,0:T(8,128)(2,1)S(1)} %slice.8), channel_id=1, source_target_pairs={{0,64},{64,128},{128,192},{192,0},{1,65},{65,129},{129,193},{193,1... | collective-permute-start | bytes 1548296 | tf_op jit(solution)/shard_map/ppermute | solution.py:39
  46.7 1.9 %collective-permute-start.5 = (bf16[4,8,48,128]{3,2,1,0:T(8,128)(2,1)S(1)}, bf16[4,8,48,128]{3,2,1,0:T(8,128)(2,1)S(1)}, u32[]{:S(2)}, u32[]{:S(2)}) collective-permute-start(bf16[4,8,48,128]{3,2,1,0:T(8,128)(2,1)S(1)} %get-tuple-element.63), channel_id=1, source_target_pairs={{0,32},{32,0},{1,33},{33,1},{2,34},{34,2},{3,35},{35,3},{4,36},{36... | collective-permute-start | bytes 1179656 | tf_op jit(solution)/shard_map/ppermute | solution.py:47
  46.8 17.3 %collective-permute-start.10 = (bf16[208,1152]{1,0:T(8,128)(2,1)S(1)}, bf16[208,1152]{1,0:T(8,128)(2,1)}, u32[]{:S(2)}, u32[]{:S(2)}) collective-permute-start(bf16[208,1152]{1,0:T(8,128)(2,1)S(1)} %slice.9), channel_id=1, source_target_pairs={{0,192},{64,0},{128,64},{192,128},{1,193},{65,1},{129,65},{193,129... | collective-permute-start | bytes 1437704 | tf_op jit(solution)/shard_map/ppermute | solution.py:39
  48.6 15.4 %collective-permute-start.6 = (bf16[8,48,128]{2,1,0:T(8,128)(2,1)S(1)}, bf16[8,48,128]{2,1,0:T(8,128)(2,1)S(1)}, u32[]{:S(2)}, u32[]{:S(2)}) collective-permute-start(bf16[8,48,128]{2,1,0:T(8,128)(2,1)S(1)} %get-tuple-element.65), channel_id=1, source_target_pairs={{0,64},{64,128},{128,192},{192,0},{1,65},{65,129},{129,193},{193,1... | collective-permute-start | bytes 294920 | tf_op jit(solution)/shard_map/ppermute | solution.py:39
  50.3 13.8 %collective-permute-start.7 = (bf16[8,48,128]{2,1,0:T(8,128)(2,1)S(1)}, bf16[8,48,128]{2,1,0:T(8,128)(2,1)S(1)}, u32[]{:S(2)}, u32[]{:S(2)}) collective-permute-start(bf16[8,48,128]{2,1,0:T(8,128)(2,1)S(1)} %get-tuple-element.66), channel_id=1, source_target_pairs={{0,128},{64,192},{128,0},{192,64},{1,129},{65,193},{129,1},{193,65... | collective-permute-start | bytes 294920 | tf_op jit(solution)/shard_map/ppermute | solution.py:39
  52.4 13.2 %collective-permute-start.8 = (bf16[8,48,128]{2,1,0:T(8,128)(2,1)S(1)}, bf16[8,48,128]{2,1,0:T(8,128)(2,1)S(1)}, u32[]{:S(2)}, u32[]{:S(2)}) collective-permute-start(bf16[8,48,128]{2,1,0:T(8,128)(2,1)S(1)} %get-tuple-element.67), channel_id=1, source_target_pairs={{0,192},{64,0},{128,64},{192,128},{1,193},{65,1},{129,65},{193,129... | collective-permute-start | bytes 294920 | tf_op jit(solution)/shard_map/ppermute | solution.py:39
  66.3 8.0 %copy-start.6 = (s32[1,32]{1,0:T(1,128)S(1)}, s32[1,32]{1,0:T(1,128)}, u32[]{:S(2)}) copy-start(s32[1,32]{1,0:T(1,128)} %slot_ref) | copy-start | bytes 388
  66.3 8.2 %collective-permute-start.11 = (bf16[432,1152]{1,0:T(8,128)(2,1)S(1)}, bf16[432,1152]{1,0:T(8,128)(2,1)}, u32[]{:S(2)}, u32[]{:S(2)}) collective-permute-start(bf16[432,1152]{1,0:T(8,128)(2,1)S(1)} %shard_map.122.refs_0_), channel_id=1, source_target_pairs={{0,32},{32,0},{1,33},{33,1},{2,34},{34,2},{3,35},{35,3},{4,36},{36... | collective-permute-start | bytes 2985992 | tf_op jit(solution)/shard_map/ppermute | solution.py:47
  66.3 8.2 %collective-permute-start.12 = (bf16[432,1152]{1,0:T(8,128)(2,1)S(1)}, bf16[432,1152]{1,0:T(8,128)(2,1)}, u32[]{:S(2)}, u32[]{:S(2)}) collective-permute-start(bf16[432,1152]{1,0:T(8,128)(2,1)S(1)} %collective-permute-done.3.refs_1_), channel_id=1, source_target_pairs={{0,32},{32,0},{1,33},{33,1},{2,34},{34,2},{3,35},{35,3},{4,36},{36... | collective-permute-start | bytes 2985992 | tf_op jit(solution)/shard_map/ppermute | solution.py:47
  66.8 7.7 %collective-permute-start.13 = (bf16[432,1152]{1,0:T(8,128)(2,1)}, bf16[432,1152]{1,0:T(8,128)(2,1)}, u32[]{:S(2)}, u32[]{:S(2)}) collective-permute-start(bf16[432,1152]{1,0:T(8,128)(2,1)} %collective-permute-done.4.refs_2_), channel_id=1, source_target_pairs={{0,32},{32,0},{1,33},{33,1},{2,34},{34,2},{3,35},{35,3},{4,36},{36... | collective-permute-start | bytes 2985992 | tf_op jit(solution)/shard_map/ppermute | solution.py:47
  66.8 7.7 %collective-permute-start.14 = (bf16[224,1152]{1,0:T(8,128)(2,1)}, bf16[224,1152]{1,0:T(8,128)(2,1)}, u32[]{:S(2)}, u32[]{:S(2)}) collective-permute-start(bf16[224,1152]{1,0:T(8,128)(2,1)} %collective-permute-done.9.refs_3_), channel_id=1, source_target_pairs={{0,32},{32,0},{1,33},{33,1},{2,34},{34,2},{3,35},{35,3},{4,36},{36... | collective-permute-start | bytes 1548296 | tf_op jit(solution)/shard_map/ppermute | solution.py:47
  67.3 7.2 %collective-permute-start.15 = (bf16[208,1152]{1,0:T(8,128)(2,1)}, bf16[208,1152]{1,0:T(8,128)(2,1)}, u32[]{:S(2)}, u32[]{:S(2)}) collective-permute-start(bf16[208,1152]{1,0:T(8,128)(2,1)} %collective-permute-done.10.refs_4_), channel_id=1, source_target_pairs={{0,32},{32,0},{1,33},{33,1},{2,34},{34,2},{3,35},{35,3},{4,36},{36... | collective-permute-start | bytes 1437704 | tf_op jit(solution)/shard_map/ppermute | solution.py:47
  68.0 15.3 %all-to-all-start.2 = ((bf16[8,48,128]{2,1,0:T(8,128)(2,1)}), bf16[8,48,128]{2,1,0:T(8,128)(2,1)S(1)}, u32[]{:S(2)}, u32[]{:S(2)}) async-start(bf16[8,48,128]{2,1,0:T(8,128)(2,1)} %shard_map.125), calls=%async_computation.2 | async-start | bytes 196608 | tf_op jit(solution)/shard_map/all_to_all | solution.py:445
  (2 other events, 6.8 us)

commit v9 on v8

--- a/solution.py
+++ b/solution.py
@@ -433,14 +433,15 @@
     )
     far = over_x(once_more[0], 1), over_x(once_more[1], 3)
     keep, give = gradient(at, arrived, shares)
-    mine, *parts = sum_core(keep, over_core(give))
+    given, opposite = lax.optimization_barrier((over_core(give), over_core(stacked)))
+    mine, *parts = sum_core(keep, given)
     parts = [over_x(part, step) for step, part in zip((1, 2, 3), parts)]
     parts, far = lax.optimization_barrier((parts, far))
     terms = sum_x(mine, parts)
 
     pieces = (stacked, from_left, from_right, *far)
     terms, pieces = lax.optimization_barrier((terms, pieces))
-    pieces = pieces + tuple(over_core(piece) for piece in pieces)
+    pieces = (*pieces, opposite, *(over_core(piece) for piece in pieces[1:]))
     terms, landed = lax.optimization_barrier((terms, landed))
     weights = add_up(lax.all_to_all(terms, "z", 0, 0, tiled=True))
     context_early, context_middle, context_late, stream = contexts(at, table, landed, pieces)

time: 84.6 us -> 84.8 us (level)
  local copies, waits for them, and re-layouts: 1.14 us -> 2.2 us
    unnamed x14 -> x18, local copies, waits for them, and re-layouts: 0.04 us -> 1.1 us
    ppermute x7, starting transfers between devices: 9.26 us -> 8.28 us  [over_x(): return lax.ppermute(array, 'x', [(i, (i + step) % 4) for i in range(4)])]
  transfers between devices with their start and end apart: 19 -> 19, of which waited for: 7 -> 8; matrix products, arithmetic and copies ran while one was open for 1% -> 1% of each run, Pallas kernels for 15% -> 15%
where the time goes in v9:
time: 84.8 us; the launch traced here: 84.3 us
  starting transfers between devices  38.9 us (46%)
  waiting for transfers between devices  26.7 us (31%)
  Pallas kernels  15.6 us (18%)
  local copies, waits for them, and re-layouts  2.2 us (3%)
  between operations  0.86 us (1%)
    ppermute x7, waiting for transfers between devices, over_x(): return lax.ppermute(array, 'x', [(i, (i + step) % 4) for i in range(4)])  13.6 us
    all_to_all x1, starting transfers between devices, local(): arrived = lax.all_to_all(message, CTX, 0, 0, tiled=True)  11.6 us
    ppermute x3, waiting for transfers between devices, over_y(): return lax.ppermute(array, 'y', [(i, (i + step) % 4) for i in range(4)])  9.88 us
    ppermute x7, starting transfers between devices, over_x(): return lax.ppermute(array, 'x', [(i, (i + step) % 4) for i in range(4)])  8.28 us
    all_to_all x1, starting transfers between devices, local(): landed = lax.all_to_all(pack(at, arrived, rows), CTX, 0, 0, tiled=True)  6.48 us
    all_to_all x1, starting transfers between devices, local(): weights = add_up(lax.all_to_all(terms, 'z', 0, 0, tiled=True))  6.34 us
    pallas_call x1, Pallas kernels, contexts(): pl.pallas_call(context_kernel, out_shape=(out,) * 4, in_specs=[SMEM, VMEM...  6.34 us
    ppermute x3, starting transfers between devices, over_y(): return lax.ppermute(array, 'y', [(i, (i + step) % 4) for i in range(4)])  4.79 us
  transfers between devices with their start and end apart: 19, of which 8 were waited for; matrix products, arithmetic and copies ran while one was open for 1% of the time, Pallas kernels for 15%

profile of v9, /device:TPU:6, one launch (start us, length us, event | category | flops | bytes accessed | tf_op | source)
XLA Modules:
  0.0 84.3 jit_solution(15994665924013986216)
XLA Ops:
  0.6 2.3 %shard_map.119 = bf16[32,16,384]{2,1,0:T(8,128)(2,1)} custom-call(s32[1,32]{1,0:T(1,128)} %slot_ref, bf16[128,1152]{1,0:T(8,128)(2,1)} %bitcast.17), custom_call_target="tpu_custom_call" | custom-call | bytes 8388608 | tf_op jit(solution)/shard_map/pallas_call | solution.py:124
  3.0 11.6 %all-to-all-start = ((bf16[32,16,384]{2,1,0:T(8,128)(2,1)}), bf16[32,16,384]{2,1,0:T(8,128)(2,1)S(1)}, u32[]{:S(2)}, u32[]{:S(2)}) async-start(bf16[32,16,384]{2,1,0:T(8,128)(2,1)} %shard_map.119), calls=%async_computation | async-start | bytes 786432 | tf_op jit(solution)/shard_map/all_to_all | solution.py:419
  14.8 0.9 %collective-permute-start.4 = (bf16[432,1152]{1,0:T(8,128)(2,1)S(1)}, bf16[432,1152]{1,0:T(8,128)(2,1)}, u32[]{:S(2)}, u32[]{:S(2)}) collective-permute-start(bf16[432,1152]{1,0:T(8,128)(2,1)S(1)} %shard_map.122.refs_0_), channel_id=1, source_target_pairs={{0,192},{64,0},{128,64},{192,128},{1,193},{65,1},{129,65},{193,129... | collective-permute-start | bytes 2985992 | tf_op jit(solution)/shard_map/ppermute | solution.py:39
  15.7 2.4 %collective-permute-start.3 = (bf16[432,1152]{1,0:T(8,128)(2,1)S(1)}, bf16[432,1152]{1,0:T(8,128)(2,1)S(1)}, u32[]{:S(2)}, u32[]{:S(2)}) collective-permute-start(bf16[432,1152]{1,0:T(8,128)(2,1)S(1)} %shard_map.122.refs_0_), channel_id=1, source_target_pairs={{0,64},{64,128},{128,192},{192,0},{1,65},{65,129},{129,193},{193,1... | collective-permute-start | bytes 2985992 | tf_op jit(solution)/shard_map/ppermute | solution.py:39
  18.3 3.1 %collective-permute-start.2 = (bf16[80,1152]{1,0:T(8,128)(2,1)S(1)}, bf16[80,1152]{1,0:T(8,128)(2,1)S(1)}, u32[]{:S(2)}, u32[]{:S(2)}) collective-permute-start(bf16[80,1152]{1,0:T(8,128)(2,1)S(1)} %shard_map.121.refs_0_), channel_id=1, source_target_pairs={{0,3},{1,0},{2,1},{3,2},{4,7},{5,4},{6,5},{7,6},{8,11},{9,8},{10,9... | collective-permute-start | bytes 552968 | tf_op jit(solution)/shard_map/ppermute | solution.py:43
  21.4 0.9 %collective-permute-start.1 = (bf16[80,1152]{1,0:T(8,128)(2,1)S(1)}, bf16[80,1152]{1,0:T(8,128)(2,1)}, u32[]{:S(2)}, u32[]{:S(2)}) collective-permute-start(bf16[80,1152]{1,0:T(8,128)(2,1)S(1)} %shard_map.121.refs_0_), channel_id=1, source_target_pairs={{0,2},{1,3},{2,0},{3,1},{4,6},{5,7},{6,4},{7,5},{8,10},{9,11},{10,... | collective-permute-start | bytes 552968 | tf_op jit(solution)/shard_map/ppermute | solution.py:43
  22.2 0.9 %collective-permute-start = (bf16[80,1152]{1,0:T(8,128)(2,1)S(1)}, bf16[80,1152]{1,0:T(8,128)(2,1)}, u32[]{:S(2)}, u32[]{:S(2)}) collective-permute-start(bf16[80,1152]{1,0:T(8,128)(2,1)S(1)} %shard_map.121.refs_0_), channel_id=1, source_target_pairs={{0,1},{1,2},{2,3},{3,0},{4,5},{5,6},{6,7},{7,4},{8,9},{9,10},{10,1... | collective-permute-start | bytes 552968 | tf_op jit(solution)/shard_map/ppermute | solution.py:43
  23.1 7.1 %collective-permute-done.2.refs_3_ = bf16[80,1152]{1,0:T(8,128)(2,1)S(1)} collective-permute-done((bf16[80,1152]{1,0:T(8,128)(2,1)S(1)}, bf16[80,1152]{1,0:T(8,128)(2,1)S(1)}, u32[]{:S(2)}, u32[]{:S(2)}) %collective-permute-start.2) | collective-permute-done | bytes 184352 | tf_op jit(solution)/shard_map/ppermute | solution.py:43
  30.2 0.7 copy-done.6
  31.3 2.6 %collective-permute-done.refs_1_ = bf16[80,1152]{1,0:T(8,128)(2,1)} collective-permute-done((bf16[80,1152]{1,0:T(8,128)(2,1)S(1)}, bf16[80,1152]{1,0:T(8,128)(2,1)}, u32[]{:S(2)}, u32[]{:S(2)}) %collective-permute-start) | collective-permute-done | bytes 184352 | tf_op jit(solution)/shard_map/ppermute | solution.py:43
  33.9 2.0 %shard_map.127 = bf16[32,8,1792]{2,1,0:T(8,128)(2,1)} custom-call(s32[3]{0:T(128)S(1)} %pad_add_fusion.at_ref, bf16[32,16,384]{2,1,0:T(8,128)(2,1)S(1)} %all-to-all-done.arrived_ref, bf16[128,3584]{1,0:T(8,128)(2,1)S(1)} %shard_map.126.rows_ref), custom_call_target="tpu_custom_call" | custom-call | bytes 41943040 | tf_op jit(solution)/shard_map/pallas_call | solution.py:223
  36.0 6.5 %all-to-all-start.1 = ((bf16[32,8,1792]{2,1,0:T(8,128)(2,1)}), bf16[32,8,1792]{2,1,0:T(8,128)(2,1)S(1)}, u32[]{:S(2)}, u32[]{:S(2)}) async-start(bf16[32,8,1792]{2,1,0:T(8,128)(2,1)} %shard_map.127), calls=%async_computation.1 | async-start | bytes 1835008 | tf_op jit(solution)/shard_map/all_to_all | solution.py:429
  42.5 1.1 %slice.9 = bf16[208,1152]{1,0:T(8,128)(2,1)S(1)} slice(bf16[432,1152]{1,0:T(8,128)(2,1)} %collective-permute-done.4.refs_2_), slice={[224:432], [0:1152]} | slice | bytes 958464 | tf_op jit(solution)/shard_map/slice | solution.py:426
  44.5 2.7 %shard_map.123 = (f32[4,8,48,128]{3,2,1,0:T(8,128)S(1)}, bf16[4,8,48,128]{3,2,1,0:T(8,128)(2,1)S(1)}) custom-call(s32[3]{0:T(128)S(1)} %pad_add_fusion.at_ref, bf16[32,16,384]{2,1,0:T(8,128)(2,1)S(1)} %all-to-all-done.arrived_ref, bf16[80,1152]{1,0:T(8,128)(2,1)S(1)} %shard_map.121.refs_0_, bf16[80,1152]{1,0:T(8,128)(2,1)} %collective-permute-done.refs_1_, ...), custom_call_target="tpu_custom_call" | custom-call | bytes 41943040 | tf_op jit(solution)/shard_map/pallas_call | solution.py:276
  47.5 1.1 %collective-permute-start.11 = (bf16[208,1152]{1,0:T(8,128)(2,1)S(1)}, bf16[208,1152]{1,0:T(8,128)(2,1)}, u32[]{:S(2)}, u32[]{:S(2)}) collective-permute-start(bf16[208,1152]{1,0:T(8,128)(2,1)S(1)} %slice.9), channel_id=1, source_target_pairs={{0,192},{64,0},{128,64},{192,128},{1,193},{65,1},{129,65},{193,129... | collective-permute-start | bytes 1437704 | tf_op jit(solution)/shard_map/ppermute | solution.py:39
  49.0 1.8 %collective-permute-start.7 = (bf16[8,48,128]{2,1,0:T(8,128)(2,1)S(1)}, bf16[8,48,128]{2,1,0:T(8,128)(2,1)S(1)}, u32[]{:S(2)}, u32[]{:S(2)}) collective-permute-start(bf16[8,48,128]{2,1,0:T(8,128)(2,1)S(1)} %get-tuple-element.68), channel_id=1, source_target_pairs={{0,64},{64,128},{128,192},{192,0},{1,65},{65,129},{129,193},{193,1... | collective-permute-start | bytes 294920 | tf_op jit(solution)/shard_map/ppermute | solution.py:39
  50.9 1.6 %collective-permute-start.8 = (bf16[8,48,128]{2,1,0:T(8,128)(2,1)S(1)}, bf16[8,48,128]{2,1,0:T(8,128)(2,1)S(1)}, u32[]{:S(2)}, u32[]{:S(2)}) collective-permute-start(bf16[8,48,128]{2,1,0:T(8,128)(2,1)S(1)} %get-tuple-element.69), channel_id=1, source_target_pairs={{0,128},{64,192},{128,0},{192,64},{1,129},{65,193},{129,1},{193,65... | collective-permute-start | bytes 294920 | tf_op jit(solution)/shard_map/ppermute | solution.py:39
  52.4 12.2 %collective-permute-done.11.refs_4_ = bf16[208,1152]{1,0:T(8,128)(2,1)} collective-permute-done((bf16[208,1152]{1,0:T(8,128)(2,1)S(1)}, bf16[208,1152]{1,0:T(8,128)(2,1)}, u32[]{:S(2)}, u32[]{:S(2)}) %collective-permute-start.11) | collective-permute-done | bytes 479264 | tf_op jit(solution)/shard_map/ppermute | solution.py:39
  64.7 1.4 %collective-permute-done.9.third = bf16[8,48,128]{2,1,0:T(8,128)(2,1)S(1)} collective-permute-done((bf16[8,48,128]{2,1,0:T(8,128)(2,1)S(1)}, bf16[8,48,128]{2,1,0:T(8,128)(2,1)S(1)}, u32[]{:S(2)}, u32[]{:S(2)}) %collective-permute-start.9) | collective-permute-done | bytes 98336 | tf_op jit(solution)/shard_map/ppermute | solution.py:39
  66.1 0.7 shard_map.125
  68.4 6.3 %all-to-all-start.2 = ((bf16[8,48,128]{2,1,0:T(8,128)(2,1)}), bf16[8,48,128]{2,1,0:T(8,128)(2,1)S(1)}, u32[]{:S(2)}, u32[]{:S(2)}) async-start(bf16[8,48,128]{2,1,0:T(8,128)(2,1)} %shard_map.125), calls=%async_computation.2 | async-start | bytes 196608 | tf_op jit(solution)/shard_map/all_to_all | solution.py:446
  75.0 6.3 %shard_map.128 = (bf16[128,1152]{1,0:T(8,128)(2,1)}, bf16[128,1152]{1,0:T(8,128)(2,1)}, bf16[128,1152]{1,0:T(8,128)(2,1)}, bf16[128,1152]{1,0:T(8,128)(2,1)}) custom-call(s32[3]{0:T(128)S(1)} %pad_add_fusion.at_ref, bf16[256,256]{1,0:T(8,128)(2,1)S(1)} %shard_map.120.table_ref, bf16[32,8,1792]{2,1,0:T(8,128)(2,1)S(1)} %all-to-all-done.1.landed_ref, ...), custom_call_target="tpu_custom_call" | custom-call | bytes 25165824 | tf_op jit(solution)/shard_map/pallas_call | solution.py:386
  81.3 2.2 %all-to-all-done.2.terms_ref = bf16[8,48,128]{2,1,0:T(8,128)(2,1)S(1)} async-done(((bf16[8,48,128]{2,1,0:T(8,128)(2,1)}), bf16[8,48,128]{2,1,0:T(8,128)(2,1)S(1)}, u32[]{:S(2)}, u32[]{:S(2)}) %all-to-all-start.2) | async-done | bytes 98336 | tf_op jit(solution)/shard_map/all_to_all | solution.py:446
  83.5 0.8 shard_map.129
  (46 shorter events, 4.3 us)
Async XLA Ops:
  0.6 14.0 %copy-start.5 = (bf16[144,1152]{1,0:T(8,128)(2,1)S(1)}, bf16[144,1152]{1,0:T(8,128)(2,1)}, u32[]{:S(2)}) copy-start(bf16[144,1152]{1,0:T(8,128)(2,1)} %late_ref) | copy-start | bytes 995332
  2.9 11.7 %copy-start.3 = (bf16[144,1152]{1,0:T(8,128)(2,1)S(1)}, bf16[144,1152]{1,0:T(8,128)(2,1)}, u32[]{:S(2)}) copy-start(bf16[144,1152]{1,0:T(8,128)(2,1)} %early_ref) | copy-start | bytes 995332
  3.0 11.7 %copy-start.4 = (bf16[144,1152]{1,0:T(8,128)(2,1)S(1)}, bf16[144,1152]{1,0:T(8,128)(2,1)}, u32[]{:S(2)}) copy-start(bf16[144,1152]{1,0:T(8,128)(2,1)} %middle_ref) | copy-start | bytes 995332
  3.0 31.0 %all-to-all-start = ((bf16[32,16,384]{2,1,0:T(8,128)(2,1)}), bf16[32,16,384]{2,1,0:T(8,128)(2,1)S(1)}, u32[]{:S(2)}, u32[]{:S(2)}) async-start(bf16[32,16,384]{2,1,0:T(8,128)(2,1)} %shard_map.119), calls=%async_computation | async-start | bytes 786432 | tf_op jit(solution)/shard_map/all_to_all | solution.py:419
  14.6 3.4 %copy-start = (bf16[1,20,4608]{2,1,0:T(8,128)(2,1)S(1)}, bf16[1,20,4608]{2,1,0:T(8,128)(2,1)}, u32[]{:S(2)}) copy-start(bf16[1,20,4608]{2,1,0:T(8,128)(2,1)} %param.8) | copy-start | bytes 552964
  14.8 27.7 %collective-permute-start.4 = (bf16[432,1152]{1,0:T(8,128)(2,1)S(1)}, bf16[432,1152]{1,0:T(8,128)(2,1)}, u32[]{:S(2)}, u32[]{:S(2)}) collective-permute-start(bf16[432,1152]{1,0:T(8,128)(2,1)S(1)} %shard_map.122.refs_0_), channel_id=1, source_target_pairs={{0,192},{64,0},{128,64},{192,128},{1,193},{65,1},{129,65},{193,129... | collective-permute-start | bytes 2985992 | tf_op jit(solution)/shard_map/ppermute | solution.py:39
  15.7 27.9 %collective-permute-start.3 = (bf16[432,1152]{1,0:T(8,128)(2,1)S(1)}, bf16[432,1152]{1,0:T(8,128)(2,1)S(1)}, u32[]{:S(2)}, u32[]{:S(2)}) collective-permute-start(bf16[432,1152]{1,0:T(8,128)(2,1)S(1)} %shard_map.122.refs_0_), channel_id=1, source_target_pairs={{0,64},{64,128},{128,192},{192,0},{1,65},{65,129},{129,193},{193,1... | collective-permute-start | bytes 2985992 | tf_op jit(solution)/shard_map/ppermute | solution.py:39
  18.3 11.9 %collective-permute-start.2 = (bf16[80,1152]{1,0:T(8,128)(2,1)S(1)}, bf16[80,1152]{1,0:T(8,128)(2,1)S(1)}, u32[]{:S(2)}, u32[]{:S(2)}) collective-permute-start(bf16[80,1152]{1,0:T(8,128)(2,1)S(1)} %shard_map.121.refs_0_), channel_id=1, source_target_pairs={{0,3},{1,0},{2,1},{3,2},{4,7},{5,4},{6,5},{7,6},{8,11},{9,8},{10,9... | collective-permute-start | bytes 552968 | tf_op jit(solution)/shard_map/ppermute | solution.py:43
  21.4 10.0 %collective-permute-start.1 = (bf16[80,1152]{1,0:T(8,128)(2,1)S(1)}, bf16[80,1152]{1,0:T(8,128)(2,1)}, u32[]{:S(2)}, u32[]{:S(2)}) collective-permute-start(bf16[80,1152]{1,0:T(8,128)(2,1)S(1)} %shard_map.121.refs_0_), channel_id=1, source_target_pairs={{0,2},{1,3},{2,0},{3,1},{4,6},{5,7},{6,4},{7,5},{8,10},{9,11},{10,... | collective-permute-start | bytes 552968 | tf_op jit(solution)/shard_map/ppermute | solution.py:43
  22.2 11.7 %collective-permute-start = (bf16[80,1152]{1,0:T(8,128)(2,1)S(1)}, bf16[80,1152]{1,0:T(8,128)(2,1)}, u32[]{:S(2)}, u32[]{:S(2)}) collective-permute-start(bf16[80,1152]{1,0:T(8,128)(2,1)S(1)} %shard_map.121.refs_0_), channel_id=1, source_target_pairs={{0,1},{1,2},{2,3},{3,0},{4,5},{5,6},{6,7},{7,4},{8,9},{9,10},{10,1... | collective-permute-start | bytes 552968 | tf_op jit(solution)/shard_map/ppermute | solution.py:43
  30.8 17.7 %collective-permute-start.6 = (bf16[432,1152]{1,0:T(8,128)(2,1)S(1)}, bf16[432,1152]{1,0:T(8,128)(2,1)}, u32[]{:S(2)}, u32[]{:S(2)}) collective-permute-start(bf16[432,1152]{1,0:T(8,128)(2,1)S(1)} %shard_map.122.refs_0_), channel_id=1, source_target_pairs={{0,32},{32,0},{1,33},{33,1},{2,34},{34,2},{3,35},{35,3},{4,36},{36... | collective-permute-start | bytes 2985992 | tf_op jit(solution)/shard_map/ppermute | solution.py:47
  36.0 32.4 %all-to-all-start.1 = ((bf16[32,8,1792]{2,1,0:T(8,128)(2,1)}), bf16[32,8,1792]{2,1,0:T(8,128)(2,1)S(1)}, u32[]{:S(2)}, u32[]{:S(2)}) async-start(bf16[32,8,1792]{2,1,0:T(8,128)(2,1)} %shard_map.127), calls=%async_computation.1 | async-start | bytes 1835008 | tf_op jit(solution)/shard_map/all_to_all | solution.py:429
  43.6 22.4 %collective-permute-start.10 = (bf16[224,1152]{1,0:T(8,128)(2,1)S(1)}, bf16[224,1152]{1,0:T(8,128)(2,1)}, u32[]{:S(2)}, u32[]{:S(2)}) collective-permute-start(bf16[224,1152]{1,0:T(8,128)(2,1)S(1)} %slice.8), channel_id=1, source_target_pairs={{0,64},{64,128},{128,192},{192,0},{1,65},{65,129},{129,193},{193,1... | collective-permute-start | bytes 1548296 | tf_op jit(solution)/shard_map/ppermute | solution.py:39
  47.2 1.8 %collective-permute-start.5 = (bf16[4,8,48,128]{3,2,1,0:T(8,128)(2,1)S(1)}, bf16[4,8,48,128]{3,2,1,0:T(8,128)(2,1)S(1)}, u32[]{:S(2)}, u32[]{:S(2)}) collective-permute-start(bf16[4,8,48,128]{3,2,1,0:T(8,128)(2,1)S(1)} %get-tuple-element.65), channel_id=1, source_target_pairs={{0,32},{32,0},{1,33},{33,1},{2,34},{34,2},{3,35},{35,3},{4,36},{36... | collective-permute-start | bytes 1179656 | tf_op jit(solution)/shard_map/ppermute | solution.py:47
  47.5 17.2 %collective-permute-start.11 = (bf16[208,1152]{1,0:T(8,128)(2,1)S(1)}, bf16[208,1152]{1,0:T(8,128)(2,1)}, u32[]{:S(2)}, u32[]{:S(2)}) collective-permute-start(bf16[208,1152]{1,0:T(8,128)(2,1)S(1)} %slice.9), channel_id=1, source_target_pairs={{0,192},{64,0},{128,64},{192,128},{1,193},{65,1},{129,65},{193,129... | collective-permute-start | bytes 1437704 | tf_op jit(solution)/shard_map/ppermute | solution.py:39
  49.0 15.6 %collective-permute-start.7 = (bf16[8,48,128]{2,1,0:T(8,128)(2,1)S(1)}, bf16[8,48,128]{2,1,0:T(8,128)(2,1)S(1)}, u32[]{:S(2)}, u32[]{:S(2)}) collective-permute-start(bf16[8,48,128]{2,1,0:T(8,128)(2,1)S(1)} %get-tuple-element.68), channel_id=1, source_target_pairs={{0,64},{64,128},{128,192},{192,0},{1,65},{65,129},{129,193},{193,1... | collective-permute-start | bytes 294920 | tf_op jit(solution)/shard_map/ppermute | solution.py:39
  50.9 13.8 %collective-permute-start.8 = (bf16[8,48,128]{2,1,0:T(8,128)(2,1)S(1)}, bf16[8,48,128]{2,1,0:T(8,128)(2,1)S(1)}, u32[]{:S(2)}, u32[]{:S(2)}) collective-permute-start(bf16[8,48,128]{2,1,0:T(8,128)(2,1)S(1)} %get-tuple-element.69), channel_id=1, source_target_pairs={{0,128},{64,192},{128,0},{192,64},{1,129},{65,193},{129,1},{193,65... | collective-permute-start | bytes 294920 | tf_op jit(solution)/shard_map/ppermute | solution.py:39
  52.4 13.6 %collective-permute-start.9 = (bf16[8,48,128]{2,1,0:T(8,128)(2,1)S(1)}, bf16[8,48,128]{2,1,0:T(8,128)(2,1)S(1)}, u32[]{:S(2)}, u32[]{:S(2)}) collective-permute-start(bf16[8,48,128]{2,1,0:T(8,128)(2,1)S(1)} %get-tuple-element.70), channel_id=1, source_target_pairs={{0,192},{64,0},{128,64},{192,128},{1,193},{65,1},{129,65},{193,129... | collective-permute-start | bytes 294920 | tf_op jit(solution)/shard_map/ppermute | solution.py:39
  66.7 8.0 %copy-start.8 = (s32[1,32]{1,0:T(1,128)S(1)}, s32[1,32]{1,0:T(1,128)}, u32[]{:S(2)}) copy-start(s32[1,32]{1,0:T(1,128)} %slot_ref) | copy-start | bytes 388
  66.7 8.2 %collective-permute-start.12 = (bf16[432,1152]{1,0:T(8,128)(2,1)S(1)}, bf16[432,1152]{1,0:T(8,128)(2,1)}, u32[]{:S(2)}, u32[]{:S(2)}) collective-permute-start(bf16[432,1152]{1,0:T(8,128)(2,1)S(1)} %collective-permute-done.3.refs_1_), channel_id=1, source_target_pairs={{0,32},{32,0},{1,33},{33,1},{2,34},{34,2},{3,35},{35,3},{4,36},{36... | collective-permute-start | bytes 2985992 | tf_op jit(solution)/shard_map/ppermute | solution.py:47
  66.7 8.2 %collective-permute-start.13 = (bf16[432,1152]{1,0:T(8,128)(2,1)}, bf16[432,1152]{1,0:T(8,128)(2,1)}, u32[]{:S(2)}, u32[]{:S(2)}) collective-permute-start(bf16[432,1152]{1,0:T(8,128)(2,1)} %collective-permute-done.4.refs_2_), channel_id=1, source_target_pairs={{0,32},{32,0},{1,33},{33,1},{2,34},{34,2},{3,35},{35,3},{4,36},{36... | collective-permute-start | bytes 2985992 | tf_op jit(solution)/shard_map/ppermute | solution.py:47
  67.2 7.7 %collective-permute-start.14 = (bf16[224,1152]{1,0:T(8,128)(2,1)}, bf16[224,1152]{1,0:T(8,128)(2,1)}, u32[]{:S(2)}, u32[]{:S(2)}) collective-permute-start(bf16[224,1152]{1,0:T(8,128)(2,1)} %collective-permute-done.10.refs_3_), channel_id=1, source_target_pairs={{0,32},{32,0},{1,33},{33,1},{2,34},{34,2},{3,35},{35,3},{4,36},{36... | collective-permute-start | bytes 1548296 | tf_op jit(solution)/shard_map/ppermute | solution.py:47
  67.3 7.7 %collective-permute-start.15 = (bf16[208,1152]{1,0:T(8,128)(2,1)}, bf16[208,1152]{1,0:T(8,128)(2,1)}, u32[]{:S(2)}, u32[]{:S(2)}) collective-permute-start(bf16[208,1152]{1,0:T(8,128)(2,1)} %collective-permute-done.11.refs_4_), channel_id=1, source_target_pairs={{0,32},{32,0},{1,33},{33,1},{2,34},{34,2},{3,35},{35,3},{4,36},{36... | collective-permute-start | bytes 1437704 | tf_op jit(solution)/shard_map/ppermute | solution.py:47
  68.4 15.1 %all-to-all-start.2 = ((bf16[8,48,128]{2,1,0:T(8,128)(2,1)}), bf16[8,48,128]{2,1,0:T(8,128)(2,1)S(1)}, u32[]{:S(2)}, u32[]{:S(2)}) async-start(bf16[8,48,128]{2,1,0:T(8,128)(2,1)} %shard_map.125), calls=%async_computation.2 | async-start | bytes 196608 | tf_op jit(solution)/shard_map/all_to_all | solution.py:446
  (4 other events, 8.4 us)
